TPU v7x, 32 devices: a whole 2x2x4 slice. The times are simulated.
32 devices in a mesh: seq: 8 (over z, y), head: 4 (over x, core).
Axes of the slice: x: 2, y: 2, z: 4, core: 2. Of those that a mesh axis runs over, the one named last changes fastest.
Arguments:
- mixer_queries: bfloat16 [4096, 2048], P('seq', 'head'), may hold values from -6 to 6
- mixer_keys: bfloat16 [4096, 2048], P('seq', 'head'), may hold values from -6 to 6
- mixer_values: bfloat16 [4096, 2048], P('seq', 'head'), may hold values from -6 to 6
- window_keys: bfloat16 [4096, 512], P('seq', 'head'), may hold values from -1800 to 1800
- window_values: bfloat16 [4096, 512], P('seq', 'head'), may hold values from -6 to 6
- out_gain: float32 [2048], P('head'), may hold values from 0.1 to 1.9
- ridge: float32 [16], P('head'), may hold values from 0.25 to 4
- out_weight: bfloat16 [2048, 2048], P('head'), may hold values from -0.125 to 0.125
Outputs:
- layer_output: bfloat16 [4096, 2048], P('seq', 'head')
All inputs are finite; a program needn't handle non-finite values.
Results may differ from a plain program's by a relative error of at most 0.019.
Values may be sent and summed in bfloat16 or wider, within the bound.
No kernel may reach another device: no remote copies, remote signals or barrier semaphores. Data moves between devices by JAX's collectives and lax.ppermute only.
A program may use at most 128 MiB of HBM per device.

v0:
```python
import math

import jax
import jax.numpy as jnp
from jax import lax
from jax.sharding import PartitionSpec as P

SPAN = 128
ITERS = 8
WINDOW = 512


HIGH = lax.Precision.HIGHEST
EPS = 1e-06


def carried_in(value, axis, join, neutral):
    count, mine = (lax.axis_size(axis), lax.axis_index(axis))
    pieces = jax.tree.map(lambda part: lax.all_gather(part, axis), value)
    running = jax.tree.map(
        lambda part, zero: jnp.full_like(part, 0) + jnp.asarray(zero, part.dtype), value, neutral
    )

    def lap(position, running):
        longer = join(running, jax.tree.map(lambda part: part[position], pieces))
        return jax.tree.map(lambda new, old: jnp.where(position < mine, new, old), longer, running)

    return lax.fori_loop(0, count - 1, lap, running)


def from_behind(block, axis, distance):
    devices = range(lax.axis_size(axis))
    route = [(i - distance, i) for i in devices if i - distance in devices]
    return lax.ppermute(block, axis, route)


def unit_rows(block_in):
    row_width = block_in.shape[-1]
    return (
        block_in
        * lax.rsqrt(jnp.mean(block_in * block_in, axis=-1, keepdims=True) + EPS)
        / math.sqrt(row_width)
    )


def apply_state(states, keys_in, row_vals, vectors, lower_mask):
    inter = jnp.einsum("hcij,hclj->hcli", states, vectors, precision=HIGH)
    intersection = jnp.einsum("hcsj,hctj->hcts", keys_in, vectors, precision=HIGH) * lower_mask
    return inter + jnp.einsum("hcts,hcsi->hcti", intersection, row_vals, precision=HIGH)


def chebyshev(queries, keys_in, starts, ridge_col, upper, lower_mask, n_iters):
    centre = (upper + ridge_col) * 0.5
    radius = (upper - ridge_col) * 0.5
    solved = jnp.zeros_like(queries)
    residue = queries
    direction = residue
    step_size = 1.0 / centre
    for step_index in range(n_iters):
        if step_index > 0:
            scaled = radius * step_size
            weight_prev = scaled * scaled * (0.5 if step_index == 1 else 0.25)
            step_size = 1.0 / (centre - weight_prev / step_size)
            direction = residue + weight_prev * direction
        solved = solved + step_size * direction
        if step_index + 1 < n_iters:
            image_vec = (
                apply_state(starts, keys_in, keys_in, direction, lower_mask) + ridge_col * direction
            )
            residue = residue - step_size * image_vec
    return solved


def to_spans(rows_in, local_heads, span_len):
    row_count, row_width = rows_in.shape
    head_width = row_width // local_heads
    return (
        rows_in.astype(jnp.float32)
        .reshape(row_count // span_len, span_len, local_heads, head_width)
        .transpose(2, 0, 1, 3)
    )


def add_pair(earlier, later):
    return (earlier[0] + later[0], earlier[1] + later[1])


def attend(q_part, k_part, v_part, row_first, col_first):
    scale = 1.0 / math.sqrt(q_part.shape[-1])
    scores = (
        jnp.einsum("qkgd,skd->kgqs", q_part, k_part, preferred_element_type=jnp.float32) * scale
    )
    rows_at = row_first + jnp.arange(q_part.shape[0], dtype=jnp.int32)
    cols_at = col_first + jnp.arange(k_part.shape[0], dtype=jnp.int32)
    allowed = (
        (cols_at[None, :] >= 0)
        & (cols_at[None, :] <= rows_at[:, None])
        & (cols_at[None, :] > rows_at[:, None] - WINDOW)
    )
    scores = jnp.where(allowed[None, None], scores, -jnp.inf)
    peak = jnp.max(scores, axis=-1, keepdims=True)
    expd = jnp.exp(scores - peak)
    weights = (expd / jnp.sum(expd, axis=-1, keepdims=True)).astype(jnp.bfloat16)
    mixed_out = jnp.einsum("kgqs,skd->qkgd", weights, v_part, preferred_element_type=jnp.float32)
    return mixed_out.astype(jnp.bfloat16).reshape(q_part.shape[0], -1)


def shards(
    mixer_queries, mixer_keys, mixer_values, window_keys, window_values, out_gain, ridge, out_weight
):
    row_count = mixer_queries.shape[0]
    local_heads = ridge.shape[0]
    head_width = mixer_queries.shape[1] // local_heads
    n_spans = row_count // SPAN
    base = lax.axis_index("seq") * row_count
    queries = unit_rows(to_spans(mixer_queries, local_heads, SPAN))
    keys_in = unit_rows(to_spans(mixer_keys, local_heads, SPAN))
    values_in = to_spans(mixer_values, local_heads, SPAN)
    span_keys = jnp.einsum("hcld,hcle->hcde", keys_in, keys_in, precision=HIGH)
    span_vals = jnp.einsum("hcli,hclj->hcij", values_in, keys_in, precision=HIGH)
    zero_state = jnp.zeros((local_heads, head_width, head_width), jnp.float32)
    prior_keys, prior_vals = carried_in(
        (jnp.sum(span_keys, axis=1), jnp.sum(span_vals, axis=1)),
        "seq",
        add_pair,
        (zero_state, zero_state),
    )
    lead_zero = jnp.zeros((local_heads, 1, head_width, head_width), jnp.float32)
    key_starts = prior_keys[:, None] + jnp.concatenate(
        [lead_zero, jnp.cumsum(span_keys, axis=1)[:, :-1]], axis=1
    )
    val_starts = prior_vals[:, None] + jnp.concatenate(
        [lead_zero, jnp.cumsum(span_vals, axis=1)[:, :-1]], axis=1
    )
    lower_mask = (jnp.arange(SPAN)[:, None] >= jnp.arange(SPAN)[None, :]).astype(jnp.float32)
    ridge_col = ridge.reshape(local_heads, 1, 1, 1)
    places = (base + jnp.arange(row_count, dtype=jnp.int32) + 1).astype(jnp.float32)
    upper = ridge_col + places.reshape(1, n_spans, SPAN, 1)
    solved = chebyshev(queries, keys_in, key_starts, ridge_col, upper, lower_mask, ITERS)
    mixed = apply_state(val_starts, keys_in, values_in, solved, lower_mask)
    gain_col = out_gain.reshape(local_heads, 1, 1, head_width)
    normed = mixed * lax.rsqrt(jnp.mean(mixed * mixed, axis=-1, keepdims=True) + EPS) * gain_col
    attn_rows = (
        normed.transpose(1, 2, 0, 3)
        .reshape(row_count, local_heads * head_width)
        .astype(jnp.bfloat16)
    )
    kv_local = window_keys.shape[1] // head_width
    group_size = local_heads // kv_local
    rim_keys, rim_vals = from_behind((window_keys, window_values), "seq", 1)
    all_keys = jnp.concatenate([rim_keys, window_keys], 0).reshape(
        row_count + WINDOW, kv_local, head_width
    )
    all_vals = jnp.concatenate([rim_vals, window_values], 0).reshape(
        row_count + WINDOW, kv_local, head_width
    )
    query_heads = attn_rows.reshape(row_count, kv_local, group_size, head_width)
    q_block = min(row_count, 512)

    def one_block(block_index):
        begin = block_index * q_block
        return attend(query_heads, all_keys, all_vals, base + begin, base + begin - WINDOW)

    attended = lax.map(one_block, jnp.arange(row_count // q_block, dtype=jnp.int32)).reshape(
        row_count, local_heads * head_width
    )
    summed = lax.psum_scatter(
        lax.dot_general(
            out_weight, attended, (((0,), (1,)), ((), ())), preferred_element_type=jnp.float32
        ),
        "head",
        scatter_dimension=0,
        tiled=True,
    )
    return summed.T.astype(jnp.bfloat16)


def solution(mesh):
    return jax.shard_map(
        shards,
        mesh=mesh,
        in_specs=(
            P("seq", "head"),
            P("seq", "head"),
            P("seq", "head"),
            P("seq", "head"),
            P("seq", "head"),
            P("head"),
            P("head"),
            P("head", None),
        ),
        out_specs=P("seq", "head"),
        check_vma=False,
    )
```

profile of v0, /device:TPU:0, one launch (start us, length us, event | category | flops | bytes accessed | tf_op | source)
XLA Modules:
  0.0 259.8 jit_solution(6289519267823794203)
XLA Ops:
  14.4 3.4 %fusion.133 = (f32[4,128,128]{1,2,0:T(8,128)S(1)}, f32[4,4,128,128]{2,3,1,0:T(8,128)}) fusion(bf16[4,128,4,128]{3,2,1,0:T(4,128)(2,1)} %reshape.300, f32[4,128,4,128]{3,2,1,0:T(4,128)S(1)} %reshape.304, f32[4,4,128]{2,1,0:T(4,128)S(1)} %get-tuple-element.206), kind=kOutput, calls=%fused_computation.175 | convolution fusion | flops 403374080 | bytes 2891776 | tf_op jit(solution)/shard_map/hcli,hclj->hcij/dot_general | solution.py:120
  18.7 4.2 %fusion.132 = (f32[4,128,128]{2,1,0:T(8,128)}, f32[4,4,128,128]{3,2,1,0:T(8,128)}) fusion(f32[4,128,4,128]{3,2,1,0:T(4,128)S(1)} %reshape.304, f32[4,4,128]{2,1,0:T(4,128)S(1)} %get-tuple-element.206), kind=kOutput, calls=%fused_computation.174 | convolution fusion | flops 403374080 | bytes 2367488 | tf_op jit(solution)/shard_map/hcld,hcle->hcde/dot_general | solution.py:119
  22.9 5.5 %collective-permute-start.1 = (bf16[512,128]{1,0:T(8,128)(2,1)}, bf16[512,128]{1,0:T(8,128)(2,1)}, u32[]{:S(2)}, u32[]{:S(2)}) collective-permute-start(bf16[512,128]{1,0:T(8,128)(2,1)} %param.13), channel_id=1, source_target_pairs={{0,4},{4,8},{8,12},{12,16},{16,20},{20,24},{24,28},{1,5},{5,9},{9,... | collective-permute-start | bytes 393224 | tf_op jit(solution)/shard_map/ppermute | solution.py:34
  30.1 3.9 %collective-permute-start = (bf16[512,128]{0,1:T(8,128)(2,1)}, bf16[512,128]{0,1:T(8,128)(2,1)}, u32[]{:S(2)}, u32[]{:S(2)}) collective-permute-start(bf16[512,128]{0,1:T(8,128)(2,1)} %copy.27), channel_id=1, source_target_pairs={{0,4},{4,8},{8,12},{12,16},{16,20},{20,24},{24,28},{1,5},{5,9},{9,... | collective-permute-start | bytes 393224 | tf_op jit(solution)/shard_map/ppermute | solution.py:34
  42.3 4.7 %convolution_multiply_fusion.7 = f32[4,4,128,128]{3,2,1,0:T(8,128)} fusion(f32[4,128,4,128]{3,2,1,0:T(4,128)} %reshape.303, f32[128,128]{1,0:T(8,128)S(1)} %fusion.69, f32[4,4,128]{2,1,0:T(4,128)S(1)} %get-tuple-element.207, f32[4,128,4,128]{3,2,1,0:T(4,128)S(1)} %reshape.304, f32[4,4,128]{2,1,0:T(4,128)S(1)} %get-tuple-element.206), kind=kOutput, calls=%fused_computation.33 | convolution fusion | flops 403963904 | bytes 3227648 | tf_op jit(solution)/shard_map/hcsj,hctj->hcts/dot_general | solution.py:48
  47.0 25.7 %all-gather.7.cloned.1.call-done = f32[32,128,128]{2,1,0:T(8,128)} async-done(((f32[4,128,128]{2,1,0:T(8,128)}), f32[32,128,128]{2,1,0:T(8,128)}) %all-gather.7.cloned.1.call-update) | async-done | bytes 2097168 | tf_op jit(solution)/shard_map/all_gather | solution.py:19
  72.7 49.9 %all-gather.5.cloned.1.call-done = f32[32,128,128]{2,1,0:T(8,128)} async-done(((f32[4,128,128]{2,1,0:T(8,128)}), f32[32,128,128]{2,1,0:T(8,128)}) %all-gather.5.cloned.1.call-update) | async-done | bytes 2097168 | tf_op jit(solution)/shard_map/all_gather | solution.py:19
  122.7 13.7 %while.20 = (s32[]{:T(128)}, f32[4,128,128]{2,1,0:T(8,128)S(1)}, f32[4,128,128]{2,1,0:T(8,128)}, s32[]{:T(128)}, f32[8,4,128,128]{3,2,1,0:T(8,128)}, /*index=5*/f32[8,4,128,128]{3,2,1,0:T(8,128)}, s32[]{:T(128)}, s32[]{:T(128)}) while((s32[]{:T(128)}, f32[4,128,128]{2,1,0:T(8,128)S(1)}, f32[4,128,128]{2,1,0:T(8,128)}, s32[]{:T(128)}, ...), condition=%wide.region_5.6_spmd.clone, body=%wide.region_4.5_spmd.clone.sunk | while | flops 393220 | bytes 1572973 | solution.py:28
  136.4 3.8 %fusion.45 = f32[4,4,128,128]{3,2,1,0:T(8,128)S(1)} fusion(f32[4,3,128,128]{3,2,1,0:T(8,128)} %slice.8, f32[4,128,4,128]{3,2,1,0:T(4,128)} %reshape.303, f32[4,128,128]{2,1,0:T(8,128)S(1)} %get-tuple-element.133, f32[4,4,128]{2,1,0:T(4,128)S(1)} %get-tuple-element.207), kind=kOutput, calls=%fused_computation.80 | convolution fusion | flops 403439616 | bytes 3153920 | tf_op jit(solution)/shard_map/hcij,hclj->hcli/dot_general | solution.py:47
  140.2 3.3 %multiply_add_fusion.5 = (f32[4,4,128,128]{3,2,1,0:T(8,128)S(1)}, f32[4,4,128,128]{3,2,1,0:T(8,128)S(1)}) fusion(f32[4,128,4,128]{3,2,1,0:T(4,128)} %reshape.303, f32[4,4,128]{2,1,0:T(4,128)} %get-tuple-element.171, f32[4,4,128]{2,1,0:T(4,128)S(1)} %get-tuple-element.207, f32[4]{0:T(128)} %broadcast_multiply_fusion.2, f32[4,4,128,128]{3,2,1,0:T(8,128)S(1)} %fusion.45, ...), kind=kOutput, calls=%fused_computation.72 | convolution fusion | flops 405536768 | bytes 6324240 | tf_op jit(solution)/shard_map/hcts,hcsi->hcti/dot_general | solution.py:49
  143.5 2.4 convolution_multiply_fusion.6
  148.2 2.5 multiply_add_fusion.4
  150.7 2.4 convolution_multiply_fusion.5
  157.7 2.4 convolution_multiply_fusion.4
  169.4 2.5 multiply_add_fusion.1
  172.0 2.4 convolution_multiply_fusion.2
  178.4 2.5 convolution_multiply_fusion.1
  183.3 4.3 %fusion.27 = f32[4,4,128,128]{3,2,1,0:T(8,128)S(1)} fusion(f32[4,4,128,128]{3,2,1,0:T(8,128)S(1)} %fusion.22, f32[4,4,128,128]{3,2,1,0:T(8,128)S(1)} %fusion.39, f32[4,4,128,128]{3,2,1,0:T(8,128)S(1)} %convolution_multiply_fusion.1, f32[4,4,128,128]{3,2,1,0:T(8,128)S(1)} %get-tuple-element.198, f32[4,4,128,128]{3,2,1,0:T(8,128)S(1)} %get-tuple-element.196, ...), kind=kOutput, calls=%fused_computation.51 | convolution fusion | flops 409731072 | bytes 11632656 | tf_op jit(solution)/shard_map/hcts,hcsi->hcti/dot_general | solution.py:49
  187.7 3.3 %convolution_multiply_fusion = f32[4,4,128,128]{3,2,1,0:T(8,128)} fusion(f32[4,4,128,128]{3,2,1,0:T(8,128)S(1)} %fusion.27, f32[128,128]{1,0:T(8,128)S(1)} %fusion.69, f32[4,128,4,128]{3,2,1,0:T(4,128)S(1)} %reshape.304, f32[4,4,128]{2,1,0:T(4,128)S(1)} %get-tuple-element.206), kind=kOutput, calls=%fused_computation.12 | convolution fusion | flops 403439616 | bytes 3219456 | tf_op jit(solution)/shard_map/hcsj,hctj->hcts/dot_general | solution.py:48
  191.1 2.7 %fusion.36 = f32[4,4,128,128]{3,2,1,0:T(8,128)S(1)} fusion(f32[4,4,128,128]{3,2,1,0:T(8,128)} %copy-done.3, f32[4,3,128,128]{2,3,1,0:T(8,128)} %slice.9, f32[4,128,128]{1,2,0:T(8,128)S(1)} %copy.35), kind=kOutput, calls=%fused_computation.64 | convolution fusion | flops 402915328 | bytes 3145728 | tf_op jit(solution)/shard_map/hcij,hclj->hcli/dot_general | solution.py:47
  196.5 2.4 fusion.1
  200.7 3.7 %fusion.28 = bf16[128,4,512]{2,0,1:T(8,128)(2,1)S(1)} fusion(f32[4,512]{1,0:T(4,128)S(1)} %fusion, f32[4,512]{1,0:T(4,128)S(1)} %get-tuple-element.202, f32[1024,512,4]{1,0,2:T(8,128)S(1)} %get-tuple-element.203, pred[512,1024]{0,1:T(8,128)(4,1)S(1)} %copy-done.5, bf16[512,128]{0,1:T(8,128)(2,1)} %copy.27, bf16[512,128]{0,1:T(8,128)(2,1)} %collective-permute-done), kind=kOutput, calls=%fused_computation.52 | convolution fusion | flops 548143104 | bytes 9715712 | tf_op jit(solution)/shard_map/while/body/eval_jaxpr/kgqs,skd->qkgd/dot_general | solution.py:104
  204.5 3.2 %convolution_bitcast_fusion = f32[2048,512]{0,1:T(8,128)} fusion(bf16[512,512]{0,1:T(8,128)(2,1)S(1)} %bitcast.149, bf16[512,2048]{1,0:T(8,128)(2,1)S(1)} %copy-done), kind=kOutput, calls=%fused_computation.9 | convolution fusion | flops 1073741824 | bytes 6815744 | tf_op jit(solution)/shard_map/dot_general | solution.py:168
  207.7 43.2 %reduce-scatter.2.cloned.1.call-done = f32[512,512]{0,1:T(8,128)} async-done(((f32[2048,512]{0,1:T(8,128)}), f32[512,512]{0,1:T(8,128)}) %reduce-scatter.2.cloned.1.call-update) | async-done | bytes 1048592 | tf_op jit(solution)/shard_map/reduce_scatter | solution.py:167
  (85 shorter events, 61.7 us)
Async XLA Ops:
  6.5 197.9 %copy-start = (bf16[512,2048]{1,0:T(8,128)(2,1)S(1)}, bf16[512,2048]{1,0:T(8,128)(2,1)}, u32[]{:S(2)}) copy-start(bf16[512,2048]{1,0:T(8,128)(2,1)} %param.17) | copy-start | bytes 6291460
  6.5 66.2 %all-gather.7.cloned.1.call-start = ((), (), s32[]{:S(2)}) async-start(), calls=%async_computation.3 | async-start | bytes 2359296 | tf_op jit(solution)/shard_map/all_gather | solution.py:19
  10.8 27.9 %copy-start.13 = (f32[4]{0:T(128)S(1)}, f32[4]{0:T(128)}, u32[]{:S(2)}) copy-start(f32[4]{0:T(128)} %param.16) | copy-start | bytes 52
  18.6 104.0 %all-gather.5.cloned.1.call-start = ((), (), s32[]{:S(2)}) async-start(), calls=%async_computation.2 | async-start | bytes 2359296 | tf_op jit(solution)/shard_map/all_gather | solution.py:19
  22.9 228.0 %reduce-scatter.2.cloned.1.call-start = ((), (), s32[]{:S(2)}) async-start(), calls=%async_computation.1 | async-start | bytes 5242880 | tf_op jit(solution)/shard_map/reduce_scatter | solution.py:167
  22.9 173.5 %collective-permute-start.1 = (bf16[512,128]{1,0:T(8,128)(2,1)}, bf16[512,128]{1,0:T(8,128)(2,1)}, u32[]{:S(2)}, u32[]{:S(2)}) collective-permute-start(bf16[512,128]{1,0:T(8,128)(2,1)} %param.13), channel_id=1, source_target_pairs={{0,4},{4,8},{8,12},{12,16},{16,20},{20,24},{24,28},{1,5},{5,9},{9,... | collective-permute-start | bytes 393224 | tf_op jit(solution)/shard_map/ppermute | solution.py:34
  30.1 170.6 %collective-permute-start = (bf16[512,128]{0,1:T(8,128)(2,1)}, bf16[512,128]{0,1:T(8,128)(2,1)}, u32[]{:S(2)}, u32[]{:S(2)}) collective-permute-start(bf16[512,128]{0,1:T(8,128)(2,1)} %copy.27), channel_id=1, source_target_pairs={{0,4},{4,8},{8,12},{12,16},{16,20},{20,24},{24,28},{1,5},{5,9},{9,... | collective-permute-start | bytes 393224 | tf_op jit(solution)/shard_map/ppermute | solution.py:34
  136.4 9.5 %copy-start.1 = (f32[4,3,128,128]{3,2,1,0:T(8,128)S(1)}, f32[4,3,128,128]{3,2,1,0:T(8,128)}, u32[]{:S(2)}) copy-start(f32[4,3,128,128]{3,2,1,0:T(8,128)} %slice.8) | copy-start | bytes 2359300
  136.4 11.8 %copy-start.8 = (f32[4,4,128]{2,1,0:T(4,128)S(1)}, f32[4,4,128]{2,1,0:T(4,128)}, u32[]{:S(2)}) copy-start(f32[4,4,128]{2,1,0:T(4,128)} %get-tuple-element.184) | copy-start | bytes 24580
  136.4 11.8 %copy-start.14 = (f32[4]{0:T(128)S(1)}, f32[4]{0:T(128)}, u32[]{:S(2)}) copy-start(f32[4]{0:T(128)} %param.16) | copy-start | bytes 52
  145.9 9.5 %copy-start.7 = (f32[4,4,128]{2,1,0:T(4,128)S(1)}, f32[4,4,128]{2,1,0:T(4,128)}, u32[]{:S(2)}) copy-start(f32[4,4,128]{2,1,0:T(4,128)} %get-tuple-element.183) | copy-start | bytes 24580
  174.3 9.0 %copy-start.2 = (f32[4,128,4,128]{3,2,1,0:T(4,128)S(1)}, f32[4,128,4,128]{3,2,1,0:T(4,128)}, u32[]{:S(2)}) copy-start(f32[4,128,4,128]{3,2,1,0:T(4,128)} %reshape.303) | copy-start | bytes 3145732
  174.3 9.0 %copy-start.9 = (f32[4,4,128]{2,1,0:T(4,128)S(1)}, f32[4,4,128]{2,1,0:T(4,128)}, u32[]{:S(2)}) copy-start(f32[4,4,128]{2,1,0:T(4,128)} %get-tuple-element.170) | copy-start | bytes 24580
  174.3 9.0 %copy-start.10 = (f32[4,4,128]{2,1,0:T(4,128)S(1)}, f32[4,4,128]{2,1,0:T(4,128)}, u32[]{:S(2)}) copy-start(f32[4,4,128]{2,1,0:T(4,128)} %get-tuple-element.172) | copy-start | bytes 24580
  174.3 9.0 %copy-start.11 = (f32[4,4,128]{2,1,0:T(4,128)S(1)}, f32[4,4,128]{2,1,0:T(4,128)}, u32[]{:S(2)}) copy-start(f32[4,4,128]{2,1,0:T(4,128)} %get-tuple-element.178) | copy-start | bytes 24580
  174.3 9.0 %copy-start.12 = (f32[4,4,128]{2,1,0:T(4,128)S(1)}, f32[4,4,128]{2,1,0:T(4,128)}, u32[]{:S(2)}) copy-start(f32[4,4,128]{2,1,0:T(4,128)} %get-tuple-element.179) | copy-start | bytes 24580
  183.3 7.7 %copy-start.4 = (f32[4,128,128]{2,1,0:T(8,128)S(1)}, f32[4,128,128]{2,1,0:T(8,128)}, u32[]{:S(2)}) copy-start(f32[4,128,128]{2,1,0:T(8,128)} %get-tuple-element.134) | copy-start | bytes 786436
  183.3 12.8 %copy-start.15 = (f32[512]{0:T(512)S(1)}, f32[512]{0:T(512)}, u32[]{:S(2)}) copy-start(f32[512]{0:T(512)} %param.15) | copy-start | bytes 6148
  187.7 3.3 %copy-start.3 = (f32[4,4,128,128]{3,2,1,0:T(8,128)}, f32[4,4,128,128]{3,2,1,0:T(8,128)S(1)}, u32[]{:S(2)}) copy-start(f32[4,4,128,128]{3,2,1,0:T(8,128)S(1)} %fusion.27) | copy-start | bytes 3145732
  191.0 5.5 %copy-start.5 = (pred[512,1024]{0,1:T(8,128)(4,1)S(1)}, pred[512,1024]{0,1:T(8,128)(4,1)}, u32[]{:S(2)}) copy-start(pred[512,1024]{0,1:T(8,128)(4,1)} %compare_and_fusion) | copy-start | bytes 1572868
  191.0 5.5 %copy-start.6 = (bf16[512,128]{1,0:T(8,128)(2,1)S(1)}, bf16[512,128]{1,0:T(8,128)(2,1)}, u32[]{:S(2)}) copy-start(bf16[512,128]{1,0:T(8,128)(2,1)} %param.13) | copy-start | bytes 393220
Sparse Core Ops, SparseCore 0:
  18.8 53.9 all-gather.6
  74.8 47.7 all-gather.4
  207.8 43.0 reduce-scatter.1
where the time goes:
time: 265 us; the launch traced here: 260 us
  waiting for transfers between devices  119 us (45%)
  matrix products  80.9 us (31%)
  other arithmetic  26.1 us (10%)
  between operations  13.8 us (5%)
  local copies, waits for them, and re-layouts  10.5 us (4%)
  starting transfers between devices  9.54 us (4%)
    all_gather x2, waiting for transfers between devices, carried_in(): pieces = jax.tree.map(lambda part: lax.all_gather(part, axis), value)  75.7 us
    reduce_scatter x1, waiting for transfers between devices, shards(): lax.psum_scatter(lax.dot_general(out_weight, attended, (((0,), (1,)), (()...  43.2 us
    dot_general x8, matrix products, apply_state(): jnp.einsum('hcsj,hctj->hcts', keys_in, vectors, precision=HIGH) * lower_mask  22.3 us
    dot_general x8, matrix products, apply_state(): jnp.einsum('hcts,hcsi->hcti', intersection, row_vals, precision=HIGH)  21.3 us
    dot_general x8, matrix products, apply_state(): inter = jnp.einsum('hcij,hclj->hcli', states, vectors, precision=HIGH)  20.4 us
    select_n x7, other arithmetic, lap(): jnp.where(position < mine, new, old)  13.7 us
    ppermute x2, starting transfers between devices, from_behind(): return lax.ppermute(block, axis, route)  9.45 us
  transfers between devices with their start and end apart: 5, of which 3 were waited for; matrix products, arithmetic and copies ran while one was open for 37% of the time, Pallas kernels for 0%

commit v1 on v0

v1 whole, which is shorter than its diff:
```python
import functools
import math

import jax
import jax.numpy as jnp
from jax import lax
from jax.experimental import pallas as pl
from jax.experimental.pallas import tpu as pltpu
from jax.sharding import PartitionSpec as P

ITERS = 8
WINDOW = 512
EPS = 1e-06
HEAD = 128
HALF = HEAD // 2
CHUNK = 256
PACKED = HALF + 8
GROUPS = 2
FAR = -1e30
F32 = jnp.float32
BF16 = jnp.bfloat16


def dot(a, b):
    return jnp.dot(a, b, preferred_element_type=F32)


def split(x):
    high = x.astype(BF16)
    return high, (x - high.astype(F32)).astype(BF16)


def unit(x):
    x = x.astype(F32)
    return x * (lax.rsqrt(jnp.mean(x * x, axis=-1, keepdims=True) + EPS) * (1.0 / math.sqrt(HEAD)))


def iota(shape, dim):
    return lax.broadcasted_iota(jnp.int32, shape, dim)


def head_cols(h):
    return slice(h * HEAD, (h + 1) * HEAD)


def pack(m):
    top, low = m[:HALF], pltpu.roll(m[HALF:], HALF, 1)
    row, col = iota((HALF, HEAD), 0), iota((HALF, HEAD), 1)
    body = jnp.where((col >= HALF) | (row > col), top, low)
    diag = jnp.sum(jnp.where(row == col, top, 0.0), axis=0, keepdims=True)
    return body, jnp.broadcast_to(diag, (8, HEAD))


def unpack(p):
    body, diag = p[:HALF], p[HALF : HALF + 1]
    row, col = iota((HALF, HEAD), 0), iota((HALF, HEAD), 1)
    top = jnp.where((col >= HALF) | (row > col), body, 0.0) + jnp.where(row == col, 0.5 * diag, 0.0)
    low = jnp.where((col < HALF) & (row <= col), body, 0.0) * jnp.where(row == col, 0.5, 1.0)
    half = jnp.concatenate([top, pltpu.roll(low, HALF, 1)], 0)
    return half + half.T


def moments_kernel(heads, keys_ref, out_ref):
    for h in range(heads):
        rows = unit(keys_ref[:, head_cols(h)])
        high, low = split(rows)
        high_t, low_t = split(rows.T)
        both = dot(high_t, jnp.concatenate([high, low], 1))
        body, diag = pack(both[:, :HEAD] + both[:, HEAD:] + dot(low_t, high))
        out_ref[h, :HALF] = body
        out_ref[h, HALF:] = diag


def prepare_kernel(
    heads, base_ref, ridge_ref, q_ref, k_ref, v_ref,
    total_ref, lk_ref, lkt_ref, qt_ref, vt_ref, kst_ref, vst_ref, coef_ref,
):
    rows = q_ref.shape[0]
    chunks = rows // CHUNK
    for h in range(heads):
        cols = head_cols(h)
        keys = unit(k_ref[:, cols])
        high, low = split(keys)
        high_t, low_t = split(keys.T)
        both = jnp.concatenate([high, low], 1)
        vals_t = v_ref[:, cols].astype(F32).T.astype(BF16)
        vt_ref[h] = vals_t
        qt_ref[h] = unit(q_ref[:, cols]).T
        key_sum = val_sum = None
        for c in range(chunks):
            span = slice(c * CHUNK, (c + 1) * CHUNK)
            if c:
                kst_ref[h, c - 1] = key_sum
                vst_ref[h, c - 1] = val_sum
            lk_ref[h, c, :CHUNK] = jnp.concatenate([high[span], high[span]], 1)
            lk_ref[h, c, CHUNK:] = jnp.concatenate([low[span], low[span]], 1)
            lkt_ref[h, c, :HEAD] = high_t[:, span]
            lkt_ref[h, c, HEAD:] = low_t[:, span]
            mv = dot(vals_t[:, span], both[span])
            mv = mv[:, :HEAD] + mv[:, HEAD:]
            val_sum = mv if c == 0 else val_sum + mv
            if c + 1 < chunks:
                mk = dot(high_t[:, span], both[span])
                mk = mk[:, :HEAD] + mk[:, HEAD:] + dot(low_t[:, span], high[span])
                key_sum = mk if c == 0 else key_sum + mk
        total_ref[h] = val_sum
        ridge = ridge_ref[h]
        places = (iota((1, rows), 1) + (base_ref[0] + 1)).astype(F32)
        upper = ridge + places
        centre = (upper + ridge) * 0.5
        radius = (upper - ridge) * 0.5
        step = 1.0 / centre
        weight = jnp.zeros_like(step)
        for i in range(ITERS):
            if i:
                scaled = radius * step
                weight = scaled * scaled * (0.5 if i == 1 else 0.25)
                step = 1.0 / (centre - weight / step)
            coef_ref[h, i : i + 1] = step
            coef_ref[h, ITERS + i : ITERS + i + 1] = weight


def gathered(flags_ref, part_refs, h):
    total = None
    for i, ref in enumerate(part_refs):
        part = jnp.where(flags_ref[i] > 0, ref[h], 0.0)
        total = part if total is None else total + part
    return total


def stack_state(state):
    high, low = split(state)
    return jnp.concatenate(
        [jnp.concatenate([high, high], 1), jnp.concatenate([low, low], 1)], 0
    )


def chebyshev_kernel(heads, parts, flags_ref, ridge_ref, *refs):
    part_refs, refs = refs[:parts], refs[parts:]
    qt_ref, lk_ref, lkt_ref, kst_ref, coef_ref, solved_ref, state, res, direction = refs
    chunks = lk_ref.shape[1]
    for h in range(heads):
        prior = unpack(gathered(flags_ref, part_refs, h))
        for c in range(chunks):
            state[h, c] = stack_state(prior if c == 0 else prior + kst_ref[h, c - 1])
        res[h] = qt_ref[h]
        direction[h] = jnp.zeros_like(direction[h])
        solved_ref[h] = jnp.zeros_like(solved_ref[h])
    keep = iota((CHUNK, CHUNK), 0) <= iota((CHUNK, CHUNK), 1)

    def advance(i, h, span):
        step = coef_ref[h, pl.ds(i, 1), span]
        weight = coef_ref[h, pl.ds(ITERS + i, 1), span]
        residue = res[h, :, span]
        way = residue + weight * direction[h, :, span]
        solved_ref[h, :, span] = solved_ref[h, :, span] + step * way
        return step, residue, way

    def body(i, carry):
        for h in range(heads):
            ridge = ridge_ref[h]
            for c in range(chunks):
                span = slice(c * CHUNK, (c + 1) * CHUNK)
                step, residue, way = advance(i, h, span)
                direction[h, :, span] = way
                right = jnp.concatenate(split(way), 0)
                inner = dot(lk_ref[h, c], right)
                inner = jnp.where(keep, inner[:CHUNK] + inner[CHUNK:], 0.0)
                high, low = split(inner)
                image = dot(state[h, c], right) + dot(lkt_ref[h, c], high)
                image = image[:HEAD] + image[HEAD:] + dot(lkt_ref[h, c, :HEAD], low)
                res[h, :, span] = residue - step * (image + ridge * way)
        return carry

    lax.fori_loop(0, ITERS - 1, body, 0)
    for h in range(heads):
        for c in range(chunks):
            advance(ITERS - 1, h, slice(c * CHUNK, (c + 1) * CHUNK))


def attend_kernel(heads, parts, first, flags_ref, base_ref, *refs):
    part_refs, refs = refs[:parts], refs[parts:]
    solved_ref, lk_ref, vt_ref, vst_ref, gain_ref, kp_ref, ko_ref, vp_ref, vo_ref, out_ref, kk, vv = refs
    chunks = lk_ref.shape[1]
    rows = ko_ref.shape[0]
    kk[:WINDOW] = kp_ref[...]
    kk[WINDOW:] = ko_ref[...]
    vv[:, :WINDOW] = vp_ref[...].astype(F32).T.astype(BF16)
    vv[:, WINDOW:] = vo_ref[...].astype(F32).T.astype(BF16)
    keep = iota((CHUNK, CHUNK), 0) <= iota((CHUNK, CHUNK), 1)
    bias = jnp.where(base_ref[0] > 0, 0.0, FAR).astype(F32)
    key_at, query_at = iota((HEAD, HEAD), 0), iota((HEAD, HEAD), 1)
    tiles = WINDOW // HEAD
    scale = 1.0 / math.sqrt(HEAD)
    for h in range(heads):
        prior = gathered(flags_ref, part_refs, h)
        gain = jnp.broadcast_to(gain_ref[:, head_cols(first + h)], (HEAD, HEAD)).T
        for c in range(chunks):
            span = slice(c * CHUNK, (c + 1) * CHUNK)
            right = jnp.concatenate(split(solved_ref[h, :, span]), 0)
            inner = dot(lk_ref[h, c], right)
            high, low = split(jnp.where(keep, inner[:CHUNK] + inner[CHUNK:], 0.0))
            mixed = dot(stack_state(prior if c == 0 else prior + vst_ref[h, c - 1]), right)
            vals = vt_ref[h, :, span]
            mixed = mixed[:HEAD] + mixed[HEAD:] + dot(vals, high) + dot(vals, low)
            rate = lax.rsqrt(jnp.mean(mixed * mixed, axis=0, keepdims=True) + EPS)
            for b in range(CHUNK // HEAD):
                lanes = slice(b * HEAD, (b + 1) * HEAD)
                query = (mixed[:, lanes] * rate[:, lanes] * gain).astype(BF16)
                j = c * (CHUNK // HEAD) + b
                near = slice(j * HEAD, (j + tiles + 1) * HEAD)
                scores = dot(kk[near], query)
                pieces = []
                for t in range(tiles + 1):
                    piece = scores[t * HEAD : (t + 1) * HEAD]
                    if t == 0:
                        piece = jnp.where(key_at > query_at, piece, FAR)
                    if t == tiles:
                        piece = jnp.where(key_at <= query_at, piece, FAR)
                    if j + t < tiles:
                        piece = piece + bias
                    pieces.append(piece)
                scores = jnp.concatenate(pieces, 0)
                peak = jnp.max(scores, axis=0, keepdims=True)
                grown = jnp.exp((scores - peak) * scale)
                share = 1.0 / jnp.sum(grown, axis=0, keepdims=True)
                weights = (grown * share).astype(BF16)
                mixed_vals = dot(vv[:, near], weights)
                out_ref[j * HEAD : (j + 1) * HEAD, head_cols(h)] = mixed_vals.T.astype(BF16)


def project_kernel(count, *refs):
    out_ref = refs[-1]
    total = None
    for i in range(count):
        part = dot(refs[i][...], refs[count + i][...])
        total = part if total is None else total + part
    out_ref[...] = total.astype(BF16)


SMEM = pl.BlockSpec(memory_space=pltpu.SMEM)
VMEM = pl.BlockSpec(memory_space=pltpu.VMEM)


def call(kernel, outs, args, scalars=0, scratch=(), flops=0, nbytes=0):
    return pl.pallas_call(
        kernel,
        out_shape=outs,
        in_specs=[SMEM] * scalars + [VMEM] * (len(args) - scalars),
        out_specs=jax.tree.map(lambda _: VMEM, outs),
        scratch_shapes=list(scratch),
        compiler_params=pltpu.CompilerParams(vmem_limit_bytes=40 * 1024 * 1024),
        cost_estimate=pl.CostEstimate(flops=flops, bytes_accessed=nbytes, transcendentals=0),
    )(*args)


def rounds_of(count):
    stride, rounds = 1, []
    while stride < count:
        left = count // stride
        radix = 4 if left % 4 == 0 else 2 if left % 2 == 0 else left
        rounds.append((stride, radix))
        stride *= radix
    return rounds


def partner(i, stride, radix, k):
    digit = (i // stride) % radix
    other = digit ^ k if radix in (2, 4) else (digit + k) % radix
    return i + (other - digit) * stride


def swap(x, axis, stride, radix, k):
    n = lax.axis_size(axis)
    return lax.ppermute(x, axis, [(i, partner(i, stride, radix, k)) for i in range(n)])


def source_digit(mine, stride, radix, k):
    digit = (mine // stride) % radix
    return digit ^ k if radix in (2, 4) else (digit - k) % radix


def before(value, axis):
    mine = lax.axis_index(axis)
    parts = []
    rounds = rounds_of(lax.axis_size(axis))
    for at, (stride, radix) in enumerate(rounds):
        got = [swap(value, axis, stride, radix, k) for k in range(1, radix)]
        parts += got
        if at + 1 < len(rounds):
            value = functools.reduce(jnp.add, got, value)
    return parts


def before_flags(axis):
    mine = lax.axis_index(axis)
    flags = []
    for stride, radix in rounds_of(lax.axis_size(axis)):
        digit = (mine // stride) % radix
        flags += [source_digit(mine, stride, radix, k) < digit for k in range(1, radix)]
    return jnp.stack(flags).astype(jnp.int32)


def shards(
    mixer_queries, mixer_keys, mixer_values, window_keys, window_values, out_gain, ridge, out_weight
):
    rows = mixer_queries.shape[0]
    heads = ridge.shape[0]
    chunks = rows // CHUNK
    seq, head = lax.axis_size("seq"), lax.axis_size("head")
    base = (lax.axis_index("seq") * rows).astype(jnp.int32).reshape(1)
    flags = before_flags("seq")
    per = heads // GROUPS
    shape = jax.ShapeDtypeStruct

    totals = call(
        functools.partial(moments_kernel, heads), shape((heads, PACKED, HEAD), F32), (mixer_keys,)
    )
    key_parts = before(totals, "seq")

    prepared = call(
        functools.partial(prepare_kernel, heads),
        (
            shape((heads, HEAD, HEAD), F32),
            shape((heads, chunks, 2 * CHUNK, 2 * HEAD), BF16),
            shape((heads, chunks, 2 * HEAD, CHUNK), BF16),
            shape((heads, HEAD, rows), F32),
            shape((heads, HEAD, rows), BF16),
            shape((heads, chunks - 1, HEAD, HEAD), F32),
            shape((heads, chunks - 1, HEAD, HEAD), F32),
            shape((heads, 2 * ITERS, rows), F32),
        ),
        (base, ridge, mixer_queries, mixer_keys, mixer_values),
        scalars=2,
    )
    val_total, lk, lkt, qt, vt, kst, vst, coef = prepared
    val_parts = before(val_total, "seq")
    rim = lax.ppermute(
        jnp.concatenate([window_keys, window_values], 1)[rows - WINDOW :],
        "seq",
        [(i, (i + 1) % seq) for i in range(seq)],
    )
    width = window_keys.shape[1]
    kp, vp = rim[:, :width], rim[:, width:]

    mine = lax.axis_index("head")
    cols = out_weight.shape[1] // head
    weights = []
    for k in range(head):
        other = partner(mine, 1, head, k) if head not in (2, 4) else mine ^ k
        piece = lax.dynamic_slice_in_dim(out_weight, other * cols, cols, 1)
        weights.append(piece if k == 0 else swap(piece, "head", 1, head, k))

    lefts, rights = [], []
    for g in range(GROUPS):
        part = slice(g * per, (g + 1) * per)
        solved = call(
            functools.partial(chebyshev_kernel, per, len(key_parts)),
            shape((per, HEAD, rows), F32),
            (flags, ridge[part], *[p[part] for p in key_parts], qt[part], lk[part], lkt[part], kst[part], coef[part]),
            scalars=2,
            scratch=(
                pltpu.VMEM((per, chunks, 2 * HEAD, 2 * HEAD), BF16),
                pltpu.VMEM((per, HEAD, rows), F32),
                pltpu.VMEM((per, HEAD, rows), F32),
            ),
            flops=10**10,
        )
        attended = call(
            functools.partial(attend_kernel, per, len(val_parts), g * per),
            shape((rows, per * HEAD), BF16),
            (
                flags, base, *[p[part] for p in val_parts], solved, lk[part], vt[part], vst[part],
                out_gain.reshape(1, -1), kp, window_keys, vp, window_values,
            ),
            scalars=2,
            scratch=(pltpu.VMEM((WINDOW + rows, width), BF16), pltpu.VMEM((width, WINDOW + rows), BF16)),
            flops=4 * 10**9,
        )
        span = slice(g * per * HEAD, (g + 1) * per * HEAD)
        if head == 4:
            far = swap(attended, "head", 1, 4, 2)
            got = [attended, swap(attended, "head", 1, 4, 1), far, swap(far, "head", 1, 4, 1)]
        else:
            got = [attended] + [swap(attended, "head", 1, head, k) for k in range(1, head)]
        lefts += got
        rights += [w[span] for w in weights]
    return call(
        functools.partial(project_kernel, len(lefts)), shape((rows, cols), BF16), (*lefts, *rights)
    )


def solution(mesh):
    return jax.shard_map(
        shards,
        mesh=mesh,
        in_specs=(
            P("seq", "head"),
            P("seq", "head"),
            P("seq", "head"),
            P("seq", "head"),
            P("seq", "head"),
            P("head"),
            P("head"),
            P("head", None),
        ),
        out_specs=P("seq", "head"),
        check_vma=False,
    )
```

time: 265 us -> 100 us (0.38); the launches traced: 260 us -> 99.4 us
  waiting for transfers between devices: 119 us -> 16.8 us
  matrix products: 80.9 us -> 0 us
  Pallas kernels: 0 us -> 35.8 us
  other arithmetic: 26.1 us -> 2.99 us
  between operations: 13.8 us -> 0.48 us
  starting transfers between devices: 9.54 us -> 21.8 us
  local copies, waits for them, and re-layouts: 10.5 us -> 21.6 us
    dot_general x29 -> x0, matrix products: 80.9 us -> none  [the longest x8 22.3 us: apply_state(): jnp.einsum('hcsj,hctj->hcts', keys_in, vectors, precision=HIGH) * lower_mask]
    all_gather x2 -> x0, waiting for transfers between devices: 75.7 us -> none  [carried_in(): pieces = jax.tree.map(lambda part: lax.all_gather(part, axis), value)]
    reduce_scatter x1 -> x0, waiting for transfers between devices: 43.2 us -> none  [shards(): lax.psum_scatter(lax.dot_general(out_weight, attended, (((0,), (1,)), (()...]
    pallas_call x0 -> x7, Pallas kernels: none -> 35.8 us  [call(): pl.pallas_call(kernel, out_shape=outs, in_specs=[SMEM] * scalars + [VMEM]...]
    ppermute x2 -> x18, waiting for transfers between devices: 0.01 us -> 16.8 us  [the longest x17 16.8 us: swap(): lax.ppermute(x, axis, [(i, partner(i, stride, radix, k)) for i in range(n)])]
    select_n x7 -> x0, other arithmetic: 13.7 us -> none  [lap(): jnp.where(position < mine, new, old)]
    ppermute x2 -> x18, starting transfers between devices: 9.45 us -> 21.8 us  [the longest x17 19.7 us: swap(): lax.ppermute(x, axis, [(i, partner(i, stride, radix, k)) for i in range(n)])]
    slice x2 -> x21, local copies, waits for them, and re-layouts: 1.9 us -> 10.5 us  [the longest x8 4.91 us: shards(): p[part]]
  transfers between devices with their start and end apart: 5 -> 18, of which waited for: 3 -> 4; matrix products, arithmetic and copies ran while one was open for 37% -> 15% of each run, Pallas kernels for 0% -> 33%
where the time goes in v1:
time: 100 us; the launch traced here: 99.4 us
  Pallas kernels  35.8 us (36%)
  starting transfers between devices  21.8 us (22%)
  local copies, waits for them, and re-layouts  21.6 us (22%)
  waiting for transfers between devices  16.8 us (17%)
  other arithmetic  2.99 us (3%)
    pallas_call x7, Pallas kernels, call(): pl.pallas_call(kernel, out_shape=outs, in_specs=[SMEM] * scalars + [VMEM]...  35.8 us
    ppermute x17, starting transfers between devices, swap(): lax.ppermute(x, axis, [(i, partner(i, stride, radix, k)) for i in range(n)])  19.7 us
    ppermute x17, waiting for transfers between devices, swap(): lax.ppermute(x, axis, [(i, partner(i, stride, radix, k)) for i in range(n)])  16.8 us
    unnamed x54, local copies, waits for them, and re-layouts  9.63 us
    slice x8, local copies, waits for them, and re-layouts, shards(): p[part]  4.91 us
    add x2, other arithmetic, before(): value = functools.reduce(jnp.add, got, value)  2.18 us
    ppermute x1, starting transfers between devices, shards(): lax.ppermute(jnp.concatenate([window_keys, window_values], 1)[rows - WIND...  2.13 us
  transfers between devices with their start and end apart: 18, of which 4 were waited for; matrix products, arithmetic and copies ran while one was open for 15% of the time, Pallas kernels for 33%

profile of v1, /device:TPU:0, one launch (start us, length us, event | category | flops | bytes accessed | tf_op | source)
XLA Modules:
  0.0 99.4 jit_solution(13375825856999068509)
XLA Ops:
  1.0 1.2 %shard_map.83 = f32[4,72,128]{2,1,0:T(8,128)S(1)} custom-call(bf16[512,512]{1,0:T(8,128)(2,1)S(1)} %copy-done), custom_call_target="tpu_custom_call" | custom-call | tf_op jit(solution)/shard_map/pallas_call | solution.py:246
  2.2 3.0 %collective-permute-start.4 = (f32[4,72,128]{2,1,0:T(8,128)S(1)}, f32[4,72,128]{2,1,0:T(8,128)}, u32[]{:S(2)}, u32[]{:S(2)}) collective-permute-start(f32[4,72,128]{2,1,0:T(8,128)S(1)} %shard_map.83), channel_id=1, source_target_pairs={{0,4},{4,0},{8,12},{12,8},{16,20},{20,16},{24,28},{28,24},{1,5},{5... | collective-permute-start | bytes 442376 | tf_op jit(solution)/shard_map/ppermute | solution.py:275
  5.2 1.6 %collective-permute-start.5 = (f32[4,72,128]{2,1,0:T(8,128)S(1)}, f32[4,72,128]{2,1,0:T(8,128)}, u32[]{:S(2)}, u32[]{:S(2)}) collective-permute-start(f32[4,72,128]{2,1,0:T(8,128)S(1)} %shard_map.83), channel_id=1, source_target_pairs={{0,8},{4,12},{8,0},{12,4},{16,24},{20,28},{24,16},{28,20},{1,9},{5... | collective-permute-start | bytes 442376 | tf_op jit(solution)/shard_map/ppermute | solution.py:275
  10.6 2.1 %shard_map.82 = (f32[4,128,128]{2,1,0:T(8,128)S(1)}, bf16[4,2,512,256]{3,2,1,0:T(8,128)(2,1)S(1)}, bf16[4,2,256,256]{3,2,1,0:T(8,128)(2,1)S(1)}, f32[4,128,512]{...) custom-call(s32[1]{0:T(128)} %bitcast.4.base_ref, ...), custom_call_target="tpu_custom_call" | custom-call | tf_op jit(solution)/shard_map/pallas_call | solution.py:246
  16.6 1.9 %collective-permute-start = (f32[4,128,128]{2,1,0:T(8,128)S(1)}, f32[4,128,128]{2,1,0:T(8,128)}, u32[]{:S(2)}, u32[]{:S(2)}) collective-permute-start(f32[4,128,128]{2,1,0:T(8,128)S(1)} %get-tuple-element.13), channel_id=1, source_target_pairs={{0,4},{4,0},{8,12},{12,8},{16,20},{20,16},{24,28},{28,24},{1,5},{5... | collective-permute-start | bytes 786440 | tf_op jit(solution)/shard_map/ppermute | solution.py:275
  18.5 1.6 %collective-permute-start.1 = (f32[4,128,128]{2,1,0:T(8,128)S(1)}, f32[4,128,128]{2,1,0:T(8,128)}, u32[]{:S(2)}, u32[]{:S(2)}) collective-permute-start(f32[4,128,128]{2,1,0:T(8,128)S(1)} %get-tuple-element.13), channel_id=1, source_target_pairs={{0,8},{4,12},{8,0},{12,4},{16,24},{20,28},{24,16},{28,20},{1,9},{5... | collective-permute-start | bytes 786440 | tf_op jit(solution)/shard_map/ppermute | solution.py:275
  20.1 1.3 %fusion.20 = (f32[2]{0:T(128)}, f32[2]{0:T(128)}) fusion(f32[4]{0:T(128)} %ridge_ref.1), kind=kLoop, calls=%fused_computation.28 | loop fusion | bytes 32 | tf_op jit(solution)/shard_map/slice | solution.py:360
  21.4 1.5 %fusion.1 = (bf16[2,2,512,256]{3,2,1,0:T(8,128)(2,1)}, bf16[2,2,512,256]{3,2,1,0:T(8,128)(2,1)}) fusion(bf16[4,2,512,256]{3,2,1,0:T(8,128)(2,1)S(1)} %get-tuple-element.15), kind=kLoop, calls=%fused_computation.9 | loop fusion | bytes 4194304 | tf_op jit(solution)/shard_map/slice | solution.py:360
  26.3 1.5 %constant_dynamic-slice_fusion.1 = (bf16[512,512]{1,0:T(8,128)(2,1)S(1)}, bf16[512,512]{1,0:T(8,128)(2,1)S(1)}, bf16[512,512]{1,0:T(8,128)(2,1)S(1)}) fusion(bf16[512,2048]{1,0:T(8,128)(2,1)} %param.15, s32[]{:T(128)S(6)} %select_n.46, s32[]{:T(128)S(6)} %select_n.44, s32[]{:T(128)S(6)} %select_n.45), kind=kLoop, calls=%fused_computation.5 | loop fusion | bytes 3145740 | tf_op jit(solution)/shard_map/dynamic_slice | solution.py:351
  28.8 2.1 %collective-permute-start.8 = (bf16[512,256]{1,0:T(8,128)(2,1)S(1)}, bf16[512,256]{1,0:T(8,128)(2,1)S(1)}, u32[]{:S(2)}, u32[]{:S(2)}) collective-permute-start(bf16[512,256]{1,0:T(8,128)(2,1)S(1)} %copy-done.26), channel_id=1, source_target_pairs={{0,4},{4,8},{8,12},{12,16},{16,20},{20,24},{24,28},{28,0},{1,5},{5... | collective-permute-start | bytes 786440 | tf_op jit(solution)/shard_map/ppermute | solution.py:338
  31.0 1.1 %add_add_fusion.1 = f32[4,72,128]{2,1,0:T(8,128)S(1)} fusion(f32[4,72,128]{2,1,0:T(8,128)} %collective-permute-done.6, f32[4,72,128]{2,1,0:T(8,128)} %collective-permute-done.5, f32[4,72,128]{2,1,0:T(8,128)S(1)} %shard_map.83, f32[4,72,128]{2,1,0:T(8,128)} %collective-permute-done.4), kind=kLoop, calls=%fused_computation.2 | loop fusion | flops 110592 | bytes 737280 | tf_op jit(solution)/shard_map/add | solution.py:291
  34.0 1.3 %collective-permute-done.2 = f32[4,128,128]{2,1,0:T(8,128)S(1)} collective-permute-done((f32[4,128,128]{2,1,0:T(8,128)S(1)}, f32[4,128,128]{2,1,0:T(8,128)S(1)}, u32[]{:S(2)}, u32[]{:S(2)}) %collective-permute-start.2) | collective-permute-done | bytes 262176 | tf_op jit(solution)/shard_map/ppermute | solution.py:275
  35.4 1.5 %collective-permute-start.16 = (bf16[512,512]{1,0:T(8,128)(2,1)S(1)}, bf16[512,512]{1,0:T(8,128)(2,1)S(1)}, u32[]{:S(2)}, u32[]{:S(2)}) collective-permute-start(bf16[512,512]{1,0:T(8,128)(2,1)S(1)} %get-tuple-element.25), channel_id=1, source_target_pairs={{0,2},{1,3},{2,0},{3,1},{4,6},{5,7},{6,4},{7,5},{8,10},{9,11},{10,... | collective-permute-start | bytes 1572872 | tf_op jit(solution)/shard_map/ppermute | solution.py:275
  38.0 7.0 %collective-permute-start.7 = (f32[4,72,128]{2,1,0:T(8,128)S(1)}, f32[4,72,128]{2,1,0:T(8,128)S(1)}, u32[]{:S(2)}, u32[]{:S(2)}) collective-permute-start(f32[4,72,128]{2,1,0:T(8,128)S(1)} %add_add_fusion.1), channel_id=1, source_target_pairs={{0,16},{4,20},{8,24},{12,28},{16,0},{20,4},{24,8},{28,12},{1,17},{... | collective-permute-start | bytes 442376 | tf_op jit(solution)/shard_map/ppermute | solution.py:275
  46.0 1.1 %add_add_fusion = f32[4,128,128]{2,1,0:T(8,128)S(1)} fusion(f32[4,128,128]{2,1,0:T(8,128)S(1)} %collective-permute-done.2, f32[4,128,128]{2,1,0:T(8,128)} %collective-permute-done.1, f32[4,128,128]{2,1,0:T(8,128)S(1)} %get-tuple-element.13, f32[4,128,128]{2,1,0:T(8,128)} %collective-permute-done), kind=kLoop, calls=%fused_computation.1 | loop fusion | flops 196608 | bytes 1310720 | tf_op jit(solution)/shard_map/add | solution.py:291
  47.2 9.3 %collective-permute-done.7 = f32[4,72,128]{2,1,0:T(8,128)S(1)} collective-permute-done((f32[4,72,128]{2,1,0:T(8,128)S(1)}, f32[4,72,128]{2,1,0:T(8,128)S(1)}, u32[]{:S(2)}, u32[]{:S(2)}) %collective-permute-start.7) | collective-permute-done | bytes 147488 | tf_op jit(solution)/shard_map/ppermute | solution.py:275
  56.6 9.9 %shard_map.86.refs_4_ = f32[2,128,512]{2,1,0:T(8,128)S(1)} custom-call(s32[4]{0:T(128)S(1)} %add_convert_fusion.flags_ref, f32[2]{0:T(128)S(1)} %copy-done.24, f32[2,72,128]{2,1,0:T(8,128)S(1)} %get-tuple-element.60.refs_0_, f32[2,72,128]{2,1,0:T(8,128)S(1)} %get-tuple-element.58.refs_1_, f32[2,72,128]{2,1,0:T(8,128)S(1)} %get-tuple-element.56.refs_2_, ...), custom_call_target="tpu_custom_call" | custom-call | flops 10000000000 | tf_op jit(solution)/shard_map/pallas_call | solution.py:246
  66.6 9.9 %shard_map.84.refs_4_ = f32[2,128,512]{2,1,0:T(8,128)S(1)} custom-call(s32[4]{0:T(128)S(1)} %add_convert_fusion.flags_ref, f32[2]{0:T(128)S(1)} %copy-done.23, f32[2,72,128]{2,1,0:T(8,128)S(1)} %get-tuple-element.61.refs_0_, f32[2,72,128]{2,1,0:T(8,128)S(1)} %get-tuple-element.59.refs_1_, f32[2,72,128]{2,1,0:T(8,128)S(1)} %get-tuple-element.57.refs_2_, ...), custom_call_target="tpu_custom_call" | custom-call | flops 10000000000 | tf_op jit(solution)/shard_map/pallas_call | solution.py:246
  76.6 5.3 %shard_map.87.refs_4_ = bf16[512,256]{1,0:T(8,128)(2,1)S(1)} custom-call(s32[4]{0:T(128)S(1)} %add_convert_fusion.flags_ref, s32[1]{0:T(128)} %bitcast.4.base_ref, f32[2,128,128]{2,1,0:T(8,128)S(1)} %get-tuple-element.50.refs_0_, f32[2,128,128]{2,1,0:T(8,128)S(1)} %get-tuple-element.48.refs_1_, f32[2,128,128]{2,1,0:T(8,128)S(1)} %get-tuple-element.46.refs_2_, ...), custom_call_target="tpu_custom_call" | custom-call | flops 4000000000 | tf_op jit(solution)/shard_map/pallas_call | solution.py:246
  82.5 5.3 %shard_map.85.refs_0_ = bf16[512,256]{1,0:T(8,128)(2,1)S(1)} custom-call(s32[4]{0:T(128)S(1)} %add_convert_fusion.flags_ref, s32[1]{0:T(128)} %bitcast.4.base_ref, f32[2,128,128]{2,1,0:T(8,128)S(1)} %get-tuple-element.51.refs_0_, f32[2,128,128]{2,1,0:T(8,128)S(1)} %get-tuple-element.49.refs_1_, f32[2,128,128]{2,1,0:T(8,128)S(1)} %get-tuple-element.47.refs_2_, ...), custom_call_target="tpu_custom_call" | custom-call | flops 4000000000 | tf_op jit(solution)/shard_map/pallas_call | solution.py:246
  87.7 1.6 %collective-permute-start.10 = (bf16[512,256]{1,0:T(8,128)(2,1)S(1)}, bf16[512,256]{1,0:T(8,128)(2,1)S(1)}, u32[]{:S(2)}, u32[]{:S(2)}) collective-permute-start(bf16[512,256]{1,0:T(8,128)(2,1)S(1)} %shard_map.85.refs_0_), channel_id=1, source_target_pairs={{0,2},{1,3},{2,0},{3,1},{4,6},{5,7},{6,4},{7,5},{8,10},{9,11},{10,... | collective-permute-start | bytes 786440 | tf_op jit(solution)/shard_map/ppermute | solution.py:275
  91.1 4.7 %collective-permute-done.10.refs_2_ = bf16[512,256]{1,0:T(8,128)(2,1)S(1)} collective-permute-done((bf16[512,256]{1,0:T(8,128)(2,1)S(1)}, bf16[512,256]{1,0:T(8,128)(2,1)S(1)}, u32[]{:S(2)}, u32[]{:S(2)}) %collective-permute-start.10) | collective-permute-done | bytes 262176 | tf_op jit(solution)/shard_map/ppermute | solution.py:275
  96.0 1.4 %collective-permute-done.11.refs_3_ = bf16[512,256]{1,0:T(8,128)(2,1)S(1)} collective-permute-done((bf16[512,256]{1,0:T(8,128)(2,1)S(1)}, bf16[512,256]{1,0:T(8,128)(2,1)S(1)}, u32[]{:S(2)}, u32[]{:S(2)}) %collective-permute-start.11) | collective-permute-done | bytes 262176 | tf_op jit(solution)/shard_map/ppermute | solution.py:275
  97.4 2.0 %shard_map.88 = bf16[512,512]{1,0:T(8,128)(2,1)} custom-call(bf16[512,256]{1,0:T(8,128)(2,1)S(1)} %shard_map.85.refs_0_, bf16[512,256]{1,0:T(8,128)(2,1)S(1)} %collective-permute-done.9.refs_1_, bf16[512,256]{1,0:T(8,128)(2,1)S(1)} %collective-permute-done.10.refs_2_, bf16[512,256]{1,0:T(8,128)(2,1)S(1)} %collective-permute-done.11.refs_3_, ...), custom_call_target="tpu_custom_call" | custom-call | tf_op jit(solution)/shard_map/pallas_call | solution.py:246
  (99 shorter events, 19.7 us)
Async XLA Ops:
  2.2 26.6 %collective-permute-start.4 = (f32[4,72,128]{2,1,0:T(8,128)S(1)}, f32[4,72,128]{2,1,0:T(8,128)}, u32[]{:S(2)}, u32[]{:S(2)}) collective-permute-start(f32[4,72,128]{2,1,0:T(8,128)S(1)} %shard_map.83), channel_id=1, source_target_pairs={{0,4},{4,0},{8,12},{12,8},{16,20},{20,16},{24,28},{28,24},{1,5},{5... | collective-permute-start | bytes 442376 | tf_op jit(solution)/shard_map/ppermute | solution.py:275
  5.2 25.7 %collective-permute-start.5 = (f32[4,72,128]{2,1,0:T(8,128)S(1)}, f32[4,72,128]{2,1,0:T(8,128)}, u32[]{:S(2)}, u32[]{:S(2)}) collective-permute-start(f32[4,72,128]{2,1,0:T(8,128)S(1)} %shard_map.83), channel_id=1, source_target_pairs={{0,8},{4,12},{8,0},{12,4},{16,24},{20,28},{24,16},{28,20},{1,9},{5... | collective-permute-start | bytes 442376 | tf_op jit(solution)/shard_map/ppermute | solution.py:275
  6.8 21.0 %collective-permute-start.6 = (f32[4,72,128]{2,1,0:T(8,128)S(1)}, f32[4,72,128]{2,1,0:T(8,128)}, u32[]{:S(2)}, u32[]{:S(2)}) collective-permute-start(f32[4,72,128]{2,1,0:T(8,128)S(1)} %shard_map.83), channel_id=1, source_target_pairs={{0,12},{4,8},{8,4},{12,0},{16,28},{20,24},{24,20},{28,16},{1,13},{... | collective-permute-start | bytes 442376 | tf_op jit(solution)/shard_map/ppermute | solution.py:275
  16.6 21.4 %collective-permute-start = (f32[4,128,128]{2,1,0:T(8,128)S(1)}, f32[4,128,128]{2,1,0:T(8,128)}, u32[]{:S(2)}, u32[]{:S(2)}) collective-permute-start(f32[4,128,128]{2,1,0:T(8,128)S(1)} %get-tuple-element.13), channel_id=1, source_target_pairs={{0,4},{4,0},{8,12},{12,8},{16,20},{20,16},{24,28},{28,24},{1,5},{5... | collective-permute-start | bytes 786440 | tf_op jit(solution)/shard_map/ppermute | solution.py:275
  18.5 18.4 %collective-permute-start.1 = (f32[4,128,128]{2,1,0:T(8,128)S(1)}, f32[4,128,128]{2,1,0:T(8,128)}, u32[]{:S(2)}, u32[]{:S(2)}) collective-permute-start(f32[4,128,128]{2,1,0:T(8,128)S(1)} %get-tuple-element.13), channel_id=1, source_target_pairs={{0,8},{4,12},{8,0},{12,4},{16,24},{20,28},{24,16},{28,20},{1,9},{5... | collective-permute-start | bytes 786440 | tf_op jit(solution)/shard_map/ppermute | solution.py:275
  27.8 7.6 %collective-permute-start.2 = (f32[4,128,128]{2,1,0:T(8,128)S(1)}, f32[4,128,128]{2,1,0:T(8,128)S(1)}, u32[]{:S(2)}, u32[]{:S(2)}) collective-permute-start(f32[4,128,128]{2,1,0:T(8,128)S(1)} %get-tuple-element.13), channel_id=1, source_target_pairs={{0,12},{4,8},{8,4},{12,0},{16,28},{20,24},{24,20},{28,16},{1,13},{... | collective-permute-start | bytes 786440 | tf_op jit(solution)/shard_map/ppermute | solution.py:275
  28.8 18.2 %collective-permute-start.8 = (bf16[512,256]{1,0:T(8,128)(2,1)S(1)}, bf16[512,256]{1,0:T(8,128)(2,1)S(1)}, u32[]{:S(2)}, u32[]{:S(2)}) collective-permute-start(bf16[512,256]{1,0:T(8,128)(2,1)S(1)} %copy-done.26), channel_id=1, source_target_pairs={{0,4},{4,8},{8,12},{12,16},{16,20},{20,24},{24,28},{28,0},{1,5},{5... | collective-permute-start | bytes 786440 | tf_op jit(solution)/shard_map/ppermute | solution.py:338
  31.0 59.4 %collective-permute-start.17 = (bf16[512,512]{1,0:T(8,128)(2,1)S(1)}, bf16[512,512]{1,0:T(8,128)(2,1)S(1)}, u32[]{:S(2)}, u32[]{:S(2)}) collective-permute-start(bf16[512,512]{1,0:T(8,128)(2,1)S(1)} %get-tuple-element.23), channel_id=1, source_target_pairs={{0,3},{1,2},{2,1},{3,0},{4,7},{5,6},{6,5},{7,4},{8,11},{9,10},{10,... | collective-permute-start | bytes 1572872 | tf_op jit(solution)/shard_map/ppermute | solution.py:275
  32.0 24.5 %copy-start.5 = (bf16[2,2,512,256]{3,2,1,0:T(8,128)(2,1)S(1)}, bf16[2,2,512,256]{3,2,1,0:T(8,128)(2,1)}, u32[]{:S(2)}) copy-start(bf16[2,2,512,256]{3,2,1,0:T(8,128)(2,1)} %get-tuple-element.26.refs_5_) | copy-start | bytes 3145732
  32.1 24.5 %copy-start.19 = (f32[2,1,128,128]{3,2,1,0:T(8,128)S(1)}, f32[2,1,128,128]{3,2,1,0:T(8,128)}, u32[]{:S(2)}) copy-start(f32[2,1,128,128]{3,2,1,0:T(8,128)} %get-tuple-element.42.refs_7_) | copy-start | bytes 393220
  32.1 24.5 %copy-start.21 = (f32[2,16,512]{2,1,0:T(8,128)S(1)}, f32[2,16,512]{2,1,0:T(8,128)}, u32[]{:S(2)}) copy-start(f32[2,16,512]{2,1,0:T(8,128)} %get-tuple-element.62.refs_8_) | copy-start | bytes 196612
  32.1 24.5 %copy-start.24 = (f32[2]{0:T(128)S(1)}, f32[2]{0:T(128)}, u32[]{:S(2)}) copy-start(f32[2]{0:T(128)} %get-tuple-element.64.ridge_ref) | copy-start | bytes 28
  35.4 55.1 %collective-permute-start.16 = (bf16[512,512]{1,0:T(8,128)(2,1)S(1)}, bf16[512,512]{1,0:T(8,128)(2,1)S(1)}, u32[]{:S(2)}, u32[]{:S(2)}) collective-permute-start(bf16[512,512]{1,0:T(8,128)(2,1)S(1)} %get-tuple-element.25), channel_id=1, source_target_pairs={{0,2},{1,3},{2,0},{3,1},{4,6},{5,7},{6,4},{7,5},{8,10},{9,11},{10,... | collective-permute-start | bytes 1572872 | tf_op jit(solution)/shard_map/ppermute | solution.py:275
  36.9 59.0 %collective-permute-start.15 = (bf16[512,512]{1,0:T(8,128)(2,1)S(1)}, bf16[512,512]{1,0:T(8,128)(2,1)S(1)}, u32[]{:S(2)}, u32[]{:S(2)}) collective-permute-start(bf16[512,512]{1,0:T(8,128)(2,1)S(1)} %get-tuple-element.24), channel_id=1, source_target_pairs={{0,1},{1,0},{2,3},{3,2},{4,5},{5,4},{6,7},{7,6},{8,9},{9,8},{10,11... | collective-permute-start | bytes 1572872 | tf_op jit(solution)/shard_map/ppermute | solution.py:275
  38.0 18.5 %collective-permute-start.7 = (f32[4,72,128]{2,1,0:T(8,128)S(1)}, f32[4,72,128]{2,1,0:T(8,128)S(1)}, u32[]{:S(2)}, u32[]{:S(2)}) collective-permute-start(f32[4,72,128]{2,1,0:T(8,128)S(1)} %add_add_fusion.1), channel_id=1, source_target_pairs={{0,16},{4,20},{8,24},{12,28},{16,0},{20,4},{24,8},{28,12},{1,17},{... | collective-permute-start | bytes 442376 | tf_op jit(solution)/shard_map/ppermute | solution.py:275
  47.1 29.5 %collective-permute-start.3 = (f32[4,128,128]{2,1,0:T(8,128)S(1)}, f32[4,128,128]{2,1,0:T(8,128)S(1)}, u32[]{:S(2)}, u32[]{:S(2)}) collective-permute-start(f32[4,128,128]{2,1,0:T(8,128)S(1)} %add_add_fusion), channel_id=1, source_target_pairs={{0,16},{4,20},{8,24},{12,28},{16,0},{20,4},{24,8},{28,12},{1,17},{... | collective-permute-start | bytes 786440 | tf_op jit(solution)/shard_map/ppermute | solution.py:275
  56.5 10.0 %copy-start.4 = (bf16[2,2,512,256]{3,2,1,0:T(8,128)(2,1)S(1)}, bf16[2,2,512,256]{3,2,1,0:T(8,128)(2,1)}, u32[]{:S(2)}) copy-start(bf16[2,2,512,256]{3,2,1,0:T(8,128)(2,1)} %get-tuple-element.27.refs_5_) | copy-start | bytes 3145732
  66.6 10.0 %copy-start.25 = (f32[512]{0:T(512)S(1)}, f32[512]{0:T(512)}, u32[]{:S(2)}) copy-start(f32[512]{0:T(512)} %param.13) | copy-start | bytes 6148
  81.9 9.2 %collective-permute-start.13 = (bf16[512,256]{1,0:T(8,128)(2,1)S(1)}, bf16[512,256]{1,0:T(8,128)(2,1)S(1)}, u32[]{:S(2)}, u32[]{:S(2)}) collective-permute-start(bf16[512,256]{1,0:T(8,128)(2,1)S(1)} %shard_map.87.refs_4_), channel_id=1, source_target_pairs={{0,2},{1,3},{2,0},{3,1},{4,6},{5,7},{6,4},{7,5},{8,10},{9,11},{10,... | collective-permute-start | bytes 786440 | tf_op jit(solution)/shard_map/ppermute | solution.py:275
  87.7 8.1 %collective-permute-start.10 = (bf16[512,256]{1,0:T(8,128)(2,1)S(1)}, bf16[512,256]{1,0:T(8,128)(2,1)S(1)}, u32[]{:S(2)}, u32[]{:S(2)}) collective-permute-start(bf16[512,256]{1,0:T(8,128)(2,1)S(1)} %shard_map.85.refs_0_), channel_id=1, source_target_pairs={{0,2},{1,3},{2,0},{3,1},{4,6},{5,7},{6,4},{7,5},{8,10},{9,11},{10,... | collective-permute-start | bytes 786440 | tf_op jit(solution)/shard_map/ppermute | solution.py:275
  90.3 5.6 %collective-permute-start.12 = (bf16[512,256]{1,0:T(8,128)(2,1)S(1)}, bf16[512,256]{1,0:T(8,128)(2,1)S(1)}, u32[]{:S(2)}, u32[]{:S(2)}) collective-permute-start(bf16[512,256]{1,0:T(8,128)(2,1)S(1)} %shard_map.87.refs_4_), channel_id=1, source_target_pairs={{0,1},{1,0},{2,3},{3,2},{4,5},{5,4},{6,7},{7,6},{8,9},{9,8},{10,11... | collective-permute-start | bytes 786440 | tf_op jit(solution)/shard_map/ppermute | solution.py:275
  90.5 5.5 %collective-permute-start.9 = (bf16[512,256]{1,0:T(8,128)(2,1)S(1)}, bf16[512,256]{1,0:T(8,128)(2,1)S(1)}, u32[]{:S(2)}, u32[]{:S(2)}) collective-permute-start(bf16[512,256]{1,0:T(8,128)(2,1)S(1)} %shard_map.85.refs_0_), channel_id=1, source_target_pairs={{0,1},{1,0},{2,3},{3,2},{4,5},{5,4},{6,7},{7,6},{8,9},{9,8},{10,11... | collective-permute-start | bytes 786440 | tf_op jit(solution)/shard_map/ppermute | solution.py:275
  91.0 4.9 %collective-permute-start.14 = (bf16[512,256]{1,0:T(8,128)(2,1)S(1)}, bf16[512,256]{1,0:T(8,128)(2,1)S(1)}, u32[]{:S(2)}, u32[]{:S(2)}) collective-permute-start(bf16[512,256]{1,0:T(8,128)(2,1)S(1)} %collective-permute-done.13.refs_6_), channel_id=1, source_target_pairs={{0,1},{1,0},{2,3},{3,2},{4,5},{5,4},{6,7},{7,6},{8,9},{9,8},{10,11... | collective-permute-start | bytes 786440 | tf_op jit(solution)/shard_map/ppermute | solution.py:275
  95.8 1.5 %collective-permute-start.11 = (bf16[512,256]{1,0:T(8,128)(2,1)S(1)}, bf16[512,256]{1,0:T(8,128)(2,1)S(1)}, u32[]{:S(2)}, u32[]{:S(2)}) collective-permute-start(bf16[512,256]{1,0:T(8,128)(2,1)S(1)} %collective-permute-done.10.refs_2_), channel_id=1, source_target_pairs={{0,1},{1,0},{2,3},{3,2},{4,5},{5,4},{6,7},{7,6},{8,9},{9,8},{10,11... | collective-permute-start | bytes 786440 | tf_op jit(solution)/shard_map/ppermute | solution.py:275
  (21 other events, 54.6 us)

commit v2 on v1

v2 whole, which is shorter than its diff:
```python
import functools
import math

import jax
import jax.numpy as jnp
from jax import lax
from jax.experimental import pallas as pl
from jax.experimental.pallas import tpu as pltpu
from jax.sharding import PartitionSpec as P

ITERS = 8
WINDOW = 512
EPS = 1e-06
HEAD = 128
HALF = HEAD // 2
CHUNK = 256
PACKED = HALF + 8
GROUPS = 2
FAR = -1e30
F32 = jnp.float32
BF16 = jnp.bfloat16


def dot(a, b):
    return jnp.dot(a, b, preferred_element_type=F32)


def split(x):
    high = x.astype(BF16)
    return high, (x - high.astype(F32)).astype(BF16)


def rate(x):
    return lax.rsqrt(jnp.mean(x * x, axis=-1, keepdims=True) + EPS) * (1.0 / math.sqrt(HEAD))


def unit(x):
    x = x.astype(F32)
    return x * rate(x)


def iota(shape, dim):
    return lax.broadcasted_iota(jnp.int32, shape, dim)


def head_cols(h):
    return slice(h * HEAD, (h + 1) * HEAD)


def pack(m):
    top, low = m[:HALF], pltpu.roll(m[HALF:], HALF, 1)
    row, col = iota((HALF, HEAD), 0), iota((HALF, HEAD), 1)
    body = jnp.where((col >= HALF) | (row > col), top, low)
    diag = jnp.sum(jnp.where(row == col, top, 0.0), axis=0, keepdims=True)
    return body, jnp.broadcast_to(diag, (8, HEAD))


def unpack(p):
    body, diag = p[:HALF], p[HALF : HALF + 1]
    row, col = iota((HALF, HEAD), 0), iota((HALF, HEAD), 1)
    top = jnp.where((col >= HALF) | (row > col), body, 0.0) + jnp.where(row == col, 0.5 * diag, 0.0)
    low = jnp.where((col < HALF) & (row <= col), body, 0.0) * jnp.where(row == col, 0.5, 1.0)
    half = jnp.concatenate([top, pltpu.roll(low, HALF, 1)], 0)
    return half + half.T


def moments_kernel(heads, keys_ref, out_ref):
    for h in range(heads):
        rows = keys_ref[:, head_cols(h)].astype(F32)
        scale = rate(rows)
        both = dot(rows.T.astype(BF16), jnp.concatenate(split(rows * (scale * scale)), 1))
        body, diag = pack(both[:, :HEAD] + both[:, HEAD:])
        out_ref[h, :HALF] = body
        out_ref[h, HALF:] = diag


def prepare_kernel(
    heads, groups, base_ref, ridge_ref, q_ref, k_ref, v_ref, wk_ref, wv_ref, total_ref, rim_ref, *outs
):
    rows = q_ref.shape[0]
    chunks = rows // CHUNK
    per = heads // groups
    keep = iota((HEAD, HEAD), 0) <= iota((HEAD, HEAD), 1)
    rim_ref[:, : wk_ref.shape[1]] = wk_ref[rows - WINDOW :]
    rim_ref[:, wk_ref.shape[1] :] = wv_ref[rows - WINDOW :]
    for head in range(heads):
        g, h = divmod(head, per)
        kk_ref, kt_ref, qt_ref, vt_ref, kst_ref, vst_ref, coef_ref, rate_ref, causal_ref = outs[9 * g : 9 * g + 9]
        cols = head_cols(head)
        raw = k_ref[:, cols]
        keys = raw.astype(F32)
        scale = rate(keys)
        square = jnp.broadcast_to(scale * scale, keys.shape)
        rate_ref[h] = jnp.broadcast_to(scale, keys.shape)
        keys_t = keys.T.astype(BF16)
        once = jnp.concatenate(split(keys * scale), 1)
        twice = jnp.concatenate(split(keys * square), 1)
        vals_t = v_ref[:, cols].astype(F32).T.astype(BF16)
        vt_ref[h] = vals_t
        qt_ref[h] = unit(q_ref[:, cols]).T
        key_sum = val_sum = None
        for c in range(chunks):
            span = slice(c * CHUNK, (c + 1) * CHUNK)
            if c:
                kst_ref[h, c - 1] = key_sum
                vst_ref[h, c - 1] = val_sum
            kk_ref[h, c] = jnp.concatenate([raw[span], raw[span]], 1)
            for r in range(CHUNK // HEAD):
                at = slice(c * CHUNK + r * HEAD, c * CHUNK + (r + 1) * HEAD)
                kt_ref[h, c, :, 2 * r * HEAD : (2 * r + 2) * HEAD] = jnp.concatenate([keys_t[:, at]] * 2, 1)
                across = jnp.where(keep, square[at], 0.0)
                causal_ref[h, c, r] = across
                if r == 0:
                    causal_ref[h, c, 2] = square[at]
            mv = dot(vals_t[:, span], once[span])
            mv = mv[:, :HEAD] + mv[:, HEAD:]
            val_sum = mv if c == 0 else val_sum + mv
            if c + 1 < chunks:
                mk = dot(keys_t[:, span], twice[span])
                mk = mk[:, :HEAD] + mk[:, HEAD:]
                key_sum = mk if c == 0 else key_sum + mk
        total_ref[head] = val_sum
        ridge = ridge_ref[head]
        places = (iota((1, rows), 1) + (base_ref[0] + 1)).astype(F32)
        upper = ridge + places
        centre = (upper + ridge) * 0.5
        radius = (upper - ridge) * 0.5
        step = 1.0 / centre
        weight = jnp.zeros_like(step)
        for i in range(ITERS):
            if i:
                scaled = radius * step
                weight = scaled * scaled * (0.5 if i == 1 else 0.25)
                step = 1.0 / (centre - weight / step)
            coef_ref[h, i : i + 1] = step
            coef_ref[h, ITERS + i : ITERS + i + 1] = weight


def gathered(flags_ref, part_refs, h):
    total = None
    for i, ref in enumerate(part_refs):
        part = jnp.where(flags_ref[i] > 0, ref[h], 0.0)
        total = part if total is None else total + part
    return total


def stack_state(state):
    high, low = split(state)
    return jnp.concatenate(
        [jnp.concatenate([high, high], 1), jnp.concatenate([low, low], 1)], 0
    )


def cheb_scratch(per, chunks):
    return (
        pltpu.VMEM((per, chunks, 2 * HEAD, 2 * HEAD), BF16),
        pltpu.VMEM((per, HEAD, chunks * CHUNK), F32),
        pltpu.VMEM((per, HEAD, chunks * CHUNK), F32),
        pltpu.VMEM((per, chunks, 2 * HEAD, CHUNK), BF16),
        pltpu.VMEM((per, chunks, CHUNK, CHUNK + HEAD), BF16),
    )


def chebyshev_kernel(heads, parts, first, flags_ref, ridge_ref, *refs):
    part_refs, refs = refs[:parts], refs[parts:]
    qt_ref, kk_ref, kt_ref, kst_ref, coef_ref, causal_ref, solved_ref, state, res, direction, rights, inners = refs
    chunks = kk_ref.shape[1]
    for h in range(heads):
        prior = unpack(gathered(flags_ref, part_refs, first + h))
        for c in range(chunks):
            state[h, c] = stack_state(prior if c == 0 else prior + kst_ref[h, c - 1])
        res[h] = qt_ref[h]
        direction[h] = jnp.zeros_like(direction[h])
        solved_ref[h] = jnp.zeros_like(solved_ref[h])
    chains = [(h, c) for h in range(heads) for c in range(chunks)]

    def span_of(c):
        return slice(c * CHUNK, (c + 1) * CHUNK)

    def advance(i, h, c):
        span = span_of(c)
        step = coef_ref[h, pl.ds(i, 1), span]
        weight = coef_ref[h, pl.ds(ITERS + i, 1), span]
        way = res[h, :, span] + weight * direction[h, :, span]
        solved_ref[h, :, span] = solved_ref[h, :, span] + step * way
        return way

    def stage1(i, h, c):
        way = advance(i, h, c)
        direction[h, :, span_of(c)] = way
        high, low = split(way)
        rights[h, c, :HEAD] = high
        rights[h, c, HEAD:] = low

    def stage2(i, h, c):
        inner = dot(kk_ref[h, c], rights[h, c])
        for r, cc, k in ((0, 0, 0), (0, 1, 2), (1, 1, 1)):
            tile = inner[r * HEAD : (r + 1) * HEAD, cc * HEAD : (cc + 1) * HEAD]
            high, low = split(tile * causal_ref[h, c, k])
            lanes = slice((r + cc) * HEAD, (r + cc + 1) * HEAD)
            inners[h, c, :HEAD, lanes] = high
            inners[h, c, HEAD:, lanes] = low

    def stage3(i, h, c):
        image = dot(state[h, c], rights[h, c])
        image = image[:HEAD] + image[HEAD:] + dot(kt_ref[h, c, :, :CHUNK], inners[h, c, :, :CHUNK])
        late = dot(kt_ref[h, c, :, CHUNK:], inners[h, c, :, CHUNK:])
        step = coef_ref[h, pl.ds(i, 1), span_of(c)]
        for k in range(CHUNK // HEAD):
            lanes = slice(k * HEAD, (k + 1) * HEAD)
            span = slice(c * CHUNK + k * HEAD, c * CHUNK + (k + 1) * HEAD)
            part = image[:, lanes] + late if k else image[:, lanes]
            res[h, :, span] = res[h, :, span] - step[:, lanes] * (part + ridge_ref[first + h] * direction[h, :, span])

    def body(i, carry):
        for ch in chains:
            stage1(i, *ch)
        for ch in chains:
            stage2(i, *ch)
        for ch in chains:
            stage3(i, *ch)
        return carry

    lax.fori_loop(0, ITERS - 1, body, 0)
    for h, c in chains:
        advance(ITERS - 1, h, c)


def attend_kernel(heads, parts, first, flags_ref, base_ref, *refs):
    part_refs, refs = refs[:parts], refs[parts:]
    solved_ref, kk_ref, rate_ref, vt_ref, vst_ref, gain_ref, rim_ref, ko_ref, vo_ref, out_ref, kk, vv = refs
    chunks = kk_ref.shape[1]
    rows = ko_ref.shape[0]
    width = ko_ref.shape[1]
    kk[:WINDOW] = rim_ref[:, :width]
    kk[WINDOW:] = ko_ref[...]
    vv[:, :WINDOW] = rim_ref[:, width:].astype(F32).T.astype(BF16)
    vv[:, WINDOW:] = vo_ref[...].astype(F32).T.astype(BF16)
    keep = iota((CHUNK, CHUNK), 0) <= iota((CHUNK, CHUNK), 1)
    bias = jnp.where(base_ref[0] > 0, 0.0, FAR).astype(F32)
    key_at, query_at = iota((HEAD, HEAD), 0), iota((HEAD, HEAD), 1)
    tiles = WINDOW // HEAD
    scale = 1.0 / math.sqrt(HEAD)
    for h in range(heads):
        prior = gathered(flags_ref, part_refs, first + h)
        gain = jnp.broadcast_to(gain_ref[:, head_cols(first + h)], (HEAD, HEAD)).T
        for c in range(chunks):
            span = slice(c * CHUNK, (c + 1) * CHUNK)
            right = jnp.concatenate(split(solved_ref[h, :, span]), 0)
            inner = dot(kk_ref[h, c], right)
            by = rate_ref[h, span]
            high, low = split(jnp.where(keep, inner * jnp.concatenate([by, by], 1), 0.0))
            mixed = dot(stack_state(prior if c == 0 else prior + vst_ref[h, c - 1]), right)
            vals = vt_ref[h, :, span]
            mixed = mixed[:HEAD] + mixed[HEAD:] + dot(vals, high) + dot(vals, low)
            rate = lax.rsqrt(jnp.mean(mixed * mixed, axis=0, keepdims=True) + EPS)
            for b in range(CHUNK // HEAD):
                lanes = slice(b * HEAD, (b + 1) * HEAD)
                query = (mixed[:, lanes] * rate[:, lanes] * gain).astype(BF16)
                j = c * (CHUNK // HEAD) + b
                near = slice(j * HEAD, (j + tiles + 1) * HEAD)
                scores = dot(kk[near], query)
                pieces = []
                for t in range(tiles + 1):
                    piece = scores[t * HEAD : (t + 1) * HEAD]
                    if t == 0:
                        piece = jnp.where(key_at > query_at, piece, FAR)
                    if t == tiles:
                        piece = jnp.where(key_at <= query_at, piece, FAR)
                    if j + t < tiles:
                        piece = piece + bias
                    pieces.append(piece)
                scores = jnp.concatenate(pieces, 0)
                peak = jnp.max(scores, axis=0, keepdims=True)
                grown = jnp.exp((scores - peak) * scale)
                share = 1.0 / jnp.sum(grown, axis=0, keepdims=True)
                weights = (grown * share).astype(BF16)
                mixed_vals = dot(vv[:, near], weights)
                out_ref[j * HEAD : (j + 1) * HEAD, head_cols(h)] = mixed_vals.T.astype(BF16)


def project_kernel(groups, count, *refs):
    out_ref = refs[-1]
    total = None
    for g in range(groups):
        for i in range(count):
            left = refs[g * count + i]
            width = left.shape[1]
            part = dot(left[...], refs[groups * count + i][g * width : (g + 1) * width])
            total = part if total is None else total + part
    out_ref[...] = total.astype(BF16)


SMEM = pl.BlockSpec(memory_space=pltpu.SMEM)
VMEM = pl.BlockSpec(memory_space=pltpu.VMEM)


def call(kernel, outs, args, scalars=0, scratch=(), flops=0, nbytes=0):
    return pl.pallas_call(
        kernel,
        out_shape=outs,
        in_specs=[SMEM] * scalars + [VMEM] * (len(args) - scalars),
        out_specs=jax.tree.map(lambda _: VMEM, outs),
        scratch_shapes=list(scratch),
        compiler_params=pltpu.CompilerParams(vmem_limit_bytes=40 * 1024 * 1024),
        cost_estimate=pl.CostEstimate(flops=flops, bytes_accessed=nbytes, transcendentals=0),
    )(*args)


def rounds_of(count):
    stride, rounds = 1, []
    while stride < count:
        left = count // stride
        radix = 4 if left % 4 == 0 else 2 if left % 2 == 0 else left
        rounds.append((stride, radix))
        stride *= radix
    return rounds


def partner(i, stride, radix, k):
    digit = (i // stride) % radix
    other = digit ^ k if radix in (2, 4) else (digit + k) % radix
    return i + (other - digit) * stride


def swap(x, axis, stride, radix, k):
    n = lax.axis_size(axis)
    return lax.ppermute(x, axis, [(i, partner(i, stride, radix, k)) for i in range(n)])


def source_digit(mine, stride, radix, k):
    digit = (mine // stride) % radix
    return digit ^ k if radix in (2, 4) else (digit - k) % radix


def before(value, axis, at):
    rounds = rounds_of(lax.axis_size(axis))
    stride, radix = rounds[at]
    got = [swap(value, axis, stride, radix, k) for k in range(1, radix)]
    return got, functools.reduce(jnp.add, got, value) if at + 1 < len(rounds) else None


def before_flags(axis):
    mine = lax.axis_index(axis)
    flags = []
    for stride, radix in rounds_of(lax.axis_size(axis)):
        digit = (mine // stride) % radix
        flags += [source_digit(mine, stride, radix, k) < digit for k in range(1, radix)]
    return jnp.stack(flags).astype(jnp.int32)


def shards(
    mixer_queries, mixer_keys, mixer_values, window_keys, window_values, out_gain, ridge, out_weight
):
    rows = mixer_queries.shape[0]
    heads = ridge.shape[0]
    chunks = rows // CHUNK
    seq, head = lax.axis_size("seq"), lax.axis_size("head")
    base = (lax.axis_index("seq") * rows).astype(jnp.int32).reshape(1)
    flags = before_flags("seq")
    per = heads // GROUPS
    shape = jax.ShapeDtypeStruct

    key_total = call(
        functools.partial(moments_kernel, heads), shape((heads, PACKED, HEAD), F32), (mixer_keys,)
    )
    width = window_keys.shape[1]
    val_total, rim, *prepared = call(
        functools.partial(prepare_kernel, heads, GROUPS),
        (
            shape((heads, HEAD, HEAD), F32),
            shape((WINDOW, 2 * width), BF16),
            *GROUPS
            * (
                shape((per, chunks, CHUNK, 2 * HEAD), BF16),
                shape((per, chunks, HEAD, 2 * CHUNK), BF16),
                shape((per, HEAD, rows), F32),
                shape((per, HEAD, rows), BF16),
                shape((per, chunks - 1, HEAD, HEAD), F32),
                shape((per, chunks - 1, HEAD, HEAD), F32),
                shape((per, 2 * ITERS, rows), F32),
                shape((per, rows, HEAD), F32),
                shape((per, chunks, 3, HEAD, HEAD), F32),
            ),
        ),
        (base, ridge, mixer_queries, mixer_keys, mixer_values, window_keys, window_values),
        scalars=2,
    )
    key_parts, val_parts = [], []
    for at in range(len(rounds_of(seq))):
        got, following = before(key_total, "seq", at)
        key_parts += got
        if following is not None:
            key_total = following
            if at == 0:
                key_total, val_total, rim, out_weight = lax.optimization_barrier(
                    (key_total, val_total, rim, out_weight)
                )
    for at in range(len(rounds_of(seq))):
        got, following = before(val_total, "seq", at)
        val_parts += got
        if following is not None:
            val_total = following
            if at == 0:
                val_total, key_parts = lax.optimization_barrier((val_total, key_parts))
    rim = lax.ppermute(rim, "seq", [(i, (i + 1) % seq) for i in range(seq)])

    mine = lax.axis_index("head")
    cols = out_weight.shape[1] // head
    rights = []
    for k in range(head):
        piece = lax.dynamic_slice_in_dim(out_weight, partner(mine, 1, head, k) * cols, cols, 1)
        rights.append(piece if k == 0 else swap(piece, "head", 1, head, k))

    lefts = []
    for g in range(GROUPS):
        kk, kt, qt, vt, kst, vst, coef, rates, causal = prepared[9 * g : 9 * g + 9]
        solved = call(
            functools.partial(chebyshev_kernel, per, len(key_parts), g * per),
            shape((per, HEAD, rows), F32),
            (flags, ridge, *key_parts, qt, kk, kt, kst, coef, causal),
            scalars=2,
            scratch=cheb_scratch(per, chunks),
            flops=10**10,
            nbytes=3 * 10**7,
        )
        attended = call(
            functools.partial(attend_kernel, per, len(val_parts), g * per),
            shape((rows, per * HEAD), BF16),
            (
                flags, base, *val_parts, solved, kk, rates, vt, vst,
                out_gain.reshape(1, -1), rim, window_keys, window_values,
            ),
            scalars=2,
            scratch=(pltpu.VMEM((WINDOW + rows, width), BF16), pltpu.VMEM((width, WINDOW + rows), BF16)),
            flops=4 * 10**9,
            nbytes=15 * 10**6,
        )
        if head == 4:
            far = swap(attended, "head", 1, 4, 2)
            lefts += [attended, swap(attended, "head", 1, 4, 1), far, swap(far, "head", 1, 4, 1)]
        else:
            lefts += [attended] + [swap(attended, "head", 1, head, k) for k in range(1, head)]
    return call(
        functools.partial(project_kernel, GROUPS, head),
        shape((rows, cols), BF16),
        (*lefts, *rights),
    )


def solution(mesh):
    return jax.shard_map(
        shards,
        mesh=mesh,
        in_specs=(
            P("seq", "head"),
            P("seq", "head"),
            P("seq", "head"),
            P("seq", "head"),
            P("seq", "head"),
            P("head"),
            P("head"),
            P("head", None),
        ),
        out_specs=P("seq", "head"),
        check_vma=False,
    )
```

time: 100 us -> 74.3 us (0.74)
  local copies, waits for them, and re-layouts: 21.6 us -> 6.89 us
  Pallas kernels: 35.8 us -> 27.3 us
  other arithmetic: 2.99 us -> 0.19 us
    slice x21 -> x0, local copies, waits for them, and re-layouts: 10.5 us -> none  [the longest x8 4.91 us: shards(): p[part]]
    pallas_call x7, Pallas kernels: 35.8 us -> 27.3 us  [call(): pl.pallas_call(kernel, out_shape=outs, in_specs=[SMEM] * scalars + [VMEM]...]
    unnamed x54 -> x24, local copies, waits for them, and re-layouts: 9.63 us -> 6.65 us
    add x2, other arithmetic: 2.18 us -> 0.11 us  [before(): functools.reduce(jnp.add, got, value)]
    ppermute x17, starting transfers between devices: 19.7 us -> 21.2 us  [swap(): lax.ppermute(x, axis, [(i, partner(i, stride, radix, k)) for i in range(n)])]
    dynamic_slice x1, local copies, waits for them, and re-layouts: 1.47 us -> 0.24 us  [shards(): lax.dynamic_slice_in_dim(out_weight, partner(mine, 1, head, k) * cols, co...]
  transfers between devices with their start and end apart: 18 -> 18, of which waited for: 4 -> 6; matrix products, arithmetic and copies ran while one was open for 15% -> 1% of each run, Pallas kernels for 33% -> 33%
where the time goes in v2:
time: 74.3 us; the launch traced here: 73.9 us
  Pallas kernels  27.3 us (37%)
  starting transfers between devices  22.7 us (31%)
  waiting for transfers between devices  16.6 us (22%)
  local copies, waits for them, and re-layouts  6.89 us (9%)
    pallas_call x7, Pallas kernels, call(): pl.pallas_call(kernel, out_shape=outs, in_specs=[SMEM] * scalars + [VMEM]...  27.3 us
    ppermute x17, starting transfers between devices, swap(): lax.ppermute(x, axis, [(i, partner(i, stride, radix, k)) for i in range(n)])  21.2 us
    ppermute x17, waiting for transfers between devices, swap(): lax.ppermute(x, axis, [(i, partner(i, stride, radix, k)) for i in range(n)])  16.6 us
    unnamed x24, local copies, waits for them, and re-layouts  6.65 us
    ppermute x1, starting transfers between devices, shards(): rim = lax.ppermute(rim, 'seq', [(i, (i + 1) % seq) for i in range(seq)])  1.52 us
  transfers between devices with their start and end apart: 18, of which 6 were waited for; matrix products, arithmetic and copies ran while one was open for 1% of the time, Pallas kernels for 33%

profile of v2, /device:TPU:0, one launch (start us, length us, event | category | flops | bytes accessed | tf_op | source)
XLA Modules:
  0.0 73.9 jit_solution(1711400971388488718)
XLA Ops:
  0.0 1.0 %copy-done = bf16[512,512]{1,0:T(8,128)(2,1)S(1)} copy-done((bf16[512,512]{1,0:T(8,128)(2,1)S(1)}, bf16[512,512]{1,0:T(8,128)(2,1)}, u32[]{:S(2)}) %copy-start) | copy-done | bytes 524312
  1.0 1.0 %shard_map.82 = f32[4,72,128]{2,1,0:T(8,128)S(1)} custom-call(bf16[512,512]{1,0:T(8,128)(2,1)S(1)} %copy-done), custom_call_target="tpu_custom_call" | custom-call | tf_op jit(solution)/shard_map/pallas_call | solution.py:299
  2.1 4.0 %collective-permute-start.2 = (f32[4,72,128]{2,1,0:T(8,128)S(1)}, f32[4,72,128]{2,1,0:T(8,128)S(1)}, u32[]{:S(2)}, u32[]{:S(2)}) collective-permute-start(f32[4,72,128]{2,1,0:T(8,128)S(1)} %shard_map.82), channel_id=1, source_target_pairs={{0,12},{4,8},{8,4},{12,0},{16,28},{20,24},{24,20},{28,16},{1,13},{... | collective-permute-start | bytes 442376 | tf_op jit(solution)/shard_map/ppermute | solution.py:328
  6.8 1.0 %copy-done.1 = bf16[512,512]{1,0:T(8,128)(2,1)S(1)} copy-done((bf16[512,512]{1,0:T(8,128)(2,1)S(1)}, bf16[512,512]{1,0:T(8,128)(2,1)}, u32[]{:S(2)}) %copy-start.1) | copy-done | bytes 524312
  7.8 1.0 %copy-done.2 = bf16[512,512]{1,0:T(8,128)(2,1)S(1)} copy-done((bf16[512,512]{1,0:T(8,128)(2,1)S(1)}, bf16[512,512]{1,0:T(8,128)(2,1)}, u32[]{:S(2)}) %copy-start.2) | copy-done | bytes 524312
  8.8 1.0 %copy-done.3 = bf16[512,512]{1,0:T(8,128)(2,1)S(1)} copy-done((bf16[512,512]{1,0:T(8,128)(2,1)S(1)}, bf16[512,512]{1,0:T(8,128)(2,1)}, u32[]{:S(2)}) %copy-start.3) | copy-done | bytes 524312
  9.9 0.9 %copy-done.4 = bf16[512,128]{1,0:T(8,128)(2,1)S(1)} copy-done((bf16[512,128]{1,0:T(8,128)(2,1)S(1)}, bf16[512,128]{1,0:T(8,128)(2,1)}, u32[]{:S(2)}) %copy-start.4) | copy-done | bytes 131096
  12.4 2.1 %shard_map.83 = (f32[4,128,128]{2,1,0:T(8,128)S(1)}, bf16[512,256]{1,0:T(8,128)(2,1)S(1)}, bf16[2,2,256,256]{3,2,1,0:T(8,128)(2,1)S(1)}, bf16[2,2,128,512]{3,2,1...) custom-call(s32[1]{0:T(128)} %bitcast.4.base_ref, ...), custom_call_target="tpu_custom_call" | custom-call | tf_op jit(solution)/shard_map/pallas_call | solution.py:299
  14.5 1.9 %collective-permute-start.3 = (f32[4,128,128]{2,1,0:T(8,128)S(1)}, f32[4,128,128]{2,1,0:T(8,128)S(1)}, u32[]{:S(2)}, u32[]{:S(2)}) collective-permute-start(f32[4,128,128]{2,1,0:T(8,128)S(1)} %get-tuple-element.36), channel_id=1, source_target_pairs={{0,4},{4,0},{8,12},{12,8},{16,20},{20,16},{24,28},{28,24},{1,5},{5... | collective-permute-start | bytes 786440 | tf_op jit(solution)/shard_map/ppermute | solution.py:328
  16.4 1.6 %collective-permute-start.4 = (f32[4,128,128]{2,1,0:T(8,128)S(1)}, f32[4,128,128]{2,1,0:T(8,128)S(1)}, u32[]{:S(2)}, u32[]{:S(2)}) collective-permute-start(f32[4,128,128]{2,1,0:T(8,128)S(1)} %get-tuple-element.36), channel_id=1, source_target_pairs={{0,8},{4,12},{8,0},{12,4},{16,24},{20,28},{24,16},{28,20},{1,9},{5... | collective-permute-start | bytes 786440 | tf_op jit(solution)/shard_map/ppermute | solution.py:328
  18.2 2.9 %collective-permute-start.6 = (f32[4,72,128]{2,1,0:T(8,128)S(1)}, f32[4,72,128]{2,1,0:T(8,128)S(1)}, u32[]{:S(2)}, u32[]{:S(2)}) collective-permute-start(f32[4,72,128]{2,1,0:T(8,128)S(1)} %add_add_fusion.1), channel_id=1, source_target_pairs={{0,16},{4,20},{8,24},{12,28},{16,0},{20,4},{24,8},{28,12},{1,17},{... | collective-permute-start | bytes 442376 | tf_op jit(solution)/shard_map/ppermute | solution.py:328
  21.1 1.5 %collective-permute-start.8 = (bf16[512,256]{1,0:T(8,128)(2,1)S(1)}, bf16[512,256]{1,0:T(8,128)(2,1)S(1)}, u32[]{:S(2)}, u32[]{:S(2)}) collective-permute-start(bf16[512,256]{1,0:T(8,128)(2,1)S(1)} %get-tuple-element.52), channel_id=1, source_target_pairs={{0,4},{4,8},{8,12},{12,16},{16,20},{20,24},{24,28},{28,0},{1,5},{5... | collective-permute-start | bytes 786440 | tf_op jit(solution)/shard_map/ppermute | solution.py:406
  22.9 5.9 %collective-permute-done.4.refs_1_ = f32[4,128,128]{2,1,0:T(8,128)S(1)} collective-permute-done((f32[4,128,128]{2,1,0:T(8,128)S(1)}, f32[4,128,128]{2,1,0:T(8,128)S(1)}, u32[]{:S(2)}, u32[]{:S(2)}) %collective-permute-start.4) | collective-permute-done | bytes 262176 | tf_op jit(solution)/shard_map/ppermute | solution.py:328
  28.8 1.5 %collective-permute-start.16 = (bf16[512,512]{1,0:T(8,128)(2,1)S(1)}, bf16[512,512]{1,0:T(8,128)(2,1)S(1)}, u32[]{:S(2)}, u32[]{:S(2)}) collective-permute-start(bf16[512,512]{1,0:T(8,128)(2,1)S(1)} %get-tuple-element.64), channel_id=1, source_target_pairs={{0,2},{1,3},{2,0},{3,1},{4,6},{5,7},{6,4},{7,5},{8,10},{9,11},{10,... | collective-permute-start | bytes 1572872 | tf_op jit(solution)/shard_map/ppermute | solution.py:328
  30.3 1.7 %collective-permute-done.5.refs_2_ = f32[4,128,128]{2,1,0:T(8,128)S(1)} collective-permute-done((f32[4,128,128]{2,1,0:T(8,128)S(1)}, f32[4,128,128]{2,1,0:T(8,128)S(1)}, u32[]{:S(2)}, u32[]{:S(2)}) %collective-permute-start.5) | collective-permute-done | bytes 262176 | tf_op jit(solution)/shard_map/ppermute | solution.py:328
  32.1 5.8 %collective-permute-start.7 = (f32[4,128,128]{2,1,0:T(8,128)S(1)}, f32[4,128,128]{2,1,0:T(8,128)S(1)}, u32[]{:S(2)}, u32[]{:S(2)}) collective-permute-start(f32[4,128,128]{2,1,0:T(8,128)S(1)} %add_add_fusion), channel_id=1, source_target_pairs={{0,16},{4,20},{8,24},{12,28},{16,0},{20,4},{24,8},{28,12},{1,17},{... | collective-permute-start | bytes 786440 | tf_op jit(solution)/shard_map/ppermute | solution.py:328
  38.0 5.7 %shard_map.84.refs_4_ = f32[2,128,512]{2,1,0:T(8,128)S(1)} custom-call(s32[4]{0:T(128)S(1)} %add_convert_fusion.flags_ref, f32[4]{0:T(128)S(1)} %copy-done.9, f32[4,72,128]{2,1,0:T(8,128)S(1)} %collective-permute-done.refs_0_, f32[4,72,128]{2,1,0:T(8,128)S(1)} %collective-permute-done.1.refs_1_, f32[4,72,128]{2,1,0:T(8,128)S(1)} %collective-permute-done.2.refs_2_, ...), custom_call_target="tpu_custom_call" | custom-call | flops 10000000000 | bytes 30000000 | tf_op jit(solution)/shard_map/pallas_call | solution.py:299
  43.8 5.8 %shard_map.86.refs_4_ = f32[2,128,512]{2,1,0:T(8,128)S(1)} custom-call(s32[4]{0:T(128)S(1)} %add_convert_fusion.flags_ref, f32[4]{0:T(128)S(1)} %copy-done.9, f32[4,72,128]{2,1,0:T(8,128)S(1)} %collective-permute-done.refs_0_, f32[4,72,128]{2,1,0:T(8,128)S(1)} %collective-permute-done.1.refs_1_, f32[4,72,128]{2,1,0:T(8,128)S(1)} %collective-permute-done.2.refs_2_, ...), custom_call_target="tpu_custom_call" | custom-call | flops 10000000000 | bytes 30000000 | tf_op jit(solution)/shard_map/pallas_call | solution.py:299
  50.4 5.3 %shard_map.85.refs_0_ = bf16[512,256]{1,0:T(8,128)(2,1)S(1)} custom-call(s32[4]{0:T(128)S(1)} %add_convert_fusion.flags_ref, s32[1]{0:T(128)} %bitcast.4.base_ref, f32[4,128,128]{2,1,0:T(8,128)S(1)} %collective-permute-done.3.refs_0_, f32[4,128,128]{2,1,0:T(8,128)S(1)} %collective-permute-done.4.refs_1_, f32[4,128,128]{2,1,0:T(8,128)S(1)} %collective-permute-done.5.refs_2_, ...), custom_call_target="tpu_custom_call" | custom-call | flops 4000000000 | bytes 15000000 | tf_op jit(solution)/shard_map/pallas_call | solution.py:299
  55.7 1.6 %collective-permute-start.10 = (bf16[512,256]{1,0:T(8,128)(2,1)S(1)}, bf16[512,256]{1,0:T(8,128)(2,1)S(1)}, u32[]{:S(2)}, u32[]{:S(2)}) collective-permute-start(bf16[512,256]{1,0:T(8,128)(2,1)S(1)} %shard_map.85.refs_0_), channel_id=1, source_target_pairs={{0,2},{1,3},{2,0},{3,1},{4,6},{5,7},{6,4},{7,5},{8,10},{9,11},{10,... | collective-permute-start | bytes 786440 | tf_op jit(solution)/shard_map/ppermute | solution.py:328
  57.2 5.3 %shard_map.87.refs_4_ = bf16[512,256]{1,0:T(8,128)(2,1)S(1)} custom-call(s32[4]{0:T(128)S(1)} %add_convert_fusion.flags_ref, s32[1]{0:T(128)} %bitcast.4.base_ref, f32[4,128,128]{2,1,0:T(8,128)S(1)} %collective-permute-done.3.refs_0_, f32[4,128,128]{2,1,0:T(8,128)S(1)} %collective-permute-done.4.refs_1_, f32[4,128,128]{2,1,0:T(8,128)S(1)} %collective-permute-done.5.refs_2_, ...), custom_call_target="tpu_custom_call" | custom-call | flops 4000000000 | bytes 15000000 | tf_op jit(solution)/shard_map/pallas_call | solution.py:299
  63.8 6.6 %collective-permute-done.13.refs_6_ = bf16[512,256]{1,0:T(8,128)(2,1)S(1)} collective-permute-done((bf16[512,256]{1,0:T(8,128)(2,1)S(1)}, bf16[512,256]{1,0:T(8,128)(2,1)S(1)}, u32[]{:S(2)}, u32[]{:S(2)}) %collective-permute-start.13) | collective-permute-done | bytes 262176 | tf_op jit(solution)/shard_map/ppermute | solution.py:328
  70.4 1.5 %collective-permute-done.14.refs_7_ = bf16[512,256]{1,0:T(8,128)(2,1)S(1)} collective-permute-done((bf16[512,256]{1,0:T(8,128)(2,1)S(1)}, bf16[512,256]{1,0:T(8,128)(2,1)S(1)}, u32[]{:S(2)}, u32[]{:S(2)}) %collective-permute-start.14) | collective-permute-done | bytes 262176 | tf_op jit(solution)/shard_map/ppermute | solution.py:328
  71.9 2.0 %shard_map.88 = bf16[512,512]{1,0:T(8,128)(2,1)} custom-call(bf16[512,256]{1,0:T(8,128)(2,1)S(1)} %shard_map.85.refs_0_, bf16[512,256]{1,0:T(8,128)(2,1)S(1)} %collective-permute-done.9.refs_1_, bf16[512,256]{1,0:T(8,128)(2,1)S(1)} %collective-permute-done.10.refs_2_, bf16[512,256]{1,0:T(8,128)(2,1)S(1)} %collective-permute-done.11.refs_3_, ...), custom_call_target="tpu_custom_call" | custom-call | tf_op jit(solution)/shard_map/pallas_call | solution.py:299
  (47 shorter events, 4.8 us)
Async XLA Ops:
  0.0 1.0 %copy-start = (bf16[512,512]{1,0:T(8,128)(2,1)S(1)}, bf16[512,512]{1,0:T(8,128)(2,1)}, u32[]{:S(2)}) copy-start(bf16[512,512]{1,0:T(8,128)(2,1)} %k_ref.1) | copy-start | bytes 1572868
  2.1 12.4 %collective-permute-start.2 = (f32[4,72,128]{2,1,0:T(8,128)S(1)}, f32[4,72,128]{2,1,0:T(8,128)S(1)}, u32[]{:S(2)}, u32[]{:S(2)}) collective-permute-start(f32[4,72,128]{2,1,0:T(8,128)S(1)} %shard_map.82), channel_id=1, source_target_pairs={{0,12},{4,8},{8,4},{12,0},{16,28},{20,24},{24,20},{28,16},{1,13},{... | collective-permute-start | bytes 442376 | tf_op jit(solution)/shard_map/ppermute | solution.py:328
  6.1 8.4 %collective-permute-start.1 = (f32[4,72,128]{2,1,0:T(8,128)S(1)}, f32[4,72,128]{2,1,0:T(8,128)S(1)}, u32[]{:S(2)}, u32[]{:S(2)}) collective-permute-start(f32[4,72,128]{2,1,0:T(8,128)S(1)} %shard_map.82), channel_id=1, source_target_pairs={{0,8},{4,12},{8,0},{12,4},{16,24},{20,28},{24,16},{28,20},{1,9},{5... | collective-permute-start | bytes 442376 | tf_op jit(solution)/shard_map/ppermute | solution.py:328
  6.6 7.9 %collective-permute-start = (f32[4,72,128]{2,1,0:T(8,128)S(1)}, f32[4,72,128]{2,1,0:T(8,128)S(1)}, u32[]{:S(2)}, u32[]{:S(2)}) collective-permute-start(f32[4,72,128]{2,1,0:T(8,128)S(1)} %shard_map.82), channel_id=1, source_target_pairs={{0,4},{4,0},{8,12},{12,8},{16,20},{20,16},{24,28},{28,24},{1,5},{5... | collective-permute-start | bytes 442376 | tf_op jit(solution)/shard_map/ppermute | solution.py:328
  12.4 10.3 %copy-start.11 = (bf16[512,2048]{1,0:T(8,128)(2,1)S(1)}, bf16[512,2048]{1,0:T(8,128)(2,1)}, u32[]{:S(2)}) copy-start(bf16[512,2048]{1,0:T(8,128)(2,1)} %param.15) | copy-start | bytes 6291460
  14.5 8.3 %collective-permute-start.3 = (f32[4,128,128]{2,1,0:T(8,128)S(1)}, f32[4,128,128]{2,1,0:T(8,128)S(1)}, u32[]{:S(2)}, u32[]{:S(2)}) collective-permute-start(f32[4,128,128]{2,1,0:T(8,128)S(1)} %get-tuple-element.36), channel_id=1, source_target_pairs={{0,4},{4,0},{8,12},{12,8},{16,20},{20,16},{24,28},{28,24},{1,5},{5... | collective-permute-start | bytes 786440 | tf_op jit(solution)/shard_map/ppermute | solution.py:328
  16.4 12.4 %collective-permute-start.4 = (f32[4,128,128]{2,1,0:T(8,128)S(1)}, f32[4,128,128]{2,1,0:T(8,128)S(1)}, u32[]{:S(2)}, u32[]{:S(2)}) collective-permute-start(f32[4,128,128]{2,1,0:T(8,128)S(1)} %get-tuple-element.36), channel_id=1, source_target_pairs={{0,8},{4,12},{8,0},{12,4},{16,24},{20,28},{24,16},{28,20},{1,9},{5... | collective-permute-start | bytes 786440 | tf_op jit(solution)/shard_map/ppermute | solution.py:328
  18.0 14.0 %collective-permute-start.5 = (f32[4,128,128]{2,1,0:T(8,128)S(1)}, f32[4,128,128]{2,1,0:T(8,128)S(1)}, u32[]{:S(2)}, u32[]{:S(2)}) collective-permute-start(f32[4,128,128]{2,1,0:T(8,128)S(1)} %get-tuple-element.36), channel_id=1, source_target_pairs={{0,12},{4,8},{8,4},{12,0},{16,28},{20,24},{24,20},{28,16},{1,13},{... | collective-permute-start | bytes 786440 | tf_op jit(solution)/shard_map/ppermute | solution.py:328
  18.2 19.8 %copy-start.9 = (f32[4]{0:T(128)S(1)}, f32[4]{0:T(128)}, u32[]{:S(2)}) copy-start(f32[4]{0:T(128)} %ridge_ref.5) | copy-start | bytes 52
  18.2 14.0 %collective-permute-start.6 = (f32[4,72,128]{2,1,0:T(8,128)S(1)}, f32[4,72,128]{2,1,0:T(8,128)S(1)}, u32[]{:S(2)}, u32[]{:S(2)}) collective-permute-start(f32[4,72,128]{2,1,0:T(8,128)S(1)} %add_add_fusion.1), channel_id=1, source_target_pairs={{0,16},{4,20},{8,24},{12,28},{16,0},{20,4},{24,8},{28,12},{1,17},{... | collective-permute-start | bytes 442376 | tf_op jit(solution)/shard_map/ppermute | solution.py:328
  21.1 28.5 %collective-permute-start.8 = (bf16[512,256]{1,0:T(8,128)(2,1)S(1)}, bf16[512,256]{1,0:T(8,128)(2,1)S(1)}, u32[]{:S(2)}, u32[]{:S(2)}) collective-permute-start(bf16[512,256]{1,0:T(8,128)(2,1)S(1)} %get-tuple-element.52), channel_id=1, source_target_pairs={{0,4},{4,8},{8,12},{12,16},{16,20},{20,24},{24,28},{28,0},{1,5},{5... | collective-permute-start | bytes 786440 | tf_op jit(solution)/shard_map/ppermute | solution.py:406
  22.9 40.3 %collective-permute-start.15 = (bf16[512,512]{1,0:T(8,128)(2,1)S(1)}, bf16[512,512]{1,0:T(8,128)(2,1)S(1)}, u32[]{:S(2)}, u32[]{:S(2)}) collective-permute-start(bf16[512,512]{1,0:T(8,128)(2,1)S(1)} %get-tuple-element.65), channel_id=1, source_target_pairs={{0,1},{1,0},{2,3},{3,2},{4,5},{5,4},{6,7},{7,6},{8,9},{9,8},{10,11... | collective-permute-start | bytes 1572872 | tf_op jit(solution)/shard_map/ppermute | solution.py:328
  28.8 34.3 %collective-permute-start.16 = (bf16[512,512]{1,0:T(8,128)(2,1)S(1)}, bf16[512,512]{1,0:T(8,128)(2,1)S(1)}, u32[]{:S(2)}, u32[]{:S(2)}) collective-permute-start(bf16[512,512]{1,0:T(8,128)(2,1)S(1)} %get-tuple-element.64), channel_id=1, source_target_pairs={{0,2},{1,3},{2,0},{3,1},{4,6},{5,7},{6,4},{7,5},{8,10},{9,11},{10,... | collective-permute-start | bytes 1572872 | tf_op jit(solution)/shard_map/ppermute | solution.py:328
  32.0 38.3 %collective-permute-start.17 = (bf16[512,512]{1,0:T(8,128)(2,1)S(1)}, bf16[512,512]{1,0:T(8,128)(2,1)S(1)}, u32[]{:S(2)}, u32[]{:S(2)}) collective-permute-start(bf16[512,512]{1,0:T(8,128)(2,1)S(1)} %get-tuple-element.63), channel_id=1, source_target_pairs={{0,3},{1,2},{2,1},{3,0},{4,7},{5,6},{6,5},{7,4},{8,11},{9,10},{10,... | collective-permute-start | bytes 1572872 | tf_op jit(solution)/shard_map/ppermute | solution.py:328
  32.1 18.2 %collective-permute-start.7 = (f32[4,128,128]{2,1,0:T(8,128)S(1)}, f32[4,128,128]{2,1,0:T(8,128)S(1)}, u32[]{:S(2)}, u32[]{:S(2)}) collective-permute-start(f32[4,128,128]{2,1,0:T(8,128)S(1)} %add_add_fusion), channel_id=1, source_target_pairs={{0,16},{4,20},{8,24},{12,28},{16,0},{20,4},{24,8},{28,12},{1,17},{... | collective-permute-start | bytes 786440 | tf_op jit(solution)/shard_map/ppermute | solution.py:328
  43.7 6.6 %copy-start.5 = (bf16[512,128]{1,0:T(8,128)(2,1)S(1)}, bf16[512,128]{1,0:T(8,128)(2,1)}, u32[]{:S(2)}) copy-start(bf16[512,128]{1,0:T(8,128)(2,1)} %refs_11_.3) | copy-start | bytes 393220
  43.7 6.6 %copy-start.7 = (bf16[512,128]{1,0:T(8,128)(2,1)S(1)}, bf16[512,128]{1,0:T(8,128)(2,1)}, u32[]{:S(2)}) copy-start(bf16[512,128]{1,0:T(8,128)(2,1)} %refs_12_.3) | copy-start | bytes 393220
  43.8 6.6 %copy-start.10 = (f32[512]{0:T(512)S(1)}, f32[512]{0:T(512)}, u32[]{:S(2)}) copy-start(f32[512]{0:T(512)} %param.13) | copy-start | bytes 6148
  55.7 8.1 %collective-permute-start.10 = (bf16[512,256]{1,0:T(8,128)(2,1)S(1)}, bf16[512,256]{1,0:T(8,128)(2,1)S(1)}, u32[]{:S(2)}, u32[]{:S(2)}) collective-permute-start(bf16[512,256]{1,0:T(8,128)(2,1)S(1)} %shard_map.85.refs_0_), channel_id=1, source_target_pairs={{0,2},{1,3},{2,0},{3,1},{4,6},{5,7},{6,4},{7,5},{8,10},{9,11},{10,... | collective-permute-start | bytes 786440 | tf_op jit(solution)/shard_map/ppermute | solution.py:328
  62.6 7.8 %collective-permute-start.13 = (bf16[512,256]{1,0:T(8,128)(2,1)S(1)}, bf16[512,256]{1,0:T(8,128)(2,1)S(1)}, u32[]{:S(2)}, u32[]{:S(2)}) collective-permute-start(bf16[512,256]{1,0:T(8,128)(2,1)S(1)} %shard_map.87.refs_4_), channel_id=1, source_target_pairs={{0,2},{1,3},{2,0},{3,1},{4,6},{5,7},{6,4},{7,5},{8,10},{9,11},{10,... | collective-permute-start | bytes 786440 | tf_op jit(solution)/shard_map/ppermute | solution.py:328
  63.2 7.2 %collective-permute-start.9 = (bf16[512,256]{1,0:T(8,128)(2,1)S(1)}, bf16[512,256]{1,0:T(8,128)(2,1)S(1)}, u32[]{:S(2)}, u32[]{:S(2)}) collective-permute-start(bf16[512,256]{1,0:T(8,128)(2,1)S(1)} %shard_map.85.refs_0_), channel_id=1, source_target_pairs={{0,1},{1,0},{2,3},{3,2},{4,5},{5,4},{6,7},{7,6},{8,9},{9,8},{10,11... | collective-permute-start | bytes 786440 | tf_op jit(solution)/shard_map/ppermute | solution.py:328
  63.2 7.2 %collective-permute-start.12 = (bf16[512,256]{1,0:T(8,128)(2,1)S(1)}, bf16[512,256]{1,0:T(8,128)(2,1)S(1)}, u32[]{:S(2)}, u32[]{:S(2)}) collective-permute-start(bf16[512,256]{1,0:T(8,128)(2,1)S(1)} %shard_map.87.refs_4_), channel_id=1, source_target_pairs={{0,1},{1,0},{2,3},{3,2},{4,5},{5,4},{6,7},{7,6},{8,9},{9,8},{10,11... | collective-permute-start | bytes 786440 | tf_op jit(solution)/shard_map/ppermute | solution.py:328
  63.8 6.6 %collective-permute-start.11 = (bf16[512,256]{1,0:T(8,128)(2,1)S(1)}, bf16[512,256]{1,0:T(8,128)(2,1)S(1)}, u32[]{:S(2)}, u32[]{:S(2)}) collective-permute-start(bf16[512,256]{1,0:T(8,128)(2,1)S(1)} %collective-permute-done.10.refs_2_), channel_id=1, source_target_pairs={{0,1},{1,0},{2,3},{3,2},{4,5},{5,4},{6,7},{7,6},{8,9},{9,8},{10,11... | collective-permute-start | bytes 786440 | tf_op jit(solution)/shard_map/ppermute | solution.py:328
  70.4 1.5 %collective-permute-start.14 = (bf16[512,256]{1,0:T(8,128)(2,1)S(1)}, bf16[512,256]{1,0:T(8,128)(2,1)S(1)}, u32[]{:S(2)}, u32[]{:S(2)}) collective-permute-start(bf16[512,256]{1,0:T(8,128)(2,1)S(1)} %collective-permute-done.13.refs_6_), channel_id=1, source_target_pairs={{0,1},{1,0},{2,3},{3,2},{4,5},{5,4},{6,7},{7,6},{8,9},{9,8},{10,11... | collective-permute-start | bytes 786440 | tf_op jit(solution)/shard_map/ppermute | solution.py:328
  (6 other events, 5.6 us)

commit v3 on v2

v3 whole, which is shorter than its diff:
```python
import functools
import math

import jax
import jax.numpy as jnp
from jax import lax
from jax.experimental import pallas as pl
from jax.experimental.pallas import tpu as pltpu
from jax.sharding import PartitionSpec as P

ITERS = 8
WINDOW = 512
EPS = 1e-06
HEAD = 128
HALF = HEAD // 2
CHUNK = 256
PACKED = HALF + 8
BOTH = PACKED + HEAD
GROUPS = 2
FAR = -1e30
F32 = jnp.float32
BF16 = jnp.bfloat16


def dot(a, b):
    return jnp.dot(a, b, preferred_element_type=F32)


def split(x):
    high = x.astype(BF16)
    return high, (x - high.astype(F32)).astype(BF16)


def rate(x):
    return lax.rsqrt(jnp.mean(x * x, axis=-1, keepdims=True) + EPS) * (1.0 / math.sqrt(HEAD))


def unit(x):
    x = x.astype(F32)
    return x * rate(x)


def iota(shape, dim):
    return lax.broadcasted_iota(jnp.int32, shape, dim)


def head_cols(h):
    return slice(h * HEAD, (h + 1) * HEAD)


def pack(m):
    top, low = m[:HALF], pltpu.roll(m[HALF:], HALF, 1)
    row, col = iota((HALF, HEAD), 0), iota((HALF, HEAD), 1)
    body = jnp.where((col >= HALF) | (row > col), top, low)
    diag = jnp.sum(jnp.where(row == col, top, 0.0), axis=0, keepdims=True)
    return body, jnp.broadcast_to(diag, (8, HEAD))


def unpack(p):
    body, diag = p[:HALF], p[HALF : HALF + 1]
    row, col = iota((HALF, HEAD), 0), iota((HALF, HEAD), 1)
    top = jnp.where((col >= HALF) | (row > col), body, 0.0) + jnp.where(row == col, 0.5 * diag, 0.0)
    low = jnp.where((col < HALF) & (row <= col), body, 0.0) * jnp.where(row == col, 0.5, 1.0)
    half = jnp.concatenate([top, pltpu.roll(low, HALF, 1)], 0)
    return half + half.T


def moments_kernel(shares, digit_ref, keys_ref, vals_ref, *outs):
    own = outs[0].shape[0]
    for k in range(shares):
        for j in range(own):
            cols = pl.ds(pl.multiple_of(((digit_ref[0] ^ k) * own + j) * HEAD, HEAD), HEAD)
            keys = keys_ref[:, cols].astype(F32)
            scale = rate(keys)
            once = keys * scale
            pair = dot(keys.T.astype(BF16), jnp.concatenate(split(once * scale), 1))
            body, diag = pack(pair[:, :HEAD] + pair[:, HEAD:])
            outs[k][j, :HALF] = body
            outs[k][j, HALF:PACKED] = diag
            vals_t = vals_ref[:, cols].astype(F32).T.astype(BF16)
            pair = dot(vals_t, jnp.concatenate(split(once), 1))
            outs[k][j, PACKED:] = pair[:, :HEAD] + pair[:, HEAD:]


def prepare(heads, first, base_ref, ridge_ref, q_ref, k_ref, v_ref, *outs):
    rows = q_ref.shape[0]
    chunks = rows // CHUNK
    kk_ref, kt_ref, qt_ref, vt_ref, kst_ref, vst_ref, coef_ref, rate_ref, causal_ref = outs
    keep = iota((HEAD, HEAD), 0) <= iota((HEAD, HEAD), 1)
    for h in range(heads):
        cols = head_cols(first + h)
        raw = k_ref[:, cols]
        keys = raw.astype(F32)
        scale = rate(keys)
        square = jnp.broadcast_to(scale * scale, keys.shape)
        rate_ref[h] = jnp.broadcast_to(scale, keys.shape)
        keys_t = keys.T.astype(BF16)
        once = jnp.concatenate(split(keys * scale), 1)
        twice = jnp.concatenate(split(keys * square), 1)
        vals_t = v_ref[:, cols].astype(F32).T.astype(BF16)
        vt_ref[h] = vals_t
        qt_ref[h] = unit(q_ref[:, cols]).T
        key_sum = val_sum = None
        for c in range(chunks):
            span = slice(c * CHUNK, (c + 1) * CHUNK)
            if c:
                kst_ref[h, c - 1] = key_sum
                vst_ref[h, c - 1] = val_sum
            kk_ref[h, c] = jnp.concatenate([raw[span], raw[span]], 1)
            for r in range(CHUNK // HEAD):
                at = slice(c * CHUNK + r * HEAD, c * CHUNK + (r + 1) * HEAD)
                kt_ref[h, c, :, 2 * r * HEAD : (2 * r + 2) * HEAD] = jnp.concatenate([keys_t[:, at]] * 2, 1)
                across = jnp.where(keep, square[at], 0.0)
                causal_ref[h, c, r] = across
                if r == 0:
                    causal_ref[h, c, 2] = square[at]
            if c + 1 < chunks:
                mv = dot(vals_t[:, span], once[span])
                mv = mv[:, :HEAD] + mv[:, HEAD:]
                val_sum = mv if c == 0 else val_sum + mv
                mk = dot(keys_t[:, span], twice[span])
                mk = mk[:, :HEAD] + mk[:, HEAD:]
                key_sum = mk if c == 0 else key_sum + mk
        ridge = ridge_ref[first + h]
        places = (iota((1, rows), 1) + (base_ref[0] + 1)).astype(F32)
        upper = ridge + places
        centre = (upper + ridge) * 0.5
        radius = (upper - ridge) * 0.5
        step = 1.0 / centre
        weight = jnp.zeros_like(step)
        for i in range(ITERS):
            if i:
                scaled = radius * step
                weight = scaled * scaled * (0.5 if i == 1 else 0.25)
                step = 1.0 / (centre - weight / step)
            coef_ref[h, i : i + 1] = step
            coef_ref[h, ITERS + i : ITERS + i + 1] = weight


def gathered(digit_ref, part_refs, h, rows):
    own = part_refs[0].shape[0]
    total = None
    for k, ref in enumerate(part_refs):
        part = jnp.where((digit_ref[0] ^ k) == h // own, ref[h % own, rows], 0.0)
        total = part if total is None else total + part
    return total


def stack_state(state):
    high, low = split(state)
    return jnp.concatenate(
        [jnp.concatenate([high, high], 1), jnp.concatenate([low, low], 1)], 0
    )


def cheb_scratch(per, chunks):
    return (
        pltpu.VMEM((per, chunks, 2 * HEAD, 2 * HEAD), BF16),
        pltpu.VMEM((per, HEAD, chunks * CHUNK), F32),
        pltpu.VMEM((per, HEAD, chunks * CHUNK), F32),
        pltpu.VMEM((per, chunks, 2 * HEAD, CHUNK), BF16),
        pltpu.VMEM((per, chunks, CHUNK, CHUNK + HEAD), BF16),
    )


def chebyshev(heads, first, digit_ref, ridge_ref, part_refs, *refs):
    kk_ref, kt_ref, kst_ref, coef_ref, causal_ref, solved_ref, state, res, direction, rights, inners = refs
    chunks = kk_ref.shape[1]
    for h in range(heads):
        prior = unpack(gathered(digit_ref, part_refs, first + h, slice(0, PACKED)))
        for c in range(chunks):
            state[h, c] = stack_state(prior if c == 0 else prior + kst_ref[h, c - 1])
        direction[h] = jnp.zeros_like(direction[h])
        solved_ref[h] = jnp.zeros_like(solved_ref[h])
    chains = [(h, c) for h in range(heads) for c in range(chunks)]

    def span_of(c):
        return slice(c * CHUNK, (c + 1) * CHUNK)

    def advance(i, h, c):
        span = span_of(c)
        step = coef_ref[h, pl.ds(i, 1), span]
        weight = coef_ref[h, pl.ds(ITERS + i, 1), span]
        way = res[h, :, span] + weight * direction[h, :, span]
        solved_ref[h, :, span] = solved_ref[h, :, span] + step * way
        return way

    def stage1(i, h, c):
        way = advance(i, h, c)
        direction[h, :, span_of(c)] = way
        high, low = split(way)
        rights[h, c, :HEAD] = high
        rights[h, c, HEAD:] = low

    def stage2(i, h, c):
        inner = dot(kk_ref[h, c], rights[h, c])
        for r, cc, k in ((0, 0, 0), (0, 1, 2), (1, 1, 1)):
            tile = inner[r * HEAD : (r + 1) * HEAD, cc * HEAD : (cc + 1) * HEAD]
            high, low = split(tile * causal_ref[h, c, k])
            lanes = slice((r + cc) * HEAD, (r + cc + 1) * HEAD)
            inners[h, c, :HEAD, lanes] = high
            inners[h, c, HEAD:, lanes] = low

    def stage3(i, h, c):
        image = dot(state[h, c], rights[h, c])
        image = image[:HEAD] + image[HEAD:] + dot(kt_ref[h, c, :, :CHUNK], inners[h, c, :, :CHUNK])
        late = dot(kt_ref[h, c, :, CHUNK:], inners[h, c, :, CHUNK:])
        step = coef_ref[h, pl.ds(i, 1), span_of(c)]
        for k in range(CHUNK // HEAD):
            lanes = slice(k * HEAD, (k + 1) * HEAD)
            span = slice(c * CHUNK + k * HEAD, c * CHUNK + (k + 1) * HEAD)
            part = image[:, lanes] + late if k else image[:, lanes]
            res[h, :, span] = res[h, :, span] - step[:, lanes] * (part + ridge_ref[first + h] * direction[h, :, span])

    def body(i, carry):
        for ch in chains:
            stage1(i, *ch)
        for ch in chains:
            stage2(i, *ch)
        for ch in chains:
            stage3(i, *ch)
        return carry

    lax.fori_loop(0, ITERS - 1, body, 0)
    for h, c in chains:
        advance(ITERS - 1, h, c)


def mix(heads, digit_ref, part_refs, solved_ref, kk_ref, rate_ref, vt_ref, vst_ref, gain_ref, outs):
    chunks = kk_ref.shape[1]
    per = outs[0].shape[0]
    keep = iota((CHUNK, CHUNK), 0) <= iota((CHUNK, CHUNK), 1)
    for h in range(heads):
        prior = gathered(digit_ref, part_refs, h, slice(PACKED, BOTH))
        gain = jnp.broadcast_to(gain_ref[:, head_cols(h)], (HEAD, HEAD)).T
        for c in range(chunks):
            span = slice(c * CHUNK, (c + 1) * CHUNK)
            right = jnp.concatenate(split(solved_ref[h, :, span]), 0)
            inner = dot(kk_ref[h, c], right)
            by = rate_ref[h, span]
            high, low = split(jnp.where(keep, inner * jnp.concatenate([by, by], 1), 0.0))
            mixed = dot(stack_state(prior if c == 0 else prior + vst_ref[h, c - 1]), right)
            vals = vt_ref[h, :, span]
            mixed = mixed[:HEAD] + mixed[HEAD:] + dot(vals, high) + dot(vals, low)
            normed = mixed * lax.rsqrt(jnp.mean(mixed * mixed, axis=0, keepdims=True) + EPS)
            normed = normed * jnp.concatenate([gain] * (CHUNK // HEAD), 1)
            outs[h // per][h % per, :, span] = normed.astype(BF16)


def attend_kernel(base_ref, query_ref, rim_ref, ko_ref, vo_ref, after_ref, out_ref, kk, vv):
    rows, width = ko_ref.shape
    kk[:WINDOW] = rim_ref[:, :width]
    kk[WINDOW:] = ko_ref[...]
    vv[:, :WINDOW] = rim_ref[:, width:].astype(F32).T.astype(BF16)
    vv[:, WINDOW:] = vo_ref[...].astype(F32).T.astype(BF16)
    bias = jnp.where(base_ref[0] > 0, 0.0, FAR).astype(F32)
    key_at, query_at = iota((HEAD, HEAD), 0), iota((HEAD, HEAD), 1)
    tiles = WINDOW // HEAD
    scale = 1.0 / math.sqrt(HEAD)
    for h in range(query_ref.shape[0]):
        for j in range(rows // HEAD):
            near = slice(j * HEAD, (j + tiles + 1) * HEAD)
            scores = dot(kk[near], query_ref[h, :, j * HEAD : (j + 1) * HEAD])
            pieces = []
            for t in range(tiles + 1):
                piece = scores[t * HEAD : (t + 1) * HEAD]
                if t == 0:
                    piece = jnp.where(key_at > query_at, piece, FAR)
                if t == tiles:
                    piece = jnp.where(key_at <= query_at, piece, FAR)
                if j + t < tiles:
                    piece = piece + bias
                pieces.append(piece)
            scores = jnp.concatenate(pieces, 0)
            peak = jnp.max(scores, axis=0, keepdims=True)
            grown = jnp.exp((scores - peak) * scale)
            share = 1.0 / jnp.sum(grown, axis=0, keepdims=True)
            mixed_vals = dot(vv[:, near], (grown * share).astype(BF16))
            out_ref[j * HEAD : (j + 1) * HEAD, head_cols(h)] = mixed_vals.T.astype(BF16)


def solve_kernel(heads, parts, groups, digit_ref, base_ref, ridge_ref, *refs):
    part_refs, refs = refs[:parts], refs[parts:]
    q_ref, k_ref, v_ref, gain_ref = refs[:4]
    outs, refs = refs[4 : 4 + groups], refs[4 + groups :]
    kk, kt, vt, kst, vst, coef, rates, causal, solved, state, res, way, rights, inners = refs
    prepare(heads, 0, base_ref, ridge_ref, q_ref, k_ref, v_ref, kk, kt, res, vt, kst, vst, coef, rates, causal)
    chebyshev(
        heads, 0, digit_ref, ridge_ref, part_refs,
        kk, kt, kst, coef, causal, solved, state, res, way, rights, inners,
    )
    mix(heads, digit_ref, part_refs, solved, kk, rates, vt, vst, gain_ref, outs)


def project_kernel(groups, count, *refs):
    out_ref = refs[-1]
    total = None
    for g in range(groups):
        for i in range(count):
            left = refs[g * count + i]
            width = left.shape[1]
            part = dot(left[...], refs[groups * count + i][g * width : (g + 1) * width])
            total = part if total is None else total + part
    out_ref[...] = total.astype(BF16)


SMEM = pl.BlockSpec(memory_space=pltpu.SMEM)
VMEM = pl.BlockSpec(memory_space=pltpu.VMEM)


def call(kernel, outs, args, scalars=0, scratch=(), flops=0, nbytes=0):
    return pl.pallas_call(
        kernel,
        out_shape=outs,
        in_specs=[SMEM] * scalars + [VMEM] * (len(args) - scalars),
        out_specs=jax.tree.map(lambda _: VMEM, outs),
        scratch_shapes=list(scratch),
        compiler_params=pltpu.CompilerParams(vmem_limit_bytes=28 * 1024 * 1024),
        cost_estimate=pl.CostEstimate(flops=flops, bytes_accessed=nbytes, transcendentals=0),
    )(*args)


def rounds_of(count, stride):
    rounds = []
    while stride < count:
        left = count // stride
        radix = 4 if left % 4 == 0 else 2 if left % 2 == 0 else left
        rounds.append((stride, radix))
        stride *= radix
    return rounds


def partner(i, stride, radix, k):
    digit = (i // stride) % radix
    other = digit ^ k if radix in (2, 4) else (digit + k) % radix
    return i + (other - digit) * stride


def swap(x, axis, stride, radix, k):
    n = lax.axis_size(axis)
    return lax.ppermute(x, axis, [(i, partner(i, stride, radix, k)) for i in range(n)])


def source_digit(mine, stride, radix, k):
    digit = (mine // stride) % radix
    return digit ^ k if radix in (2, 4) else (digit - k) % radix


def before_flags(axis, first):
    mine = lax.axis_index(axis)
    flags = [mine < 0]
    for stride, radix in rounds_of(lax.axis_size(axis), first):
        digit = (mine // stride) % radix
        flags += [source_digit(mine, stride, radix, k) < digit for k in range(1, radix)]
    return jnp.stack(flags[1:] or flags).astype(jnp.int32)


def shards(
    mixer_queries, mixer_keys, mixer_values, window_keys, window_values, out_gain, ridge, out_weight
):
    rows = mixer_queries.shape[0]
    heads = ridge.shape[0]
    chunks = rows // CHUNK
    seq, head = lax.axis_size("seq"), lax.axis_size("head")
    base = (lax.axis_index("seq") * rows).astype(jnp.int32).reshape(1)
    shares = next(n for n in (4, 2, 1) if heads % n == 0 and seq % n == 0)
    own = heads // shares
    digit = (lax.axis_index("seq") % shares).astype(jnp.int32).reshape(1)
    flags = before_flags("seq", shares)
    per = heads // GROUPS
    shape = jax.ShapeDtypeStruct
    width = window_keys.shape[1]
    block = shape((own, BOTH, HEAD), F32)

    def traded(parts):
        return [parts[0]] + [swap(parts[k], "seq", 1, shares, k) for k in range(1, shares)]

    rim = jnp.concatenate([window_keys, window_values], 1)[rows - WINDOW :]
    moments = call(
        functools.partial(moments_kernel, shares),
        (block,) * shares,
        (digit, mixer_keys, mixer_values),
        scalars=1,
    )
    moments = traded(moments)
    total = functools.reduce(jnp.add, moments)
    total, rim, out_weight = lax.optimization_barrier((total, rim, out_weight))
    mine = lax.axis_index("head")
    cols = out_weight.shape[1] // head
    rights = []
    for k in range(head):
        piece = lax.dynamic_slice_in_dim(out_weight, partner(mine, 1, head, k) * cols, cols, 1)
        rights.append(piece if k == 0 else swap(piece, "head", 1, head, k))
    common = jnp.zeros_like(total)
    rounds = rounds_of(seq, shares)
    i = 0
    for at, (stride, radix) in enumerate(rounds):
        got = [swap(total, "seq", stride, radix, k) for k in range(1, radix)]
        for part in got:
            common = common + jnp.where(flags[i] > 0, part, 0.0)
            i += 1
        if at + 1 < len(rounds):
            total = functools.reduce(jnp.add, got, total)
    priors = []
    for k in range(shares):
        prior = common
        for j in range(shares):
            if j != k:
                prior = prior + jnp.where((digit[0] ^ j) < (digit[0] ^ k), moments[j], 0.0)
        priors.append(prior)
    priors = traded(priors)
    priors, rim = lax.optimization_barrier((priors, rim))
    rim = lax.ppermute(rim, "seq", [(i, (i + 1) % seq) for i in range(seq)])

    queries = call(
        functools.partial(solve_kernel, heads, shares, GROUPS),
        (shape((per, HEAD, rows), BF16),) * GROUPS,
        (
            digit, base, ridge, *priors, mixer_queries, mixer_keys, mixer_values,
            out_gain.reshape(1, -1),
        ),
        scalars=3,
        scratch=(
            pltpu.VMEM((heads, chunks, CHUNK, 2 * HEAD), BF16),
            pltpu.VMEM((heads, chunks, HEAD, 2 * CHUNK), BF16),
            pltpu.VMEM((heads, HEAD, rows), BF16),
            pltpu.VMEM((heads, chunks - 1, HEAD, HEAD), F32),
            pltpu.VMEM((heads, chunks - 1, HEAD, HEAD), F32),
            pltpu.VMEM((heads, 2 * ITERS, rows), F32),
            pltpu.VMEM((heads, rows, HEAD), F32),
            pltpu.VMEM((heads, chunks, 3, HEAD, HEAD), F32),
            pltpu.VMEM((heads, HEAD, rows), F32),
            *cheb_scratch(heads, chunks),
        ),
        flops=10**10,
        nbytes=3 * 10**7,
    )
    lefts = []
    after = rim
    for g in range(GROUPS):
        (attended,) = call(
            attend_kernel,
            (shape((rows, per * HEAD), BF16),),
            (base, queries[g], rim, window_keys, window_values, after),
            scalars=1,
            scratch=(pltpu.VMEM((WINDOW + rows, width), BF16), pltpu.VMEM((width, WINDOW + rows), BF16)),
            flops=4 * 10**9,
            nbytes=15 * 10**6,
        )
        after = attended
        if head == 4:
            far = swap(attended, "head", 1, 4, 2)
            lefts += [attended, swap(attended, "head", 1, 4, 1), far, swap(far, "head", 1, 4, 1)]
        else:
            lefts += [attended] + [swap(attended, "head", 1, head, k) for k in range(1, head)]
    return call(
        functools.partial(project_kernel, GROUPS, head),
        shape((rows, cols), BF16),
        (*lefts, *rights),
    )


def solution(mesh):
    return jax.shard_map(
        shards,
        mesh=mesh,
        in_specs=(
            P("seq", "head"),
            P("seq", "head"),
            P("seq", "head"),
            P("seq", "head"),
            P("seq", "head"),
            P("head"),
            P("head"),
            P("head", None),
        ),
        out_specs=P("seq", "head"),
        check_vma=False,
    )
```

time: 74.3 us -> 65.3 us (0.88)
  waiting for transfers between devices: 16.6 us -> 25.9 us
  Pallas kernels: 27.3 us -> 19.2 us
  starting transfers between devices: 22.7 us -> 16.3 us
  local copies, waits for them, and re-layouts: 6.89 us -> 2.36 us
  other arithmetic: 0.19 us -> 1.13 us
    ppermute x17 -> x16, waiting for transfers between devices: 16.6 us -> 25.9 us  [swap(): lax.ppermute(x, axis, [(i, partner(i, stride, radix, k)) for i in range(n)])]
    pallas_call x7 -> x5, Pallas kernels: 27.3 us -> 19.2 us  [call(): pl.pallas_call(kernel, out_shape=outs, in_specs=[SMEM] * scalars + [VMEM]...]
    ppermute x17 -> x16, starting transfers between devices: 21.2 us -> 15.4 us  [swap(): lax.ppermute(x, axis, [(i, partner(i, stride, radix, k)) for i in range(n)])]
    unnamed x24 -> x20, local copies, waits for them, and re-layouts: 6.65 us -> 2.12 us
    concatenate x0 -> x1, other arithmetic: none -> 1 us  [shards(): rim = jnp.concatenate([window_keys, window_values], 1)[rows - WINDOW:]]
  transfers between devices with their start and end apart: 18 -> 17, of which waited for: 6 -> 8; matrix products, arithmetic and copies ran while one was open for 1% -> 2% of each run, Pallas kernels for 33% -> 24%
where the time goes in v3:
time: 65.3 us; the launch traced here: 65.1 us
  waiting for transfers between devices  25.9 us (40%)
  Pallas kernels  19.2 us (29%)
  starting transfers between devices  16.3 us (25%)
  local copies, waits for them, and re-layouts  2.36 us (4%)
  other arithmetic  1.13 us (2%)
    ppermute x16, waiting for transfers between devices, swap(): lax.ppermute(x, axis, [(i, partner(i, stride, radix, k)) for i in range(n)])  25.9 us
    pallas_call x5, Pallas kernels, call(): pl.pallas_call(kernel, out_shape=outs, in_specs=[SMEM] * scalars + [VMEM]...  19.2 us
    ppermute x16, starting transfers between devices, swap(): lax.ppermute(x, axis, [(i, partner(i, stride, radix, k)) for i in range(n)])  15.4 us
    unnamed x20, local copies, waits for them, and re-layouts  2.12 us
  transfers between devices with their start and end apart: 17, of which 8 were waited for; matrix products, arithmetic and copies ran while one was open for 2% of the time, Pallas kernels for 24%

profile of v3, /device:TPU:0, one launch (start us, length us, event | category | flops | bytes accessed | tf_op | source)
XLA Modules:
  0.0 65.1 jit_solution(5659178076995188608)
XLA Ops:
  0.0 1.0 %copy-done = bf16[512,512]{1,0:T(8,128)(2,1)S(1)} copy-done((bf16[512,512]{1,0:T(8,128)(2,1)S(1)}, bf16[512,512]{1,0:T(8,128)(2,1)}, u32[]{:S(2)}) %copy-start) | copy-done | bytes 524312
  1.0 1.0 %copy-done.2 = bf16[512,512]{1,0:T(8,128)(2,1)S(1)} copy-done((bf16[512,512]{1,0:T(8,128)(2,1)S(1)}, bf16[512,512]{1,0:T(8,128)(2,1)}, u32[]{:S(2)}) %copy-start.2) | copy-done | bytes 524312
  2.1 1.6 %shard_map.82 = (f32[1,200,128]{2,1,0:T(8,128)S(1)}, f32[1,200,128]{2,1,0:T(8,128)S(1)}, f32[1,200,128]{2,1,0:T(8,128)S(1)}, f32[1,200,128]{2,1,0:T(8,128)S(1)}) custom-call(s32[1]{0:T(128)} %bitcast.1.digit_ref, bf16[512,512]{1,0:T(8,128)(2,1)S(1)} %copy-done, bf16[512,512]{1,0:T(8,128)(2,1)S(1)} %copy-done.2), custom_call_target="tpu_custom_call" | custom-call | tf_op jit(solution)/shard_map/pallas_call | solution.py:312
  3.7 3.0 %collective-permute-start = (f32[1,200,128]{2,1,0:T(8,128)S(1)}, f32[1,200,128]{2,1,0:T(8,128)S(1)}, u32[]{:S(2)}, u32[]{:S(2)}) collective-permute-start(f32[1,200,128]{2,1,0:T(8,128)S(1)} %get-tuple-element.20), channel_id=1, source_target_pairs={{0,4},{4,0},{8,12},{12,8},{16,20},{20,16},{24,28},{28,24},{1,5},{5... | collective-permute-start | bytes 307208 | tf_op jit(solution)/shard_map/ppermute | solution.py:341
  6.7 1.6 %collective-permute-start.1 = (f32[1,200,128]{2,1,0:T(8,128)S(1)}, f32[1,200,128]{2,1,0:T(8,128)S(1)}, u32[]{:S(2)}, u32[]{:S(2)}) collective-permute-start(f32[1,200,128]{2,1,0:T(8,128)S(1)} %get-tuple-element.21), channel_id=1, source_target_pairs={{0,8},{4,12},{8,0},{12,4},{16,24},{20,28},{24,16},{28,20},{1,9},{5... | collective-permute-start | bytes 307208 | tf_op jit(solution)/shard_map/ppermute | solution.py:341
  8.3 1.0 %pad_maximum_fusion = bf16[512,256]{1,0:T(8,128)(2,1)S(1)} fusion(bf16[512,128]{1,0:T(8,128)(2,1)} %vo_ref.3, bf16[512,128]{1,0:T(8,128)(2,1)} %ko_ref.3), kind=kLoop, calls=%fused_computation | loop fusion | flops 524288 | bytes 524288 | tf_op jit(solution)/shard_map/concatenate | solution.py:378
  9.6 2.7 %collective-permute-done.1 = f32[1,200,128]{2,1,0:T(8,128)S(1)} collective-permute-done((f32[1,200,128]{2,1,0:T(8,128)S(1)}, f32[1,200,128]{2,1,0:T(8,128)S(1)}, u32[]{:S(2)}, u32[]{:S(2)}) %collective-permute-start.1) | collective-permute-done | bytes 102432 | tf_op jit(solution)/shard_map/ppermute | solution.py:341
  12.3 1.6 %collective-permute-done.2 = f32[1,200,128]{2,1,0:T(8,128)S(1)} collective-permute-done((f32[1,200,128]{2,1,0:T(8,128)S(1)}, f32[1,200,128]{2,1,0:T(8,128)S(1)}, u32[]{:S(2)}, u32[]{:S(2)}) %collective-permute-start.2) | collective-permute-done | bytes 102432 | tf_op jit(solution)/shard_map/ppermute | solution.py:341
  13.9 2.6 %collective-permute-start.3 = (f32[1,200,128]{2,1,0:T(8,128)S(1)}, f32[1,200,128]{2,1,0:T(8,128)S(1)}, u32[]{:S(2)}, u32[]{:S(2)}) collective-permute-start(f32[1,200,128]{2,1,0:T(8,128)S(1)} %add_add_fusion), channel_id=1, source_target_pairs={{0,16},{4,20},{8,24},{12,28},{16,0},{20,4},{24,8},{28,12},{1,17},{... | collective-permute-start | bytes 307208 | tf_op jit(solution)/shard_map/ppermute | solution.py:341
  16.5 4.1 %collective-permute-done.3 = f32[1,200,128]{2,1,0:T(8,128)S(1)} collective-permute-done((f32[1,200,128]{2,1,0:T(8,128)S(1)}, f32[1,200,128]{2,1,0:T(8,128)S(1)}, u32[]{:S(2)}, u32[]{:S(2)}) %collective-permute-start.3) | collective-permute-done | bytes 102432 | tf_op jit(solution)/shard_map/ppermute | solution.py:341
  20.7 1.1 %collective-permute-start.4 = (f32[1,200,128]{2,1,0:T(8,128)S(1)}, f32[1,200,128]{2,1,0:T(8,128)S(1)}, u32[]{:S(2)}, u32[]{:S(2)}) collective-permute-start(f32[1,200,128]{2,1,0:T(8,128)S(1)} %get-tuple-element.39), channel_id=1, source_target_pairs={{0,4},{4,0},{8,12},{12,8},{16,20},{20,16},{24,28},{28,24},{1,5},{5... | collective-permute-start | bytes 307208 | tf_op jit(solution)/shard_map/ppermute | solution.py:341
  21.8 0.6 collective-permute-start.5
  22.4 1.9 %collective-permute-start.6 = (f32[1,200,128]{2,1,0:T(8,128)S(1)}, f32[1,200,128]{2,1,0:T(8,128)S(1)}, u32[]{:S(2)}, u32[]{:S(2)}) collective-permute-start(f32[1,200,128]{2,1,0:T(8,128)S(1)} %get-tuple-element.37), channel_id=1, source_target_pairs={{0,12},{4,8},{8,4},{12,0},{16,28},{20,24},{24,20},{28,16},{1,13},{... | collective-permute-start | bytes 307208 | tf_op jit(solution)/shard_map/ppermute | solution.py:341
  24.7 1.6 %collective-permute-start.15 = (bf16[512,512]{1,0:T(8,128)(2,1)S(1)}, bf16[512,512]{1,0:T(8,128)(2,1)S(1)}, u32[]{:S(2)}, u32[]{:S(2)}) collective-permute-start(bf16[512,512]{1,0:T(8,128)(2,1)S(1)} %get-tuple-element.34), channel_id=1, source_target_pairs={{0,2},{1,3},{2,0},{3,1},{4,6},{5,7},{6,4},{7,5},{8,10},{9,11},{10,... | collective-permute-start | bytes 1572872 | tf_op jit(solution)/shard_map/ppermute | solution.py:341
  26.5 1.5 %collective-permute-done.6.refs_3_ = f32[1,200,128]{2,1,0:T(8,128)S(1)} collective-permute-done((f32[1,200,128]{2,1,0:T(8,128)S(1)}, f32[1,200,128]{2,1,0:T(8,128)S(1)}, u32[]{:S(2)}, u32[]{:S(2)}) %collective-permute-start.6) | collective-permute-done | bytes 102432 | tf_op jit(solution)/shard_map/ppermute | solution.py:341
  28.1 0.9 %collective-permute-start.7 = (bf16[512,256]{1,0:T(8,128)(2,1)S(1)}, bf16[512,256]{1,0:T(8,128)(2,1)S(1)}, u32[]{:S(2)}, u32[]{:S(2)}) collective-permute-start(bf16[512,256]{1,0:T(8,128)(2,1)S(1)} %pad_maximum_fusion), channel_id=1, source_target_pairs={{0,4},{4,8},{8,12},{12,16},{16,20},{20,24},{24,28},{28,0},{1,5},{5... | collective-permute-start | bytes 786440 | tf_op jit(solution)/shard_map/ppermute | solution.py:413
  29.0 12.3 %shard_map.83 = (bf16[2,128,512]{2,1,0:T(8,128)(2,1)S(1)}, bf16[2,128,512]{2,1,0:T(8,128)(2,1)S(1)}) custom-call(s32[1]{0:T(128)} %bitcast.1.digit_ref, s32[1]{0:T(128)} %bitcast.base_ref, f32[4]{0:T(128)S(1)} %copy-done.8, f32[1,200,128]{2,1,0:T(8,128)S(1)} %get-tuple-element.25.refs_0_, f32[1,200,128]{2,1,0:T(8,128)S(1)} %collective-permute-done.4.refs_1_, ...), custom_call_target="tpu_custom_call" | custom-call | flops 10000000000 | bytes 30000000 | tf_op jit(solution)/shard_map/pallas_call | solution.py:312
  41.4 1.6 %shard_map.84.after_ref.refs_0_ = bf16[512,256]{1,0:T(8,128)(2,1)S(1)} custom-call(s32[1]{0:T(128)} %bitcast.base_ref, bf16[2,128,512]{2,1,0:T(8,128)(2,1)S(1)} %get-tuple-element.29.query_ref, bf16[512,256]{1,0:T(8,128)(2,1)S(1)} %collective-permute-done.7.rim_ref.after_ref, bf16[512,128]{1,0:T(8,128)(2,1)S(1)} %copy-done.5, ...), custom_call_target="tpu_custom_call" | custom-call | flops 4000000000 | bytes 15000000 | tf_op jit(solution)/shard_map/pallas_call | solution.py:312
  43.0 1.7 %shard_map.85.refs_4_ = bf16[512,256]{1,0:T(8,128)(2,1)S(1)} custom-call(s32[1]{0:T(128)} %bitcast.base_ref, bf16[2,128,512]{2,1,0:T(8,128)(2,1)S(1)} %get-tuple-element.31.query_ref, bf16[512,256]{1,0:T(8,128)(2,1)S(1)} %collective-permute-done.7.rim_ref.after_ref, bf16[512,128]{1,0:T(8,128)(2,1)S(1)} %copy-done.5, bf16[512,128]{1,0:T(8,128)(2,1)S(1)} %copy-done.4, ...), custom_call_target="tpu_custom_call" | custom-call | flops 4000000000 | bytes 15000000 | tf_op jit(solution)/shard_map/pallas_call | solution.py:312
  44.7 1.6 %collective-permute-start.12 = (bf16[512,256]{1,0:T(8,128)(2,1)S(1)}, bf16[512,256]{1,0:T(8,128)(2,1)S(1)}, u32[]{:S(2)}, u32[]{:S(2)}) collective-permute-start(bf16[512,256]{1,0:T(8,128)(2,1)S(1)} %shard_map.85.refs_4_), channel_id=1, source_target_pairs={{0,2},{1,3},{2,0},{3,1},{4,6},{5,7},{6,4},{7,5},{8,10},{9,11},{10,... | collective-permute-start | bytes 786440 | tf_op jit(solution)/shard_map/ppermute | solution.py:341
  47.3 9.0 %collective-permute-done.12.refs_6_ = bf16[512,256]{1,0:T(8,128)(2,1)S(1)} collective-permute-done((bf16[512,256]{1,0:T(8,128)(2,1)S(1)}, bf16[512,256]{1,0:T(8,128)(2,1)S(1)}, u32[]{:S(2)}, u32[]{:S(2)}) %collective-permute-start.12) | collective-permute-done | bytes 262176 | tf_op jit(solution)/shard_map/ppermute | solution.py:341
  56.3 5.2 %collective-permute-done.9.refs_2_ = bf16[512,256]{1,0:T(8,128)(2,1)S(1)} collective-permute-done((bf16[512,256]{1,0:T(8,128)(2,1)S(1)}, bf16[512,256]{1,0:T(8,128)(2,1)S(1)}, u32[]{:S(2)}, u32[]{:S(2)}) %collective-permute-start.9) | collective-permute-done | bytes 262176 | tf_op jit(solution)/shard_map/ppermute | solution.py:341
  61.5 1.5 %collective-permute-done.10.refs_3_ = bf16[512,256]{1,0:T(8,128)(2,1)S(1)} collective-permute-done((bf16[512,256]{1,0:T(8,128)(2,1)S(1)}, bf16[512,256]{1,0:T(8,128)(2,1)S(1)}, u32[]{:S(2)}, u32[]{:S(2)}) %collective-permute-start.10) | collective-permute-done | bytes 262176 | tf_op jit(solution)/shard_map/ppermute | solution.py:341
  63.0 2.0 %shard_map.86 = bf16[512,512]{1,0:T(8,128)(2,1)} custom-call(bf16[512,256]{1,0:T(8,128)(2,1)S(1)} %shard_map.84.after_ref.refs_0_, bf16[512,256]{1,0:T(8,128)(2,1)S(1)} %collective-permute-done.8.refs_1_, bf16[512,256]{1,0:T(8,128)(2,1)S(1)} %collective-permute-done.9.refs_2_, bf16[512,256]{1,0:T(8,128)(2,1)S(1)} %collective-permute-done.10.refs_3_, ...), custom_call_target="tpu_custom_call" | custom-call | tf_op jit(solution)/shard_map/pallas_call | solution.py:312
  (39 shorter events, 2.2 us)
Async XLA Ops:
  2.1 22.3 %copy-start.9 = (bf16[512,2048]{1,0:T(8,128)(2,1)S(1)}, bf16[512,2048]{1,0:T(8,128)(2,1)}, u32[]{:S(2)}) copy-start(bf16[512,2048]{1,0:T(8,128)(2,1)} %param.15) | copy-start | bytes 6291460
  3.7 5.9 %collective-permute-start = (f32[1,200,128]{2,1,0:T(8,128)S(1)}, f32[1,200,128]{2,1,0:T(8,128)S(1)}, u32[]{:S(2)}, u32[]{:S(2)}) collective-permute-start(f32[1,200,128]{2,1,0:T(8,128)S(1)} %get-tuple-element.20), channel_id=1, source_target_pairs={{0,4},{4,0},{8,12},{12,8},{16,20},{20,16},{24,28},{28,24},{1,5},{5... | collective-permute-start | bytes 307208 | tf_op jit(solution)/shard_map/ppermute | solution.py:341
  6.7 5.6 %collective-permute-start.1 = (f32[1,200,128]{2,1,0:T(8,128)S(1)}, f32[1,200,128]{2,1,0:T(8,128)S(1)}, u32[]{:S(2)}, u32[]{:S(2)}) collective-permute-start(f32[1,200,128]{2,1,0:T(8,128)S(1)} %get-tuple-element.21), channel_id=1, source_target_pairs={{0,8},{4,12},{8,0},{12,4},{16,24},{20,28},{24,16},{28,20},{1,9},{5... | collective-permute-start | bytes 307208 | tf_op jit(solution)/shard_map/ppermute | solution.py:341
  8.3 5.6 %collective-permute-start.2 = (f32[1,200,128]{2,1,0:T(8,128)S(1)}, f32[1,200,128]{2,1,0:T(8,128)S(1)}, u32[]{:S(2)}, u32[]{:S(2)}) collective-permute-start(f32[1,200,128]{2,1,0:T(8,128)S(1)} %get-tuple-element.22), channel_id=1, source_target_pairs={{0,12},{4,8},{8,4},{12,0},{16,28},{20,24},{24,20},{28,16},{1,13},{... | collective-permute-start | bytes 307208 | tf_op jit(solution)/shard_map/ppermute | solution.py:341
  13.9 6.7 %collective-permute-start.3 = (f32[1,200,128]{2,1,0:T(8,128)S(1)}, f32[1,200,128]{2,1,0:T(8,128)S(1)}, u32[]{:S(2)}, u32[]{:S(2)}) collective-permute-start(f32[1,200,128]{2,1,0:T(8,128)S(1)} %add_add_fusion), channel_id=1, source_target_pairs={{0,16},{4,20},{8,24},{12,28},{16,0},{20,4},{24,8},{28,12},{1,17},{... | collective-permute-start | bytes 307208 | tf_op jit(solution)/shard_map/ppermute | solution.py:341
  20.7 5.5 %collective-permute-start.4 = (f32[1,200,128]{2,1,0:T(8,128)S(1)}, f32[1,200,128]{2,1,0:T(8,128)S(1)}, u32[]{:S(2)}, u32[]{:S(2)}) collective-permute-start(f32[1,200,128]{2,1,0:T(8,128)S(1)} %get-tuple-element.39), channel_id=1, source_target_pairs={{0,4},{4,0},{8,12},{12,8},{16,20},{20,16},{24,28},{28,24},{1,5},{5... | collective-permute-start | bytes 307208 | tf_op jit(solution)/shard_map/ppermute | solution.py:341
  21.8 4.8 %collective-permute-start.5 = (f32[1,200,128]{2,1,0:T(8,128)S(1)}, f32[1,200,128]{2,1,0:T(8,128)S(1)}, u32[]{:S(2)}, u32[]{:S(2)}) collective-permute-start(f32[1,200,128]{2,1,0:T(8,128)S(1)} %get-tuple-element.38), channel_id=1, source_target_pairs={{0,8},{4,12},{8,0},{12,4},{16,24},{20,28},{24,16},{28,20},{1,9},{5... | collective-permute-start | bytes 307208 | tf_op jit(solution)/shard_map/ppermute | solution.py:341
  22.4 6.6 %copy-start.3 = (bf16[512,512]{1,0:T(8,128)(2,1)S(1)}, bf16[512,512]{1,0:T(8,128)(2,1)}, u32[]{:S(2)}) copy-start(bf16[512,512]{1,0:T(8,128)(2,1)} %refs_6_.1) | copy-start | bytes 1572868
  22.4 6.6 %copy-start.6 = (bf16[512,512]{1,0:T(8,128)(2,1)S(1)}, bf16[512,512]{1,0:T(8,128)(2,1)}, u32[]{:S(2)}) copy-start(bf16[512,512]{1,0:T(8,128)(2,1)} %refs_4_.1) | copy-start | bytes 1572868
  22.4 6.6 %copy-start.7 = (f32[512]{0:T(512)S(1)}, f32[512]{0:T(512)}, u32[]{:S(2)}) copy-start(f32[512]{0:T(512)} %param.13) | copy-start | bytes 6148
  22.4 6.6 %copy-start.8 = (f32[4]{0:T(128)S(1)}, f32[4]{0:T(128)}, u32[]{:S(2)}) copy-start(f32[4]{0:T(128)} %ridge_ref.1) | copy-start | bytes 52
  22.4 5.6 %collective-permute-start.6 = (f32[1,200,128]{2,1,0:T(8,128)S(1)}, f32[1,200,128]{2,1,0:T(8,128)S(1)}, u32[]{:S(2)}, u32[]{:S(2)}) collective-permute-start(f32[1,200,128]{2,1,0:T(8,128)S(1)} %get-tuple-element.37), channel_id=1, source_target_pairs={{0,12},{4,8},{8,4},{12,0},{16,28},{20,24},{24,20},{28,16},{1,13},{... | collective-permute-start | bytes 307208 | tf_op jit(solution)/shard_map/ppermute | solution.py:341
  24.6 22.2 %collective-permute-start.14 = (bf16[512,512]{1,0:T(8,128)(2,1)S(1)}, bf16[512,512]{1,0:T(8,128)(2,1)S(1)}, u32[]{:S(2)}, u32[]{:S(2)}) collective-permute-start(bf16[512,512]{1,0:T(8,128)(2,1)S(1)} %get-tuple-element.35), channel_id=1, source_target_pairs={{0,1},{1,0},{2,3},{3,2},{4,5},{5,4},{6,7},{7,6},{8,9},{9,8},{10,11... | collective-permute-start | bytes 1572872 | tf_op jit(solution)/shard_map/ppermute | solution.py:341
  24.7 22.1 %collective-permute-start.15 = (bf16[512,512]{1,0:T(8,128)(2,1)S(1)}, bf16[512,512]{1,0:T(8,128)(2,1)S(1)}, u32[]{:S(2)}, u32[]{:S(2)}) collective-permute-start(bf16[512,512]{1,0:T(8,128)(2,1)S(1)} %get-tuple-element.34), channel_id=1, source_target_pairs={{0,2},{1,3},{2,0},{3,1},{4,6},{5,7},{6,4},{7,5},{8,10},{9,11},{10,... | collective-permute-start | bytes 1572872 | tf_op jit(solution)/shard_map/ppermute | solution.py:341
  26.2 35.3 %collective-permute-start.16 = (bf16[512,512]{1,0:T(8,128)(2,1)S(1)}, bf16[512,512]{1,0:T(8,128)(2,1)S(1)}, u32[]{:S(2)}, u32[]{:S(2)}) collective-permute-start(bf16[512,512]{1,0:T(8,128)(2,1)S(1)} %get-tuple-element.33), channel_id=1, source_target_pairs={{0,3},{1,2},{2,1},{3,0},{4,7},{5,6},{6,5},{7,4},{8,11},{9,10},{10,... | collective-permute-start | bytes 1572872 | tf_op jit(solution)/shard_map/ppermute | solution.py:341
  28.1 13.3 %collective-permute-start.7 = (bf16[512,256]{1,0:T(8,128)(2,1)S(1)}, bf16[512,256]{1,0:T(8,128)(2,1)S(1)}, u32[]{:S(2)}, u32[]{:S(2)}) collective-permute-start(bf16[512,256]{1,0:T(8,128)(2,1)S(1)} %pad_maximum_fusion), channel_id=1, source_target_pairs={{0,4},{4,8},{8,12},{12,16},{16,20},{20,24},{24,28},{28,0},{1,5},{5... | collective-permute-start | bytes 786440 | tf_op jit(solution)/shard_map/ppermute | solution.py:413
  29.0 12.3 %copy-start.4 = (bf16[512,128]{1,0:T(8,128)(2,1)S(1)}, bf16[512,128]{1,0:T(8,128)(2,1)}, u32[]{:S(2)}) copy-start(bf16[512,128]{1,0:T(8,128)(2,1)} %vo_ref.3) | copy-start | bytes 393220
  29.0 12.3 %copy-start.5 = (bf16[512,128]{1,0:T(8,128)(2,1)S(1)}, bf16[512,128]{1,0:T(8,128)(2,1)}, u32[]{:S(2)}) copy-start(bf16[512,128]{1,0:T(8,128)(2,1)} %ko_ref.3) | copy-start | bytes 393220
  44.7 11.6 %collective-permute-start.12 = (bf16[512,256]{1,0:T(8,128)(2,1)S(1)}, bf16[512,256]{1,0:T(8,128)(2,1)S(1)}, u32[]{:S(2)}, u32[]{:S(2)}) collective-permute-start(bf16[512,256]{1,0:T(8,128)(2,1)S(1)} %shard_map.85.refs_4_), channel_id=1, source_target_pairs={{0,2},{1,3},{2,0},{3,1},{4,6},{5,7},{6,4},{7,5},{8,10},{9,11},{10,... | collective-permute-start | bytes 786440 | tf_op jit(solution)/shard_map/ppermute | solution.py:341
  46.2 15.2 %collective-permute-start.9 = (bf16[512,256]{1,0:T(8,128)(2,1)S(1)}, bf16[512,256]{1,0:T(8,128)(2,1)S(1)}, u32[]{:S(2)}, u32[]{:S(2)}) collective-permute-start(bf16[512,256]{1,0:T(8,128)(2,1)S(1)} %shard_map.84.after_ref.refs_0_), channel_id=1, source_target_pairs={{0,2},{1,3},{2,0},{3,1},{4,6},{5,7},{6,4},{7,5},{8,10},{9,11},{10,... | collective-permute-start | bytes 786440 | tf_op jit(solution)/shard_map/ppermute | solution.py:341
  46.8 14.7 %collective-permute-start.11 = (bf16[512,256]{1,0:T(8,128)(2,1)S(1)}, bf16[512,256]{1,0:T(8,128)(2,1)S(1)}, u32[]{:S(2)}, u32[]{:S(2)}) collective-permute-start(bf16[512,256]{1,0:T(8,128)(2,1)S(1)} %shard_map.85.refs_4_), channel_id=1, source_target_pairs={{0,1},{1,0},{2,3},{3,2},{4,5},{5,4},{6,7},{7,6},{8,9},{9,8},{10,11... | collective-permute-start | bytes 786440 | tf_op jit(solution)/shard_map/ppermute | solution.py:341
  46.8 14.7 %collective-permute-start.8 = (bf16[512,256]{1,0:T(8,128)(2,1)S(1)}, bf16[512,256]{1,0:T(8,128)(2,1)S(1)}, u32[]{:S(2)}, u32[]{:S(2)}) collective-permute-start(bf16[512,256]{1,0:T(8,128)(2,1)S(1)} %shard_map.84.after_ref.refs_0_), channel_id=1, source_target_pairs={{0,1},{1,0},{2,3},{3,2},{4,5},{5,4},{6,7},{7,6},{8,9},{9,8},{10,11... | collective-permute-start | bytes 786440 | tf_op jit(solution)/shard_map/ppermute | solution.py:341
  56.3 5.2 %collective-permute-start.13 = (bf16[512,256]{1,0:T(8,128)(2,1)S(1)}, bf16[512,256]{1,0:T(8,128)(2,1)S(1)}, u32[]{:S(2)}, u32[]{:S(2)}) collective-permute-start(bf16[512,256]{1,0:T(8,128)(2,1)S(1)} %collective-permute-done.12.refs_6_), channel_id=1, source_target_pairs={{0,1},{1,0},{2,3},{3,2},{4,5},{5,4},{6,7},{7,6},{8,9},{9,8},{10,11... | collective-permute-start | bytes 786440 | tf_op jit(solution)/shard_map/ppermute | solution.py:341
  61.5 1.5 %collective-permute-start.10 = (bf16[512,256]{1,0:T(8,128)(2,1)S(1)}, bf16[512,256]{1,0:T(8,128)(2,1)S(1)}, u32[]{:S(2)}, u32[]{:S(2)}) collective-permute-start(bf16[512,256]{1,0:T(8,128)(2,1)S(1)} %collective-permute-done.9.refs_2_), channel_id=1, source_target_pairs={{0,1},{1,0},{2,3},{3,2},{4,5},{5,4},{6,7},{7,6},{8,9},{9,8},{10,11... | collective-permute-start | bytes 786440 | tf_op jit(solution)/shard_map/ppermute | solution.py:341
  (3 other events, 8.7 us)

commit v4 on v3

--- a/solution.py
+++ b/solution.py
@@ -16,7 +16,6 @@
 CHUNK = 256
 PACKED = HALF + 8
 BOTH = PACKED + HEAD
-GROUPS = 2
 FAR = -1e30
 F32 = jnp.float32
 BF16 = jnp.bfloat16
@@ -63,6 +62,10 @@
     low = jnp.where((col < HALF) & (row <= col), body, 0.0) * jnp.where(row == col, 0.5, 1.0)
     half = jnp.concatenate([top, pltpu.roll(low, HALF, 1)], 0)
     return half + half.T
+
+
+def group_sizes(heads):
+    return [heads - heads // 2, heads // 2] if heads > 1 else [1]
 
 
 def moments_kernel(shares, digit_ref, keys_ref, vals_ref, *outs):
@@ -226,13 +229,12 @@
         advance(ITERS - 1, h, c)
 
 
-def mix(heads, digit_ref, part_refs, solved_ref, kk_ref, rate_ref, vt_ref, vst_ref, gain_ref, outs):
+def mix(heads, first, digit_ref, part_refs, solved_ref, kk_ref, rate_ref, vt_ref, vst_ref, gain_ref, out_ref):
     chunks = kk_ref.shape[1]
-    per = outs[0].shape[0]
     keep = iota((CHUNK, CHUNK), 0) <= iota((CHUNK, CHUNK), 1)
     for h in range(heads):
-        prior = gathered(digit_ref, part_refs, h, slice(PACKED, BOTH))
-        gain = jnp.broadcast_to(gain_ref[:, head_cols(h)], (HEAD, HEAD)).T
+        prior = gathered(digit_ref, part_refs, first + h, slice(PACKED, BOTH))
+        gain = jnp.broadcast_to(gain_ref[:, head_cols(first + h)], (HEAD, HEAD)).T
         for c in range(chunks):
             span = slice(c * CHUNK, (c + 1) * CHUNK)
             right = jnp.concatenate(split(solved_ref[h, :, span]), 0)
@@ -244,7 +246,7 @@
             mixed = mixed[:HEAD] + mixed[HEAD:] + dot(vals, high) + dot(vals, low)
             normed = mixed * lax.rsqrt(jnp.mean(mixed * mixed, axis=0, keepdims=True) + EPS)
             normed = normed * jnp.concatenate([gain] * (CHUNK // HEAD), 1)
-            outs[h // per][h % per, :, span] = normed.astype(BF16)
+            out_ref[h, :, span] = normed.astype(BF16)
 
 
 def attend_kernel(base_ref, query_ref, rim_ref, ko_ref, vo_ref, after_ref, out_ref, kk, vv):
@@ -279,29 +281,24 @@
             out_ref[j * HEAD : (j + 1) * HEAD, head_cols(h)] = mixed_vals.T.astype(BF16)
 
 
-def solve_kernel(heads, parts, groups, digit_ref, base_ref, ridge_ref, *refs):
+def solve_kernel(heads, parts, first, digit_ref, base_ref, ridge_ref, *refs):
     part_refs, refs = refs[:parts], refs[parts:]
-    q_ref, k_ref, v_ref, gain_ref = refs[:4]
-    outs, refs = refs[4 : 4 + groups], refs[4 + groups :]
+    q_ref, k_ref, v_ref, gain_ref, after_ref, out_ref, *refs = refs
     kk, kt, vt, kst, vst, coef, rates, causal, solved, state, res, way, rights, inners = refs
-    prepare(heads, 0, base_ref, ridge_ref, q_ref, k_ref, v_ref, kk, kt, res, vt, kst, vst, coef, rates, causal)
+    prepare(heads, first, base_ref, ridge_ref, q_ref, k_ref, v_ref, kk, kt, res, vt, kst, vst, coef, rates, causal)
     chebyshev(
-        heads, 0, digit_ref, ridge_ref, part_refs,
+        heads, first, digit_ref, ridge_ref, part_refs,
         kk, kt, kst, coef, causal, solved, state, res, way, rights, inners,
     )
-    mix(heads, digit_ref, part_refs, solved, kk, rates, vt, vst, gain_ref, outs)
-
-
-def project_kernel(groups, count, *refs):
-    out_ref = refs[-1]
-    total = None
-    for g in range(groups):
-        for i in range(count):
-            left = refs[g * count + i]
-            width = left.shape[1]
-            part = dot(left[...], refs[groups * count + i][g * width : (g + 1) * width])
-            total = part if total is None else total + part
-    out_ref[...] = total.astype(BF16)
+    mix(heads, first, digit_ref, part_refs, solved, kk, rates, vt, vst, gain_ref, out_ref)
+
+
+def project_kernel(pairs, count, *refs):
+    out_ref, last = refs[-1], refs[-2][...] if len(refs) > count + 1 else None
+    for left, right, row in pairs:
+        part = dot(refs[left][...], refs[right][row : row + refs[left].shape[1]])
+        last = part if last is None else last + part
+    out_ref[...] = last.astype(out_ref.dtype)
 
 
 SMEM = pl.BlockSpec(memory_space=pltpu.SMEM)
@@ -367,7 +364,7 @@
     own = heads // shares
     digit = (lax.axis_index("seq") % shares).astype(jnp.int32).reshape(1)
     flags = before_flags("seq", shares)
-    per = heads // GROUPS
+    sizes = group_sizes(heads)
     shape = jax.ShapeDtypeStruct
     width = window_keys.shape[1]
     block = shape((own, BOTH, HEAD), F32)
@@ -384,13 +381,21 @@
     )
     moments = traded(moments)
     total = functools.reduce(jnp.add, moments)
-    total, rim, out_weight = lax.optimization_barrier((total, rim, out_weight))
     mine = lax.axis_index("head")
     cols = out_weight.shape[1] // head
-    rights = []
-    for k in range(head):
-        piece = lax.dynamic_slice_in_dim(out_weight, partner(mine, 1, head, k) * cols, cols, 1)
-        rights.append(piece if k == 0 else swap(piece, "head", 1, head, k))
+    def columns(x, block, count=1):
+        return lax.dynamic_slice_in_dim(x, block * cols, count * cols, 1)
+
+    w_far = rim
+    if head == 4:
+        core = mine % 2
+        near = swap(columns(out_weight, mine ^ 1), "head", 1, 4, 1)
+        w_far = swap(columns(out_weight, (mine // 2 ^ 1) * 2, 2), "head", 1, 4, 2)
+        relayed = swap(columns(w_far, core ^ 1), "head", 1, 4, 1)
+        rights = [columns(out_weight, mine), near, columns(w_far, core), relayed]
+    else:
+        rights = [columns(out_weight, mine)]
+        rights += [swap(columns(out_weight, partner(mine, 1, head, k)), "head", 1, head, k) for k in range(1, head)]
     common = jnp.zeros_like(total)
     rounds = rounds_of(seq, shares)
     i = 0
@@ -409,55 +414,68 @@
                 prior = prior + jnp.where((digit[0] ^ j) < (digit[0] ^ k), moments[j], 0.0)
         priors.append(prior)
     priors = traded(priors)
-    priors, rim = lax.optimization_barrier((priors, rim))
     rim = lax.ppermute(rim, "seq", [(i, (i + 1) % seq) for i in range(seq)])
 
-    queries = call(
-        functools.partial(solve_kernel, heads, shares, GROUPS),
-        (shape((per, HEAD, rows), BF16),) * GROUPS,
-        (
-            digit, base, ridge, *priors, mixer_queries, mixer_keys, mixer_values,
-            out_gain.reshape(1, -1),
-        ),
-        scalars=3,
-        scratch=(
-            pltpu.VMEM((heads, chunks, CHUNK, 2 * HEAD), BF16),
-            pltpu.VMEM((heads, chunks, HEAD, 2 * CHUNK), BF16),
-            pltpu.VMEM((heads, HEAD, rows), BF16),
-            pltpu.VMEM((heads, chunks - 1, HEAD, HEAD), F32),
-            pltpu.VMEM((heads, chunks - 1, HEAD, HEAD), F32),
-            pltpu.VMEM((heads, 2 * ITERS, rows), F32),
-            pltpu.VMEM((heads, rows, HEAD), F32),
-            pltpu.VMEM((heads, chunks, 3, HEAD, HEAD), F32),
-            pltpu.VMEM((heads, HEAD, rows), F32),
-            *cheb_scratch(heads, chunks),
-        ),
-        flops=10**10,
-        nbytes=3 * 10**7,
-    )
     lefts = []
-    after = rim
-    for g in range(GROUPS):
+    attended, far = rim, w_far
+    first = 0
+    for per in sizes:
+        (queries,) = call(
+            functools.partial(solve_kernel, per, shares, first),
+            (shape((per, HEAD, rows), BF16),),
+            (
+                digit, base, ridge, *priors, mixer_queries, mixer_keys, mixer_values,
+                out_gain.reshape(1, -1), attended if first else out_gain.reshape(1, -1),
+            ),
+            scalars=3,
+            scratch=(
+                pltpu.VMEM((per, chunks, CHUNK, 2 * HEAD), BF16),
+                pltpu.VMEM((per, chunks, HEAD, 2 * CHUNK), BF16),
+                pltpu.VMEM((per, HEAD, rows), BF16),
+                pltpu.VMEM((per, chunks - 1, HEAD, HEAD), F32),
+                pltpu.VMEM((per, chunks - 1, HEAD, HEAD), F32),
+                pltpu.VMEM((per, 2 * ITERS, rows), F32),
+                pltpu.VMEM((per, rows, HEAD), F32),
+                pltpu.VMEM((per, chunks, 3, HEAD, HEAD), F32),
+                pltpu.VMEM((per, HEAD, rows), F32),
+                *cheb_scratch(per, chunks),
+            ),
+            flops=10**10,
+            nbytes=3 * 10**7,
+        )
         (attended,) = call(
             attend_kernel,
             (shape((rows, per * HEAD), BF16),),
-            (base, queries[g], rim, window_keys, window_values, after),
+            (base, queries, rim, window_keys, window_values, far),
             scalars=1,
             scratch=(pltpu.VMEM((WINDOW + rows, width), BF16), pltpu.VMEM((width, WINDOW + rows), BF16)),
             flops=4 * 10**9,
             nbytes=15 * 10**6,
         )
-        after = attended
+        first += per
         if head == 4:
             far = swap(attended, "head", 1, 4, 2)
             lefts += [attended, swap(attended, "head", 1, 4, 1), far, swap(far, "head", 1, 4, 1)]
         else:
             lefts += [attended] + [swap(attended, "head", 1, head, k) for k in range(1, head)]
-    return call(
-        functools.partial(project_kernel, GROUPS, head),
-        shape((rows, cols), BF16),
-        (*lefts, *rights),
-    )
+    def project(chosen, kind, *more):
+        left = [lefts[g * head + k] for g, k in chosen]
+        rows_of = [sum(sizes[:g]) * HEAD for g, _ in chosen]
+        right = [rights[k] for _, k in chosen]
+        count = 2 * len(chosen)
+        pairs = [(i, len(chosen) + i, row) for i, row in enumerate(rows_of)]
+        return call(
+            functools.partial(project_kernel, pairs, count),
+            (shape((rows, cols), kind),),
+            (*left, *right, *more),
+        )[0]
+
+    last = len(sizes) - 1
+    early = [(g, k) for g in range(len(sizes)) for k in range(head) if g < last or k < 2]
+    late = [(last, k) for k in range(2, head)]
+    if not late:
+        return project(early, BF16)
+    return project(late, BF16, project(early, F32))
 
 
 def solution(mesh):

time: 65.3 us -> 63.9 us (0.979)
  waiting for transfers between devices: 25.9 us -> 14.8 us
  local copies, waits for them, and re-layouts: 2.36 us -> 5.77 us
  starting transfers between devices: 16.3 us -> 19.1 us
  Pallas kernels: 19.2 us -> 21.4 us
  other arithmetic: 1.13 us -> 2.4 us
    ppermute x16, waiting for transfers between devices: 25.9 us -> 14.8 us  [swap(): lax.ppermute(x, axis, [(i, partner(i, stride, radix, k)) for i in range(n)])]
    dynamic_slice x1 -> x3, local copies, waits for them, and re-layouts: 0.24 us -> 3.66 us  [columns(): return lax.dynamic_slice_in_dim(x, block * cols, count * cols, 1)]
    ppermute x16, starting transfers between devices: 15.4 us -> 18.1 us  [swap(): lax.ppermute(x, axis, [(i, partner(i, stride, radix, k)) for i in range(n)])]
    pallas_call x5 -> x7, Pallas kernels: 19.2 us -> 21.4 us  [call(): pl.pallas_call(kernel, out_shape=outs, in_specs=[SMEM] * scalars + [VMEM]...]
    add x1, other arithmetic: 0.09 us -> 0.99 us  [shards(): prior = prior + jnp.where(digit[0] ^ j < digit[0] ^ k, moments[j], 0.0)]
  transfers between devices with their start and end apart: 17 -> 17, of which waited for: 8 -> 7; matrix products, arithmetic and copies ran while one was open for 2% -> 10% of each run, Pallas kernels for 24% -> 29%
where the time goes in v4:
time: 63.9 us; the launch traced here: 63.6 us
  Pallas kernels  21.4 us (33%)
  starting transfers between devices  19.1 us (30%)
  waiting for transfers between devices  14.8 us (23%)
  local copies, waits for them, and re-layouts  5.77 us (9%)
  other arithmetic  2.4 us (4%)
    pallas_call x7, Pallas kernels, call(): pl.pallas_call(kernel, out_shape=outs, in_specs=[SMEM] * scalars + [VMEM]...  21.4 us
    ppermute x16, starting transfers between devices, swap(): lax.ppermute(x, axis, [(i, partner(i, stride, radix, k)) for i in range(n)])  18.1 us
    ppermute x16, waiting for transfers between devices, swap(): lax.ppermute(x, axis, [(i, partner(i, stride, radix, k)) for i in range(n)])  14.8 us
    dynamic_slice x3, local copies, waits for them, and re-layouts, columns(): return lax.dynamic_slice_in_dim(x, block * cols, count * cols, 1)  3.66 us
    unnamed x20, local copies, waits for them, and re-layouts  2.12 us
  transfers between devices with their start and end apart: 17, of which 7 were waited for; matrix products, arithmetic and copies ran while one was open for 10% of the time, Pallas kernels for 29%

profile of v4, /device:TPU:0, one launch (start us, length us, event | category | flops | bytes accessed | tf_op | source)
XLA Modules:
  0.0 63.6 jit_solution(17906063624318029100)
XLA Ops:
  0.0 1.0 %copy-done = bf16[512,512]{1,0:T(8,128)(2,1)S(1)} copy-done((bf16[512,512]{1,0:T(8,128)(2,1)S(1)}, bf16[512,512]{1,0:T(8,128)(2,1)}, u32[]{:S(2)}) %copy-start) | copy-done | bytes 524312
  1.0 1.0 %copy-done.2 = bf16[512,512]{1,0:T(8,128)(2,1)S(1)} copy-done((bf16[512,512]{1,0:T(8,128)(2,1)S(1)}, bf16[512,512]{1,0:T(8,128)(2,1)}, u32[]{:S(2)}) %copy-start.2) | copy-done | bytes 524312
  2.1 1.6 %shard_map.82 = (f32[1,200,128]{2,1,0:T(8,128)S(1)}, f32[1,200,128]{2,1,0:T(8,128)S(1)}, f32[1,200,128]{2,1,0:T(8,128)S(1)}, f32[1,200,128]{2,1,0:T(8,128)S(1)}) custom-call(s32[1]{0:T(128)} %bitcast.1.digit_ref, bf16[512,512]{1,0:T(8,128)(2,1)S(1)} %copy-done, bf16[512,512]{1,0:T(8,128)(2,1)S(1)} %copy-done.2), custom_call_target="tpu_custom_call" | custom-call | tf_op jit(solution)/shard_map/pallas_call | solution.py:309
  3.7 3.0 %collective-permute-start = (f32[1,200,128]{2,1,0:T(8,128)S(1)}, f32[1,200,128]{2,1,0:T(8,128)S(1)}, u32[]{:S(2)}, u32[]{:S(2)}) collective-permute-start(f32[1,200,128]{2,1,0:T(8,128)S(1)} %get-tuple-element.10), channel_id=1, source_target_pairs={{0,4},{4,0},{8,12},{12,8},{16,20},{20,16},{24,28},{28,24},{1,5},{5... | collective-permute-start | bytes 307208 | tf_op jit(solution)/shard_map/ppermute | solution.py:338
  6.7 1.6 %collective-permute-start.1 = (f32[1,200,128]{2,1,0:T(8,128)S(1)}, f32[1,200,128]{2,1,0:T(8,128)S(1)}, u32[]{:S(2)}, u32[]{:S(2)}) collective-permute-start(f32[1,200,128]{2,1,0:T(8,128)S(1)} %get-tuple-element.11), channel_id=1, source_target_pairs={{0,8},{4,12},{8,0},{12,4},{16,24},{20,28},{24,16},{28,20},{1,9},{5... | collective-permute-start | bytes 307208 | tf_op jit(solution)/shard_map/ppermute | solution.py:338
  8.3 2.3 %constant_dynamic-slice_fusion.4 = bf16[512,1024]{1,0:T(8,128)(2,1)} fusion(bf16[512,2048]{1,0:T(8,128)(2,1)} %param.15, s32[]{:T(128)S(6)} %select_n.150), kind=kLoop, calls=%fused_computation.10 | loop fusion | bytes 2097156 | tf_op jit(solution)/shard_map/dynamic_slice | solution.py:387
  10.6 1.9 %collective-permute-start.8 = (bf16[512,1024]{1,0:T(8,128)(2,1)}, bf16[512,1024]{1,0:T(8,128)(2,1)S(1)}, u32[]{:S(2)}, u32[]{:S(2)}) collective-permute-start(bf16[512,1024]{1,0:T(8,128)(2,1)} %constant_dynamic-slice_fusion.4), channel_id=1, source_target_pairs={{0,2},{1,3},{2,0},{3,1},{4,6},{5,7},{6,4},{7,5},{8,10},{9,11},{10,... | collective-permute-start | bytes 3145736 | tf_op jit(solution)/shard_map/ppermute | solution.py:338
  12.5 1.4 %collective-permute-done.2 = f32[1,200,128]{2,1,0:T(8,128)S(1)} collective-permute-done((f32[1,200,128]{2,1,0:T(8,128)S(1)}, f32[1,200,128]{2,1,0:T(8,128)S(1)}, u32[]{:S(2)}, u32[]{:S(2)}) %collective-permute-start.2) | collective-permute-done | bytes 102432 | tf_op jit(solution)/shard_map/ppermute | solution.py:338
  14.6 2.6 %collective-permute-start.3 = (f32[1,200,128]{2,1,0:T(8,128)}, f32[1,200,128]{2,1,0:T(8,128)}, u32[]{:S(2)}, u32[]{:S(2)}) collective-permute-start(f32[1,200,128]{2,1,0:T(8,128)} %add_add_fusion), channel_id=1, source_target_pairs={{0,16},{4,20},{8,24},{12,28},{16,0},{20,4},{24,8},{28,12},{1,17},{... | collective-permute-start | bytes 307208 | tf_op jit(solution)/shard_map/ppermute | solution.py:338
  17.9 1.0 %collective-permute-start.7 = (bf16[512,256]{1,0:T(8,128)(2,1)}, bf16[512,256]{1,0:T(8,128)(2,1)S(1)}, u32[]{:S(2)}, u32[]{:S(2)}) collective-permute-start(bf16[512,256]{1,0:T(8,128)(2,1)} %pad_maximum_fusion), channel_id=1, source_target_pairs={{0,4},{4,8},{8,12},{12,16},{16,20},{20,24},{24,28},{28,0},{1,5},{5... | collective-permute-start | bytes 786440 | tf_op jit(solution)/shard_map/ppermute | solution.py:417
  18.9 2.6 %collective-permute-done.3 = f32[1,200,128]{2,1,0:T(8,128)} collective-permute-done((f32[1,200,128]{2,1,0:T(8,128)}, f32[1,200,128]{2,1,0:T(8,128)}, u32[]{:S(2)}, u32[]{:S(2)}) %collective-permute-start.3) | collective-permute-done | bytes 102432 | tf_op jit(solution)/shard_map/ppermute | solution.py:338
  21.5 1.0 %select_add_fusion = (f32[1,200,128]{2,1,0:T(8,128)S(1)}, f32[1,200,128]{2,1,0:T(8,128)S(1)}, f32[1,200,128]{2,1,0:T(8,128)S(1)}, f32[1,200,128]{2,1,0:T(8,128)S(1)}) fusion(f32[1,200,128]{2,1,0:T(8,128)S(1)} %collective-permute-done.1, f32[1,200,128]{2,1,0:T(8,128)S(1)} %collective-permute-done, f32[1,200,128]{2,1,0:T(8,128)S(1)} %get-tuple-element.9, ...), kind=kLoop, calls=%fused_computation.1 | loop fusion | flops 640000 | bytes 921613 | tf_op jit(solution)/shard_map/add | solution.py:414
  22.5 4.5 %collective-permute-start.4 = (f32[1,200,128]{2,1,0:T(8,128)S(1)}, f32[1,200,128]{2,1,0:T(8,128)S(1)}, u32[]{:S(2)}, u32[]{:S(2)}) collective-permute-start(f32[1,200,128]{2,1,0:T(8,128)S(1)} %get-tuple-element.19), channel_id=1, source_target_pairs={{0,4},{4,0},{8,12},{12,8},{16,20},{20,16},{24,28},{28,24},{1,5},{5... | collective-permute-start | bytes 307208 | tf_op jit(solution)/shard_map/ppermute | solution.py:338
  27.1 1.5 %collective-permute-start.6 = (f32[1,200,128]{2,1,0:T(8,128)S(1)}, f32[1,200,128]{2,1,0:T(8,128)S(1)}, u32[]{:S(2)}, u32[]{:S(2)}) collective-permute-start(f32[1,200,128]{2,1,0:T(8,128)S(1)} %get-tuple-element.17), channel_id=1, source_target_pairs={{0,12},{4,8},{8,4},{12,0},{16,28},{20,24},{24,20},{28,16},{1,13},{... | collective-permute-start | bytes 307208 | tf_op jit(solution)/shard_map/ppermute | solution.py:338
  28.6 1.3 %constant_dynamic-slice_fusion = (bf16[512,512]{1,0:T(8,128)(2,1)S(1)}, bf16[512,512]{1,0:T(8,128)(2,1)S(1)}) fusion(bf16[512,2048]{1,0:T(8,128)(2,1)} %param.15, s32[]{:T(128)S(6)} %select_n.155, s32[]{:T(128)S(6)} %select_n.154), kind=kLoop, calls=%fused_computation.6 | loop fusion | bytes 2097160 | tf_op jit(solution)/shard_map/dynamic_slice | solution.py:387
  30.8 0.9 %collective-permute-done.5.refs_2_ = f32[1,200,128]{2,1,0:T(8,128)S(1)} collective-permute-done((f32[1,200,128]{2,1,0:T(8,128)S(1)}, f32[1,200,128]{2,1,0:T(8,128)S(1)}, u32[]{:S(2)}, u32[]{:S(2)}) %collective-permute-start.5) | collective-permute-done | bytes 102432 | tf_op jit(solution)/shard_map/ppermute | solution.py:338
  32.7 7.2 %shard_map.83.query_ref = bf16[2,128,512]{2,1,0:T(8,128)(2,1)S(1)} custom-call(s32[1]{0:T(128)} %bitcast.1.digit_ref, s32[1]{0:T(128)} %bitcast.base_ref, f32[4]{0:T(128)S(1)} %copy-done.8, f32[1,200,128]{2,1,0:T(8,128)S(1)} %get-tuple-element.20.refs_0_, f32[1,200,128]{2,1,0:T(8,128)S(1)} %collective-permute-done.4.refs_1_, ...), custom_call_target="tpu_custom_call" | custom-call | flops 10000000000 | bytes 30000000 | tf_op jit(solution)/shard_map/pallas_call | solution.py:309
  39.9 1.7 %shard_map.84.refs_8_.refs_0_ = bf16[512,256]{1,0:T(8,128)(2,1)S(1)} custom-call(s32[1]{0:T(128)} %bitcast.base_ref, bf16[2,128,512]{2,1,0:T(8,128)(2,1)S(1)} %shard_map.83.query_ref, bf16[512,256]{1,0:T(8,128)(2,1)S(1)} %collective-permute-done.7.rim_ref, bf16[512,128]{1,0:T(8,128)(2,1)S(1)} %copy-done.5, bf16[512,128]{1,0:T(8,128)(2,1)S(1)} %copy-done.4, ...), custom_call_target="tpu_custom_call" | custom-call | flops 4000000000 | bytes 15000000 | tf_op jit(solution)/shard_map/pallas_call | solution.py:309
  41.5 1.5 %collective-permute-start.9 = (bf16[512,256]{1,0:T(8,128)(2,1)S(1)}, bf16[512,256]{1,0:T(8,128)(2,1)S(1)}, u32[]{:S(2)}, u32[]{:S(2)}) collective-permute-start(bf16[512,256]{1,0:T(8,128)(2,1)S(1)} %shard_map.84.refs_8_.refs_0_), channel_id=1, source_target_pairs={{0,2},{1,3},{2,0},{3,1},{4,6},{5,7},{6,4},{7,5},{8,10},{9,11},{10,... | collective-permute-start | bytes 786440 | tf_op jit(solution)/shard_map/ppermute | solution.py:338
  43.3 7.2 %shard_map.85.query_ref = bf16[2,128,512]{2,1,0:T(8,128)(2,1)S(1)} custom-call(s32[1]{0:T(128)} %bitcast.1.digit_ref, s32[1]{0:T(128)} %bitcast.base_ref, f32[4]{0:T(128)S(1)} %copy-done.8, f32[1,200,128]{2,1,0:T(8,128)S(1)} %get-tuple-element.20.refs_0_, f32[1,200,128]{2,1,0:T(8,128)S(1)} %collective-permute-done.4.refs_1_, ...), custom_call_target="tpu_custom_call" | custom-call | flops 10000000000 | bytes 30000000 | tf_op jit(solution)/shard_map/pallas_call | solution.py:309
  50.4 1.7 %shard_map.86.refs_4_ = bf16[512,256]{1,0:T(8,128)(2,1)S(1)} custom-call(s32[1]{0:T(128)} %bitcast.base_ref, bf16[2,128,512]{2,1,0:T(8,128)(2,1)S(1)} %shard_map.85.query_ref, bf16[512,256]{1,0:T(8,128)(2,1)S(1)} %collective-permute-done.7.rim_ref, bf16[512,128]{1,0:T(8,128)(2,1)S(1)} %copy-done.5, bf16[512,128]{1,0:T(8,128)(2,1)S(1)} %copy-done.4, ...), custom_call_target="tpu_custom_call" | custom-call | flops 4000000000 | bytes 15000000 | tf_op jit(solution)/shard_map/pallas_call | solution.py:309
  53.4 7.4 %collective-permute-done.10.refs_0_ = bf16[512,256]{1,0:T(8,128)(2,1)S(1)} collective-permute-done((bf16[512,256]{1,0:T(8,128)(2,1)S(1)}, bf16[512,256]{1,0:T(8,128)(2,1)S(1)}, u32[]{:S(2)}, u32[]{:S(2)}) %collective-permute-start.10) | collective-permute-done | bytes 262176 | tf_op jit(solution)/shard_map/ppermute | solution.py:338
  60.9 1.0 %shard_map.87.refs_4_ = f32[512,512]{1,0:T(8,128)S(1)} custom-call(bf16[512,256]{1,0:T(8,128)(2,1)S(1)} %shard_map.84.refs_8_.refs_0_, bf16[512,256]{1,0:T(8,128)(2,1)S(1)} %collective-permute-done.13.refs_1_, bf16[512,256]{1,0:T(8,128)(2,1)S(1)} %collective-permute-done.9.after_ref.refs_2_, bf16[512,256]{1,0:T(8,128)(2,1)S(1)} %collective-permute-done.14.refs_3_, ...), custom_call_target="tpu_custom_call" | custom-call | tf_op jit(solution)/shard_map/pallas_call | solution.py:309
  62.4 1.2 %shard_map.88 = bf16[512,512]{1,0:T(8,128)(2,1)} custom-call(bf16[512,256]{1,0:T(8,128)(2,1)S(1)} %collective-permute-done.10.refs_0_, bf16[512,256]{1,0:T(8,128)(2,1)S(1)} %collective-permute-done.11.refs_1_, bf16[512,512]{1,0:T(8,128)(2,1)S(1)} %get-tuple-element.16.refs_8_.refs_2_, bf16[512,512]{1,0:T(8,128)(2,1)S(1)} %collective-permute-done.12.refs_9_.refs_3_, ...), custom_call_target="tpu_custom_call" | custom-call | tf_op jit(solution)/shard_map/pallas_call | solution.py:309
  (43 shorter events, 5.3 us)
Async XLA Ops:
  2.1 15.1 %copy-start.4 = (bf16[512,128]{1,0:T(8,128)(2,1)S(1)}, bf16[512,128]{1,0:T(8,128)(2,1)}, u32[]{:S(2)}) copy-start(bf16[512,128]{1,0:T(8,128)(2,1)} %vo_ref.3) | copy-start | bytes 393220
  2.1 15.1 %copy-start.5 = (bf16[512,128]{1,0:T(8,128)(2,1)S(1)}, bf16[512,128]{1,0:T(8,128)(2,1)}, u32[]{:S(2)}) copy-start(bf16[512,128]{1,0:T(8,128)(2,1)} %ko_ref.3) | copy-start | bytes 393220
  3.7 8.8 %collective-permute-start = (f32[1,200,128]{2,1,0:T(8,128)S(1)}, f32[1,200,128]{2,1,0:T(8,128)S(1)}, u32[]{:S(2)}, u32[]{:S(2)}) collective-permute-start(f32[1,200,128]{2,1,0:T(8,128)S(1)} %get-tuple-element.10), channel_id=1, source_target_pairs={{0,4},{4,0},{8,12},{12,8},{16,20},{20,16},{24,28},{28,24},{1,5},{5... | collective-permute-start | bytes 307208 | tf_op jit(solution)/shard_map/ppermute | solution.py:338
  6.7 5.7 %collective-permute-start.1 = (f32[1,200,128]{2,1,0:T(8,128)S(1)}, f32[1,200,128]{2,1,0:T(8,128)S(1)}, u32[]{:S(2)}, u32[]{:S(2)}) collective-permute-start(f32[1,200,128]{2,1,0:T(8,128)S(1)} %get-tuple-element.11), channel_id=1, source_target_pairs={{0,8},{4,12},{8,0},{12,4},{16,24},{20,28},{24,16},{28,20},{1,9},{5... | collective-permute-start | bytes 307208 | tf_op jit(solution)/shard_map/ppermute | solution.py:338
  8.3 5.6 %collective-permute-start.2 = (f32[1,200,128]{2,1,0:T(8,128)S(1)}, f32[1,200,128]{2,1,0:T(8,128)S(1)}, u32[]{:S(2)}, u32[]{:S(2)}) collective-permute-start(f32[1,200,128]{2,1,0:T(8,128)S(1)} %get-tuple-element.12), channel_id=1, source_target_pairs={{0,12},{4,8},{8,4},{12,0},{16,28},{20,24},{24,20},{28,16},{1,13},{... | collective-permute-start | bytes 307208 | tf_op jit(solution)/shard_map/ppermute | solution.py:338
  10.6 29.3 %collective-permute-start.8 = (bf16[512,1024]{1,0:T(8,128)(2,1)}, bf16[512,1024]{1,0:T(8,128)(2,1)S(1)}, u32[]{:S(2)}, u32[]{:S(2)}) collective-permute-start(bf16[512,1024]{1,0:T(8,128)(2,1)} %constant_dynamic-slice_fusion.4), channel_id=1, source_target_pairs={{0,2},{1,3},{2,0},{3,1},{4,6},{5,7},{6,4},{7,5},{8,10},{9,11},{10,... | collective-permute-start | bytes 3145736 | tf_op jit(solution)/shard_map/ppermute | solution.py:338
  13.9 18.8 %copy-start.1 = (bf16[512,512]{1,0:T(8,128)(2,1)S(1)}, bf16[512,512]{1,0:T(8,128)(2,1)}, u32[]{:S(2)}) copy-start(bf16[512,512]{1,0:T(8,128)(2,1)} %refs_5_.3) | copy-start | bytes 1572868
  13.9 18.8 %copy-start.3 = (bf16[512,512]{1,0:T(8,128)(2,1)S(1)}, bf16[512,512]{1,0:T(8,128)(2,1)}, u32[]{:S(2)}) copy-start(bf16[512,512]{1,0:T(8,128)(2,1)} %refs_6_.3) | copy-start | bytes 1572868
  13.9 18.8 %copy-start.6 = (bf16[512,512]{1,0:T(8,128)(2,1)S(1)}, bf16[512,512]{1,0:T(8,128)(2,1)}, u32[]{:S(2)}) copy-start(bf16[512,512]{1,0:T(8,128)(2,1)} %refs_4_.3) | copy-start | bytes 1572868
  13.9 18.8 %copy-start.7 = (f32[512]{0:T(512)S(1)}, f32[512]{0:T(512)}, u32[]{:S(2)}) copy-start(f32[512]{0:T(512)} %param.13) | copy-start | bytes 6148
  13.9 18.8 %copy-start.8 = (f32[4]{0:T(128)S(1)}, f32[4]{0:T(128)}, u32[]{:S(2)}) copy-start(f32[4]{0:T(128)} %ridge_ref.3) | copy-start | bytes 52
  14.6 7.0 %collective-permute-start.3 = (f32[1,200,128]{2,1,0:T(8,128)}, f32[1,200,128]{2,1,0:T(8,128)}, u32[]{:S(2)}, u32[]{:S(2)}) collective-permute-start(f32[1,200,128]{2,1,0:T(8,128)} %add_add_fusion), channel_id=1, source_target_pairs={{0,16},{4,20},{8,24},{12,28},{16,0},{20,4},{24,8},{28,12},{1,17},{... | collective-permute-start | bytes 307208 | tf_op jit(solution)/shard_map/ppermute | solution.py:338
  17.9 22.0 %collective-permute-start.7 = (bf16[512,256]{1,0:T(8,128)(2,1)}, bf16[512,256]{1,0:T(8,128)(2,1)S(1)}, u32[]{:S(2)}, u32[]{:S(2)}) collective-permute-start(bf16[512,256]{1,0:T(8,128)(2,1)} %pad_maximum_fusion), channel_id=1, source_target_pairs={{0,4},{4,8},{8,12},{12,16},{16,20},{20,24},{24,28},{28,0},{1,5},{5... | collective-permute-start | bytes 786440 | tf_op jit(solution)/shard_map/ppermute | solution.py:417
  22.5 8.3 %collective-permute-start.4 = (f32[1,200,128]{2,1,0:T(8,128)S(1)}, f32[1,200,128]{2,1,0:T(8,128)S(1)}, u32[]{:S(2)}, u32[]{:S(2)}) collective-permute-start(f32[1,200,128]{2,1,0:T(8,128)S(1)} %get-tuple-element.19), channel_id=1, source_target_pairs={{0,4},{4,0},{8,12},{12,8},{16,20},{20,16},{24,28},{28,24},{1,5},{5... | collective-permute-start | bytes 307208 | tf_op jit(solution)/shard_map/ppermute | solution.py:338
  27.1 4.7 %collective-permute-start.5 = (f32[1,200,128]{2,1,0:T(8,128)S(1)}, f32[1,200,128]{2,1,0:T(8,128)S(1)}, u32[]{:S(2)}, u32[]{:S(2)}) collective-permute-start(f32[1,200,128]{2,1,0:T(8,128)S(1)} %get-tuple-element.18), channel_id=1, source_target_pairs={{0,8},{4,12},{8,0},{12,4},{16,24},{20,28},{24,16},{28,20},{1,9},{5... | collective-permute-start | bytes 307208 | tf_op jit(solution)/shard_map/ppermute | solution.py:338
  27.1 5.6 %collective-permute-start.6 = (f32[1,200,128]{2,1,0:T(8,128)S(1)}, f32[1,200,128]{2,1,0:T(8,128)S(1)}, u32[]{:S(2)}, u32[]{:S(2)}) collective-permute-start(f32[1,200,128]{2,1,0:T(8,128)S(1)} %get-tuple-element.17), channel_id=1, source_target_pairs={{0,12},{4,8},{8,4},{12,0},{16,28},{20,24},{24,20},{28,16},{1,13},{... | collective-permute-start | bytes 307208 | tf_op jit(solution)/shard_map/ppermute | solution.py:338
  30.8 22.4 %collective-permute-start.16 = (bf16[512,512]{1,0:T(8,128)(2,1)S(1)}, bf16[512,512]{1,0:T(8,128)(2,1)S(1)}, u32[]{:S(2)}, u32[]{:S(2)}) collective-permute-start(bf16[512,512]{1,0:T(8,128)(2,1)S(1)} %get-tuple-element.13), channel_id=1, source_target_pairs={{0,1},{1,0},{2,3},{3,2},{4,5},{5,4},{6,7},{7,6},{8,9},{9,8},{10,11... | collective-permute-start | bytes 1572872 | tf_op jit(solution)/shard_map/ppermute | solution.py:338
  41.5 8.9 %collective-permute-start.9 = (bf16[512,256]{1,0:T(8,128)(2,1)S(1)}, bf16[512,256]{1,0:T(8,128)(2,1)S(1)}, u32[]{:S(2)}, u32[]{:S(2)}) collective-permute-start(bf16[512,256]{1,0:T(8,128)(2,1)S(1)} %shard_map.84.refs_8_.refs_0_), channel_id=1, source_target_pairs={{0,2},{1,3},{2,0},{3,1},{4,6},{5,7},{6,4},{7,5},{8,10},{9,11},{10,... | collective-permute-start | bytes 786440 | tf_op jit(solution)/shard_map/ppermute | solution.py:338
  43.2 17.7 %collective-permute-start.12 = (bf16[512,512]{1,0:T(8,128)(2,1)S(1)}, bf16[512,512]{1,0:T(8,128)(2,1)S(1)}, u32[]{:S(2)}, u32[]{:S(2)}) collective-permute-start(bf16[512,512]{1,0:T(8,128)(2,1)S(1)} %get-tuple-element.15), channel_id=1, source_target_pairs={{0,1},{1,0},{2,3},{3,2},{4,5},{5,4},{6,7},{7,6},{8,9},{9,8},{10,11... | collective-permute-start | bytes 1572872 | tf_op jit(solution)/shard_map/ppermute | solution.py:338
  52.1 8.8 %collective-permute-start.10 = (bf16[512,256]{1,0:T(8,128)(2,1)S(1)}, bf16[512,256]{1,0:T(8,128)(2,1)S(1)}, u32[]{:S(2)}, u32[]{:S(2)}) collective-permute-start(bf16[512,256]{1,0:T(8,128)(2,1)S(1)} %shard_map.86.refs_4_), channel_id=1, source_target_pairs={{0,2},{1,3},{2,0},{3,1},{4,6},{5,7},{6,4},{7,5},{8,10},{9,11},{10,... | collective-permute-start | bytes 786440 | tf_op jit(solution)/shard_map/ppermute | solution.py:338
  52.7 8.2 %collective-permute-start.13 = (bf16[512,256]{1,0:T(8,128)(2,1)S(1)}, bf16[512,256]{1,0:T(8,128)(2,1)S(1)}, u32[]{:S(2)}, u32[]{:S(2)}) collective-permute-start(bf16[512,256]{1,0:T(8,128)(2,1)S(1)} %shard_map.84.refs_8_.refs_0_), channel_id=1, source_target_pairs={{0,1},{1,0},{2,3},{3,2},{4,5},{5,4},{6,7},{7,6},{8,9},{9,8},{10,11... | collective-permute-start | bytes 786440 | tf_op jit(solution)/shard_map/ppermute | solution.py:338
  52.9 8.0 %collective-permute-start.15 = (bf16[512,256]{1,0:T(8,128)(2,1)S(1)}, bf16[512,256]{1,0:T(8,128)(2,1)S(1)}, u32[]{:S(2)}, u32[]{:S(2)}) collective-permute-start(bf16[512,256]{1,0:T(8,128)(2,1)S(1)} %shard_map.86.refs_4_), channel_id=1, source_target_pairs={{0,1},{1,0},{2,3},{3,2},{4,5},{5,4},{6,7},{7,6},{8,9},{9,8},{10,11... | collective-permute-start | bytes 786440 | tf_op jit(solution)/shard_map/ppermute | solution.py:338
  53.2 7.7 %collective-permute-start.14 = (bf16[512,256]{1,0:T(8,128)(2,1)S(1)}, bf16[512,256]{1,0:T(8,128)(2,1)S(1)}, u32[]{:S(2)}, u32[]{:S(2)}) collective-permute-start(bf16[512,256]{1,0:T(8,128)(2,1)S(1)} %collective-permute-done.9.after_ref.refs_2_), channel_id=1, source_target_pairs={{0,1},{1,0},{2,3},{3,2},{4,5},{5,4},{6,7},{7,6},{8,9},{9,8},{10,11... | collective-permute-start | bytes 786440 | tf_op jit(solution)/shard_map/ppermute | solution.py:338
  60.9 1.5 %collective-permute-start.11 = (bf16[512,256]{1,0:T(8,128)(2,1)S(1)}, bf16[512,256]{1,0:T(8,128)(2,1)S(1)}, u32[]{:S(2)}, u32[]{:S(2)}) collective-permute-start(bf16[512,256]{1,0:T(8,128)(2,1)S(1)} %collective-permute-done.10.refs_0_), channel_id=1, source_target_pairs={{0,1},{1,0},{2,3},{3,2},{4,5},{5,4},{6,7},{7,6},{8,9},{9,8},{10,11... | collective-permute-start | bytes 786440 | tf_op jit(solution)/shard_map/ppermute | solution.py:338
  (3 other events, 5.4 us)

commit v5 on v4

--- a/solution.py
+++ b/solution.py
@@ -224,7 +224,8 @@
             stage3(i, *ch)
         return carry
 
-    lax.fori_loop(0, ITERS - 1, body, 0)
+    for i in range(ITERS - 1):
+        body(i, 0)
     for h, c in chains:
         advance(ITERS - 1, h, c)
 

time: 63.9 us -> 61.3 us (0.959)
  Pallas kernels: 21.4 us -> 18.7 us
    pallas_call x7, Pallas kernels: 21.4 us -> 18.7 us  [call(): pl.pallas_call(kernel, out_shape=outs, in_specs=[SMEM] * scalars + [VMEM]...]
  transfers between devices with their start and end apart: 17 -> 17, of which waited for: 7 -> 7; matrix products, arithmetic and copies ran while one was open for 10% -> 10% of each run, Pallas kernels for 29% -> 26%
where the time goes in v5:
time: 61.3 us; the launch traced here: 61 us
  starting transfers between devices  19.2 us (31%)
  Pallas kernels  18.7 us (31%)
  waiting for transfers between devices  14.7 us (24%)
  local copies, waits for them, and re-layouts  5.77 us (9%)
  other arithmetic  2.4 us (4%)
    pallas_call x7, Pallas kernels, call(): pl.pallas_call(kernel, out_shape=outs, in_specs=[SMEM] * scalars + [VMEM]...  18.7 us
    ppermute x16, starting transfers between devices, swap(): lax.ppermute(x, axis, [(i, partner(i, stride, radix, k)) for i in range(n)])  18.2 us
    ppermute x16, waiting for transfers between devices, swap(): lax.ppermute(x, axis, [(i, partner(i, stride, radix, k)) for i in range(n)])  14.7 us
    dynamic_slice x3, local copies, waits for them, and re-layouts, columns(): return lax.dynamic_slice_in_dim(x, block * cols, count * cols, 1)  3.66 us
    unnamed x20, local copies, waits for them, and re-layouts  2.12 us
  transfers between devices with their start and end apart: 17, of which 7 were waited for; matrix products, arithmetic and copies ran while one was open for 10% of the time, Pallas kernels for 26%

profile of v5, /device:TPU:0, one launch (start us, length us, event | category | flops | bytes accessed | tf_op | source)
XLA Modules:
  0.0 61.0 jit_solution(12732122708678699594)
XLA Ops:
  0.0 1.0 %copy-done = bf16[512,512]{1,0:T(8,128)(2,1)S(1)} copy-done((bf16[512,512]{1,0:T(8,128)(2,1)S(1)}, bf16[512,512]{1,0:T(8,128)(2,1)}, u32[]{:S(2)}) %copy-start) | copy-done | bytes 524312
  1.0 1.0 %copy-done.2 = bf16[512,512]{1,0:T(8,128)(2,1)S(1)} copy-done((bf16[512,512]{1,0:T(8,128)(2,1)S(1)}, bf16[512,512]{1,0:T(8,128)(2,1)}, u32[]{:S(2)}) %copy-start.2) | copy-done | bytes 524312
  2.1 1.6 %shard_map.82 = (f32[1,200,128]{2,1,0:T(8,128)S(1)}, f32[1,200,128]{2,1,0:T(8,128)S(1)}, f32[1,200,128]{2,1,0:T(8,128)S(1)}, f32[1,200,128]{2,1,0:T(8,128)S(1)}) custom-call(s32[1]{0:T(128)} %bitcast.1.digit_ref, bf16[512,512]{1,0:T(8,128)(2,1)S(1)} %copy-done, bf16[512,512]{1,0:T(8,128)(2,1)S(1)} %copy-done.2), custom_call_target="tpu_custom_call" | custom-call | tf_op jit(solution)/shard_map/pallas_call | solution.py:310
  3.7 3.0 %collective-permute-start = (f32[1,200,128]{2,1,0:T(8,128)S(1)}, f32[1,200,128]{2,1,0:T(8,128)S(1)}, u32[]{:S(2)}, u32[]{:S(2)}) collective-permute-start(f32[1,200,128]{2,1,0:T(8,128)S(1)} %get-tuple-element.10), channel_id=1, source_target_pairs={{0,4},{4,0},{8,12},{12,8},{16,20},{20,16},{24,28},{28,24},{1,5},{5... | collective-permute-start | bytes 307208 | tf_op jit(solution)/shard_map/ppermute | solution.py:339
  6.7 1.6 %collective-permute-start.1 = (f32[1,200,128]{2,1,0:T(8,128)S(1)}, f32[1,200,128]{2,1,0:T(8,128)S(1)}, u32[]{:S(2)}, u32[]{:S(2)}) collective-permute-start(f32[1,200,128]{2,1,0:T(8,128)S(1)} %get-tuple-element.11), channel_id=1, source_target_pairs={{0,8},{4,12},{8,0},{12,4},{16,24},{20,28},{24,16},{28,20},{1,9},{5... | collective-permute-start | bytes 307208 | tf_op jit(solution)/shard_map/ppermute | solution.py:339
  8.3 2.3 %constant_dynamic-slice_fusion.4 = bf16[512,1024]{1,0:T(8,128)(2,1)} fusion(bf16[512,2048]{1,0:T(8,128)(2,1)} %param.15, s32[]{:T(128)S(6)} %select_n.150), kind=kLoop, calls=%fused_computation.10 | loop fusion | bytes 2097156 | tf_op jit(solution)/shard_map/dynamic_slice | solution.py:388
  10.6 1.9 %collective-permute-start.8 = (bf16[512,1024]{1,0:T(8,128)(2,1)}, bf16[512,1024]{1,0:T(8,128)(2,1)S(1)}, u32[]{:S(2)}, u32[]{:S(2)}) collective-permute-start(bf16[512,1024]{1,0:T(8,128)(2,1)} %constant_dynamic-slice_fusion.4), channel_id=1, source_target_pairs={{0,2},{1,3},{2,0},{3,1},{4,6},{5,7},{6,4},{7,5},{8,10},{9,11},{10,... | collective-permute-start | bytes 3145736 | tf_op jit(solution)/shard_map/ppermute | solution.py:339
  12.5 1.4 %collective-permute-done.2 = f32[1,200,128]{2,1,0:T(8,128)S(1)} collective-permute-done((f32[1,200,128]{2,1,0:T(8,128)S(1)}, f32[1,200,128]{2,1,0:T(8,128)S(1)}, u32[]{:S(2)}, u32[]{:S(2)}) %collective-permute-start.2) | collective-permute-done | bytes 102432 | tf_op jit(solution)/shard_map/ppermute | solution.py:339
  14.6 2.6 %collective-permute-start.3 = (f32[1,200,128]{2,1,0:T(8,128)}, f32[1,200,128]{2,1,0:T(8,128)}, u32[]{:S(2)}, u32[]{:S(2)}) collective-permute-start(f32[1,200,128]{2,1,0:T(8,128)} %add_add_fusion), channel_id=1, source_target_pairs={{0,16},{4,20},{8,24},{12,28},{16,0},{20,4},{24,8},{28,12},{1,17},{... | collective-permute-start | bytes 307208 | tf_op jit(solution)/shard_map/ppermute | solution.py:339
  17.9 1.0 %collective-permute-start.7 = (bf16[512,256]{1,0:T(8,128)(2,1)}, bf16[512,256]{1,0:T(8,128)(2,1)S(1)}, u32[]{:S(2)}, u32[]{:S(2)}) collective-permute-start(bf16[512,256]{1,0:T(8,128)(2,1)} %pad_maximum_fusion), channel_id=1, source_target_pairs={{0,4},{4,8},{8,12},{12,16},{16,20},{20,24},{24,28},{28,0},{1,5},{5... | collective-permute-start | bytes 786440 | tf_op jit(solution)/shard_map/ppermute | solution.py:418
  18.9 2.6 %collective-permute-done.3 = f32[1,200,128]{2,1,0:T(8,128)} collective-permute-done((f32[1,200,128]{2,1,0:T(8,128)}, f32[1,200,128]{2,1,0:T(8,128)}, u32[]{:S(2)}, u32[]{:S(2)}) %collective-permute-start.3) | collective-permute-done | bytes 102432 | tf_op jit(solution)/shard_map/ppermute | solution.py:339
  21.5 1.0 %select_add_fusion = (f32[1,200,128]{2,1,0:T(8,128)S(1)}, f32[1,200,128]{2,1,0:T(8,128)S(1)}, f32[1,200,128]{2,1,0:T(8,128)S(1)}, f32[1,200,128]{2,1,0:T(8,128)S(1)}) fusion(f32[1,200,128]{2,1,0:T(8,128)S(1)} %collective-permute-done.1, f32[1,200,128]{2,1,0:T(8,128)S(1)} %collective-permute-done, f32[1,200,128]{2,1,0:T(8,128)S(1)} %get-tuple-element.9, ...), kind=kLoop, calls=%fused_computation.1 | loop fusion | flops 640000 | bytes 921613 | tf_op jit(solution)/shard_map/add | solution.py:415
  22.5 4.6 %collective-permute-start.4 = (f32[1,200,128]{2,1,0:T(8,128)S(1)}, f32[1,200,128]{2,1,0:T(8,128)S(1)}, u32[]{:S(2)}, u32[]{:S(2)}) collective-permute-start(f32[1,200,128]{2,1,0:T(8,128)S(1)} %get-tuple-element.19), channel_id=1, source_target_pairs={{0,4},{4,0},{8,12},{12,8},{16,20},{20,16},{24,28},{28,24},{1,5},{5... | collective-permute-start | bytes 307208 | tf_op jit(solution)/shard_map/ppermute | solution.py:339
  27.1 1.5 %collective-permute-start.6 = (f32[1,200,128]{2,1,0:T(8,128)S(1)}, f32[1,200,128]{2,1,0:T(8,128)S(1)}, u32[]{:S(2)}, u32[]{:S(2)}) collective-permute-start(f32[1,200,128]{2,1,0:T(8,128)S(1)} %get-tuple-element.17), channel_id=1, source_target_pairs={{0,12},{4,8},{8,4},{12,0},{16,28},{20,24},{24,20},{28,16},{1,13},{... | collective-permute-start | bytes 307208 | tf_op jit(solution)/shard_map/ppermute | solution.py:339
  28.6 1.3 %constant_dynamic-slice_fusion = (bf16[512,512]{1,0:T(8,128)(2,1)S(1)}, bf16[512,512]{1,0:T(8,128)(2,1)S(1)}) fusion(bf16[512,2048]{1,0:T(8,128)(2,1)} %param.15, s32[]{:T(128)S(6)} %select_n.155, s32[]{:T(128)S(6)} %select_n.154), kind=kLoop, calls=%fused_computation.6 | loop fusion | bytes 2097160 | tf_op jit(solution)/shard_map/dynamic_slice | solution.py:388
  30.8 1.0 %collective-permute-done.5.refs_2_ = f32[1,200,128]{2,1,0:T(8,128)S(1)} collective-permute-done((f32[1,200,128]{2,1,0:T(8,128)S(1)}, f32[1,200,128]{2,1,0:T(8,128)S(1)}, u32[]{:S(2)}, u32[]{:S(2)}) %collective-permute-start.5) | collective-permute-done | bytes 102432 | tf_op jit(solution)/shard_map/ppermute | solution.py:339
  32.7 5.7 %shard_map.83.query_ref = bf16[2,128,512]{2,1,0:T(8,128)(2,1)S(1)} custom-call(s32[1]{0:T(128)} %bitcast.1.digit_ref, s32[1]{0:T(128)} %bitcast.base_ref, f32[4]{0:T(128)S(1)} %copy-done.8, f32[1,200,128]{2,1,0:T(8,128)S(1)} %get-tuple-element.20.refs_0_, f32[1,200,128]{2,1,0:T(8,128)S(1)} %collective-permute-done.4.refs_1_, ...), custom_call_target="tpu_custom_call" | custom-call | flops 10000000000 | bytes 30000000 | tf_op jit(solution)/shard_map/pallas_call | solution.py:310
  38.4 1.7 %shard_map.84.refs_8_.refs_0_ = bf16[512,256]{1,0:T(8,128)(2,1)S(1)} custom-call(s32[1]{0:T(128)} %bitcast.base_ref, bf16[2,128,512]{2,1,0:T(8,128)(2,1)S(1)} %shard_map.83.query_ref, bf16[512,256]{1,0:T(8,128)(2,1)S(1)} %collective-permute-done.7.rim_ref, bf16[512,128]{1,0:T(8,128)(2,1)S(1)} %copy-done.5, bf16[512,128]{1,0:T(8,128)(2,1)S(1)} %copy-done.4, ...), custom_call_target="tpu_custom_call" | custom-call | flops 4000000000 | bytes 15000000 | tf_op jit(solution)/shard_map/pallas_call | solution.py:310
  40.1 1.5 %collective-permute-start.9 = (bf16[512,256]{1,0:T(8,128)(2,1)S(1)}, bf16[512,256]{1,0:T(8,128)(2,1)S(1)}, u32[]{:S(2)}, u32[]{:S(2)}) collective-permute-start(bf16[512,256]{1,0:T(8,128)(2,1)S(1)} %shard_map.84.refs_8_.refs_0_), channel_id=1, source_target_pairs={{0,2},{1,3},{2,0},{3,1},{4,6},{5,7},{6,4},{7,5},{8,10},{9,11},{10,... | collective-permute-start | bytes 786440 | tf_op jit(solution)/shard_map/ppermute | solution.py:339
  41.8 5.9 %shard_map.85.query_ref = bf16[2,128,512]{2,1,0:T(8,128)(2,1)S(1)} custom-call(s32[1]{0:T(128)} %bitcast.1.digit_ref, s32[1]{0:T(128)} %bitcast.base_ref, f32[4]{0:T(128)S(1)} %copy-done.8, f32[1,200,128]{2,1,0:T(8,128)S(1)} %get-tuple-element.20.refs_0_, f32[1,200,128]{2,1,0:T(8,128)S(1)} %collective-permute-done.4.refs_1_, ...), custom_call_target="tpu_custom_call" | custom-call | flops 10000000000 | bytes 30000000 | tf_op jit(solution)/shard_map/pallas_call | solution.py:310
  47.8 1.7 %shard_map.86.refs_4_ = bf16[512,256]{1,0:T(8,128)(2,1)S(1)} custom-call(s32[1]{0:T(128)} %bitcast.base_ref, bf16[2,128,512]{2,1,0:T(8,128)(2,1)S(1)} %shard_map.85.query_ref, bf16[512,256]{1,0:T(8,128)(2,1)S(1)} %collective-permute-done.7.rim_ref, bf16[512,128]{1,0:T(8,128)(2,1)S(1)} %copy-done.5, bf16[512,128]{1,0:T(8,128)(2,1)S(1)} %copy-done.4, ...), custom_call_target="tpu_custom_call" | custom-call | flops 4000000000 | bytes 15000000 | tf_op jit(solution)/shard_map/pallas_call | solution.py:310
  50.8 7.4 %collective-permute-done.10.refs_0_ = bf16[512,256]{1,0:T(8,128)(2,1)S(1)} collective-permute-done((bf16[512,256]{1,0:T(8,128)(2,1)S(1)}, bf16[512,256]{1,0:T(8,128)(2,1)S(1)}, u32[]{:S(2)}, u32[]{:S(2)}) %collective-permute-start.10) | collective-permute-done | bytes 262176 | tf_op jit(solution)/shard_map/ppermute | solution.py:339
  58.2 1.0 %shard_map.87.refs_4_ = f32[512,512]{1,0:T(8,128)S(1)} custom-call(bf16[512,256]{1,0:T(8,128)(2,1)S(1)} %shard_map.84.refs_8_.refs_0_, bf16[512,256]{1,0:T(8,128)(2,1)S(1)} %collective-permute-done.13.refs_1_, bf16[512,256]{1,0:T(8,128)(2,1)S(1)} %collective-permute-done.9.after_ref.refs_2_, bf16[512,256]{1,0:T(8,128)(2,1)S(1)} %collective-permute-done.14.refs_3_, ...), custom_call_target="tpu_custom_call" | custom-call | tf_op jit(solution)/shard_map/pallas_call | solution.py:310
  59.7 1.2 %shard_map.88 = bf16[512,512]{1,0:T(8,128)(2,1)} custom-call(bf16[512,256]{1,0:T(8,128)(2,1)S(1)} %collective-permute-done.10.refs_0_, bf16[512,256]{1,0:T(8,128)(2,1)S(1)} %collective-permute-done.11.refs_1_, bf16[512,512]{1,0:T(8,128)(2,1)S(1)} %get-tuple-element.16.refs_8_.refs_2_, bf16[512,512]{1,0:T(8,128)(2,1)S(1)} %collective-permute-done.12.refs_9_.refs_3_, ...), custom_call_target="tpu_custom_call" | custom-call | tf_op jit(solution)/shard_map/pallas_call | solution.py:310
  (43 shorter events, 5.3 us)
Async XLA Ops:
  2.1 15.1 %copy-start.4 = (bf16[512,128]{1,0:T(8,128)(2,1)S(1)}, bf16[512,128]{1,0:T(8,128)(2,1)}, u32[]{:S(2)}) copy-start(bf16[512,128]{1,0:T(8,128)(2,1)} %vo_ref.3) | copy-start | bytes 393220
  2.1 15.1 %copy-start.5 = (bf16[512,128]{1,0:T(8,128)(2,1)S(1)}, bf16[512,128]{1,0:T(8,128)(2,1)}, u32[]{:S(2)}) copy-start(bf16[512,128]{1,0:T(8,128)(2,1)} %ko_ref.3) | copy-start | bytes 393220
  3.7 8.8 %collective-permute-start = (f32[1,200,128]{2,1,0:T(8,128)S(1)}, f32[1,200,128]{2,1,0:T(8,128)S(1)}, u32[]{:S(2)}, u32[]{:S(2)}) collective-permute-start(f32[1,200,128]{2,1,0:T(8,128)S(1)} %get-tuple-element.10), channel_id=1, source_target_pairs={{0,4},{4,0},{8,12},{12,8},{16,20},{20,16},{24,28},{28,24},{1,5},{5... | collective-permute-start | bytes 307208 | tf_op jit(solution)/shard_map/ppermute | solution.py:339
  6.7 5.7 %collective-permute-start.1 = (f32[1,200,128]{2,1,0:T(8,128)S(1)}, f32[1,200,128]{2,1,0:T(8,128)S(1)}, u32[]{:S(2)}, u32[]{:S(2)}) collective-permute-start(f32[1,200,128]{2,1,0:T(8,128)S(1)} %get-tuple-element.11), channel_id=1, source_target_pairs={{0,8},{4,12},{8,0},{12,4},{16,24},{20,28},{24,16},{28,20},{1,9},{5... | collective-permute-start | bytes 307208 | tf_op jit(solution)/shard_map/ppermute | solution.py:339
  8.3 5.6 %collective-permute-start.2 = (f32[1,200,128]{2,1,0:T(8,128)S(1)}, f32[1,200,128]{2,1,0:T(8,128)S(1)}, u32[]{:S(2)}, u32[]{:S(2)}) collective-permute-start(f32[1,200,128]{2,1,0:T(8,128)S(1)} %get-tuple-element.12), channel_id=1, source_target_pairs={{0,12},{4,8},{8,4},{12,0},{16,28},{20,24},{24,20},{28,16},{1,13},{... | collective-permute-start | bytes 307208 | tf_op jit(solution)/shard_map/ppermute | solution.py:339
  10.6 27.9 %collective-permute-start.8 = (bf16[512,1024]{1,0:T(8,128)(2,1)}, bf16[512,1024]{1,0:T(8,128)(2,1)S(1)}, u32[]{:S(2)}, u32[]{:S(2)}) collective-permute-start(bf16[512,1024]{1,0:T(8,128)(2,1)} %constant_dynamic-slice_fusion.4), channel_id=1, source_target_pairs={{0,2},{1,3},{2,0},{3,1},{4,6},{5,7},{6,4},{7,5},{8,10},{9,11},{10,... | collective-permute-start | bytes 3145736 | tf_op jit(solution)/shard_map/ppermute | solution.py:339
  13.9 18.8 %copy-start.1 = (bf16[512,512]{1,0:T(8,128)(2,1)S(1)}, bf16[512,512]{1,0:T(8,128)(2,1)}, u32[]{:S(2)}) copy-start(bf16[512,512]{1,0:T(8,128)(2,1)} %refs_5_.3) | copy-start | bytes 1572868
  13.9 18.8 %copy-start.3 = (bf16[512,512]{1,0:T(8,128)(2,1)S(1)}, bf16[512,512]{1,0:T(8,128)(2,1)}, u32[]{:S(2)}) copy-start(bf16[512,512]{1,0:T(8,128)(2,1)} %refs_6_.3) | copy-start | bytes 1572868
  13.9 18.8 %copy-start.6 = (bf16[512,512]{1,0:T(8,128)(2,1)S(1)}, bf16[512,512]{1,0:T(8,128)(2,1)}, u32[]{:S(2)}) copy-start(bf16[512,512]{1,0:T(8,128)(2,1)} %refs_4_.3) | copy-start | bytes 1572868
  13.9 18.8 %copy-start.7 = (f32[512]{0:T(512)S(1)}, f32[512]{0:T(512)}, u32[]{:S(2)}) copy-start(f32[512]{0:T(512)} %param.13) | copy-start | bytes 6148
  13.9 18.8 %copy-start.8 = (f32[4]{0:T(128)S(1)}, f32[4]{0:T(128)}, u32[]{:S(2)}) copy-start(f32[4]{0:T(128)} %ridge_ref.3) | copy-start | bytes 52
  14.6 7.0 %collective-permute-start.3 = (f32[1,200,128]{2,1,0:T(8,128)}, f32[1,200,128]{2,1,0:T(8,128)}, u32[]{:S(2)}, u32[]{:S(2)}) collective-permute-start(f32[1,200,128]{2,1,0:T(8,128)} %add_add_fusion), channel_id=1, source_target_pairs={{0,16},{4,20},{8,24},{12,28},{16,0},{20,4},{24,8},{28,12},{1,17},{... | collective-permute-start | bytes 307208 | tf_op jit(solution)/shard_map/ppermute | solution.py:339
  17.9 20.5 %collective-permute-start.7 = (bf16[512,256]{1,0:T(8,128)(2,1)}, bf16[512,256]{1,0:T(8,128)(2,1)S(1)}, u32[]{:S(2)}, u32[]{:S(2)}) collective-permute-start(bf16[512,256]{1,0:T(8,128)(2,1)} %pad_maximum_fusion), channel_id=1, source_target_pairs={{0,4},{4,8},{8,12},{12,16},{16,20},{20,24},{24,28},{28,0},{1,5},{5... | collective-permute-start | bytes 786440 | tf_op jit(solution)/shard_map/ppermute | solution.py:418
  22.5 8.3 %collective-permute-start.4 = (f32[1,200,128]{2,1,0:T(8,128)S(1)}, f32[1,200,128]{2,1,0:T(8,128)S(1)}, u32[]{:S(2)}, u32[]{:S(2)}) collective-permute-start(f32[1,200,128]{2,1,0:T(8,128)S(1)} %get-tuple-element.19), channel_id=1, source_target_pairs={{0,4},{4,0},{8,12},{12,8},{16,20},{20,16},{24,28},{28,24},{1,5},{5... | collective-permute-start | bytes 307208 | tf_op jit(solution)/shard_map/ppermute | solution.py:339
  27.1 4.7 %collective-permute-start.5 = (f32[1,200,128]{2,1,0:T(8,128)S(1)}, f32[1,200,128]{2,1,0:T(8,128)S(1)}, u32[]{:S(2)}, u32[]{:S(2)}) collective-permute-start(f32[1,200,128]{2,1,0:T(8,128)S(1)} %get-tuple-element.18), channel_id=1, source_target_pairs={{0,8},{4,12},{8,0},{12,4},{16,24},{20,28},{24,16},{28,20},{1,9},{5... | collective-permute-start | bytes 307208 | tf_op jit(solution)/shard_map/ppermute | solution.py:339
  27.1 5.6 %collective-permute-start.6 = (f32[1,200,128]{2,1,0:T(8,128)S(1)}, f32[1,200,128]{2,1,0:T(8,128)S(1)}, u32[]{:S(2)}, u32[]{:S(2)}) collective-permute-start(f32[1,200,128]{2,1,0:T(8,128)S(1)} %get-tuple-element.17), channel_id=1, source_target_pairs={{0,12},{4,8},{8,4},{12,0},{16,28},{20,24},{24,20},{28,16},{1,13},{... | collective-permute-start | bytes 307208 | tf_op jit(solution)/shard_map/ppermute | solution.py:339
  30.8 20.0 %collective-permute-start.16 = (bf16[512,512]{1,0:T(8,128)(2,1)S(1)}, bf16[512,512]{1,0:T(8,128)(2,1)S(1)}, u32[]{:S(2)}, u32[]{:S(2)}) collective-permute-start(bf16[512,512]{1,0:T(8,128)(2,1)S(1)} %get-tuple-element.13), channel_id=1, source_target_pairs={{0,1},{1,0},{2,3},{3,2},{4,5},{5,4},{6,7},{7,6},{8,9},{9,8},{10,11... | collective-permute-start | bytes 1572872 | tf_op jit(solution)/shard_map/ppermute | solution.py:339
  40.1 7.7 %collective-permute-start.9 = (bf16[512,256]{1,0:T(8,128)(2,1)S(1)}, bf16[512,256]{1,0:T(8,128)(2,1)S(1)}, u32[]{:S(2)}, u32[]{:S(2)}) collective-permute-start(bf16[512,256]{1,0:T(8,128)(2,1)S(1)} %shard_map.84.refs_8_.refs_0_), channel_id=1, source_target_pairs={{0,2},{1,3},{2,0},{3,1},{4,6},{5,7},{6,4},{7,5},{8,10},{9,11},{10,... | collective-permute-start | bytes 786440 | tf_op jit(solution)/shard_map/ppermute | solution.py:339
  41.7 16.5 %collective-permute-start.12 = (bf16[512,512]{1,0:T(8,128)(2,1)S(1)}, bf16[512,512]{1,0:T(8,128)(2,1)S(1)}, u32[]{:S(2)}, u32[]{:S(2)}) collective-permute-start(bf16[512,512]{1,0:T(8,128)(2,1)S(1)} %get-tuple-element.15), channel_id=1, source_target_pairs={{0,1},{1,0},{2,3},{3,2},{4,5},{5,4},{6,7},{7,6},{8,9},{9,8},{10,11... | collective-permute-start | bytes 1572872 | tf_op jit(solution)/shard_map/ppermute | solution.py:339
  49.4 8.8 %collective-permute-start.10 = (bf16[512,256]{1,0:T(8,128)(2,1)S(1)}, bf16[512,256]{1,0:T(8,128)(2,1)S(1)}, u32[]{:S(2)}, u32[]{:S(2)}) collective-permute-start(bf16[512,256]{1,0:T(8,128)(2,1)S(1)} %shard_map.86.refs_4_), channel_id=1, source_target_pairs={{0,2},{1,3},{2,0},{3,1},{4,6},{5,7},{6,4},{7,5},{8,10},{9,11},{10,... | collective-permute-start | bytes 786440 | tf_op jit(solution)/shard_map/ppermute | solution.py:339
  50.3 7.9 %collective-permute-start.13 = (bf16[512,256]{1,0:T(8,128)(2,1)S(1)}, bf16[512,256]{1,0:T(8,128)(2,1)S(1)}, u32[]{:S(2)}, u32[]{:S(2)}) collective-permute-start(bf16[512,256]{1,0:T(8,128)(2,1)S(1)} %shard_map.84.refs_8_.refs_0_), channel_id=1, source_target_pairs={{0,1},{1,0},{2,3},{3,2},{4,5},{5,4},{6,7},{7,6},{8,9},{9,8},{10,11... | collective-permute-start | bytes 786440 | tf_op jit(solution)/shard_map/ppermute | solution.py:339
  50.3 7.9 %collective-permute-start.15 = (bf16[512,256]{1,0:T(8,128)(2,1)S(1)}, bf16[512,256]{1,0:T(8,128)(2,1)S(1)}, u32[]{:S(2)}, u32[]{:S(2)}) collective-permute-start(bf16[512,256]{1,0:T(8,128)(2,1)S(1)} %shard_map.86.refs_4_), channel_id=1, source_target_pairs={{0,1},{1,0},{2,3},{3,2},{4,5},{5,4},{6,7},{7,6},{8,9},{9,8},{10,11... | collective-permute-start | bytes 786440 | tf_op jit(solution)/shard_map/ppermute | solution.py:339
  50.8 7.4 %collective-permute-start.14 = (bf16[512,256]{1,0:T(8,128)(2,1)S(1)}, bf16[512,256]{1,0:T(8,128)(2,1)S(1)}, u32[]{:S(2)}, u32[]{:S(2)}) collective-permute-start(bf16[512,256]{1,0:T(8,128)(2,1)S(1)} %collective-permute-done.9.after_ref.refs_2_), channel_id=1, source_target_pairs={{0,1},{1,0},{2,3},{3,2},{4,5},{5,4},{6,7},{7,6},{8,9},{9,8},{10,11... | collective-permute-start | bytes 786440 | tf_op jit(solution)/shard_map/ppermute | solution.py:339
  58.2 1.5 %collective-permute-start.11 = (bf16[512,256]{1,0:T(8,128)(2,1)S(1)}, bf16[512,256]{1,0:T(8,128)(2,1)S(1)}, u32[]{:S(2)}, u32[]{:S(2)}) collective-permute-start(bf16[512,256]{1,0:T(8,128)(2,1)S(1)} %collective-permute-done.10.refs_0_), channel_id=1, source_target_pairs={{0,1},{1,0},{2,3},{3,2},{4,5},{5,4},{6,7},{7,6},{8,9},{9,8},{10,11... | collective-permute-start | bytes 786440 | tf_op jit(solution)/shard_map/ppermute | solution.py:339
  (3 other events, 5.4 us)
